TPU v7x, 128 devices: a whole 4x4x4 slice. The times are simulated.
128 devices in a mesh: ctx: 8 (over y_lo, x), head: 16 (over z, y_hi, core).
Axes of the slice: x: 4, y: 4 (y_hi: 2, y_lo: 2; y = y_hi * 2 + y_lo), z: 4, core: 2. Of those that a mesh axis runs over, the one named last changes fastest.
Arguments:
- latent: bfloat16 [2048, 576], P('ctx'), may hold values from -6 to 6
- queries: bfloat16 [2048, 24576], P('ctx', 'head'), may hold values from -300 to 300
- up_weight: bfloat16 [512, 32768], P(None, 'head'), may hold values from -0.25 to 0.25
- out_grad: bfloat16 [2048, 16384], P('ctx', 'head'), may hold values from -6 to 6
- logratio: float32 [2048], P('ctx'), may hold values from -1.5 to 1.5
- student_logprob: float32 [2048], P('ctx'), may hold values from -4 to -0.05
- teacher_logprob: float32 [2048], P('ctx'), may hold values from -4 to -0.05
- group_order: int32 [16], replicated, may hold values from 0 to 15, each once
Outputs:
- attn_output: bfloat16 [2048, 16384], P('ctx', 'head')
- query_grad: bfloat16 [2048, 24576], P('ctx', 'head')
- latent_grad: float32 [2048, 576], P(('ctx', 'head'))
- weight_grad: float32 [512, 32768], P('ctx', 'head')
Inputs may be any that keep to these rules, and one draw needn't show every extreme that they name: Row r of the sequence arrays stands at position group_order[r // 128] * 128 + r % 128 of the rollout.
All inputs are finite; a program needn't handle non-finite values.
Results may differ from a plain program's by a relative error of at most 0.035.
Values may be sent and summed in bfloat16 or wider, within the bound.
No kernel may reach another device: no remote copies, remote signals or barrier semaphores. Data moves between devices by JAX's collectives and lax.ppermute only.
A program may use at most 64 MiB of HBM per device.

v0:
```python
import jax
import jax.numpy as jnp
from jax import lax
from jax.sharding import PartitionSpec as P

NOPE = 128
VDIM = 128
KV_RANK = 512
QK = 192


def contract_last(former, latter):
    return lax.dot_general(
        former, latter, (((1,), (1,)), ((), ())), preferred_element_type=jnp.float32
    )


def contract_first(former, latter):
    return lax.dot_general(
        former, latter, (((0,), (0,)), ((), ())), preferred_element_type=jnp.float32
    )


def positions_of(group_order, row_count, group_len):
    row_index = jnp.arange(row_count, dtype=jnp.int32)
    group_slot = row_index // group_len
    onehot = group_slot[:, None] == jnp.arange(group_order.shape[0], dtype=jnp.int32)[None, :]
    starts = jnp.sum(jnp.where(onehot, group_order[None, :], 0), axis=1)
    return starts * group_len + row_index % group_len


def token_weight(logratio, student_logprob, teacher_logprob):
    return jnp.clip(jnp.exp(logratio), 0.8, 1.25) * (teacher_logprob - student_logprob)


def local(
    latent, queries, up_weight, out_grad, logratio, student_logprob, teacher_logprob, group_order
):
    local_rows = latent.shape[0]
    gathered = lax.all_gather(latent, "ctx", axis=0, tiled=True)
    all_rows = gathered.shape[0]
    positions = positions_of(group_order, all_rows, local_rows // 2)
    own_pos = lax.dynamic_slice_in_dim(positions, lax.axis_index("ctx") * local_rows, local_rows)
    visible = positions[None, :] <= own_pos[:, None]
    tok_weight = token_weight(logratio, student_logprob, teacher_logprob)
    head_count = queries.shape[1] // QK
    q_heads = queries.reshape(local_rows, head_count, QK).transpose(1, 0, 2)
    g_heads = out_grad.reshape(local_rows, head_count, VDIM).transpose(1, 0, 2)
    w_heads = up_weight.reshape(KV_RANK, head_count, NOPE + VDIM).transpose(1, 0, 2)
    latent_main = gathered[:, :KV_RANK]
    latent_rope = gathered[:, KV_RANK:]
    logit_scale = QK ** (-0.5)

    def head_step(running, sliced):
        head_query, head_grad, head_weight = sliced
        key_value = jnp.dot(latent_main, head_weight, preferred_element_type=jnp.float32).astype(
            jnp.bfloat16
        )
        key_matrix = jnp.concatenate([key_value[:, :NOPE], latent_rope], axis=1)
        value_matrix = key_value[:, NOPE:]
        score_matrix = contract_last(head_query, key_matrix) * logit_scale
        score_matrix = jnp.where(visible, score_matrix, -jnp.inf)
        row_max = jnp.max(score_matrix, axis=1, keepdims=True)
        numerator = jnp.exp(score_matrix - row_max)
        attn_prob = numerator / jnp.sum(numerator, axis=1, keepdims=True)
        probability_lowered = attn_prob.astype(jnp.bfloat16)
        attention_result = jnp.dot(
            probability_lowered, value_matrix, preferred_element_type=jnp.float32
        )
        output_gradient = (tok_weight[:, None] * head_grad.astype(jnp.float32)).astype(jnp.bfloat16)
        probability_gradient = contract_last(output_gradient, value_matrix)
        row_delta = jnp.sum(
            output_gradient.astype(jnp.float32) * attention_result, axis=1, keepdims=True
        )
        score_gradient = (attn_prob * (probability_gradient - row_delta) * logit_scale).astype(
            jnp.bfloat16
        )
        query_gradient = jnp.dot(score_gradient, key_matrix, preferred_element_type=jnp.float32)
        key_gradient = contract_first(score_gradient, head_query)
        value_gradient = contract_first(probability_lowered, output_gradient)
        grad_kv = jnp.concatenate([key_gradient[:, :NOPE], value_gradient], axis=1).astype(
            jnp.bfloat16
        )
        grad_main = contract_last(grad_kv, head_weight)
        running = running + jnp.concatenate([grad_main, key_gradient[:, NOPE:]], axis=1)
        grad_weight = contract_first(latent_main, grad_kv)
        return (
            running,
            (
                attention_result.astype(jnp.bfloat16),
                query_gradient.astype(jnp.bfloat16),
                grad_weight,
            ),
        )

    start_value = jnp.zeros((all_rows, gathered.shape[1]), jnp.float32)
    latent_terms, stacked = lax.scan(head_step, start_value, (q_heads, g_heads, w_heads))
    attn_output = stacked[0].transpose(1, 0, 2).reshape(local_rows, head_count * VDIM)
    query_grad = stacked[1].transpose(1, 0, 2).reshape(local_rows, head_count * QK)
    weight_terms = stacked[2].transpose(1, 0, 2).reshape(KV_RANK, head_count * (NOPE + VDIM))
    latent_grad = lax.psum_scatter(latent_terms, ("ctx", "head"), scatter_dimension=0, tiled=True)
    weight_grad = lax.psum_scatter(weight_terms, "ctx", scatter_dimension=0, tiled=True)
    return (attn_output, query_grad, latent_grad, weight_grad)


def solution(mesh):
    placed = (
        P("ctx", None),
        P("ctx", "head"),
        P(None, "head"),
        P("ctx", "head"),
        P("ctx"),
        P("ctx"),
        P("ctx"),
        P(),
    )
    return jax.shard_map(
        local,
        mesh=mesh,
        in_specs=placed,
        out_specs=(P("ctx", "head"), P("ctx", "head"), P(("ctx", "head"), None), P("ctx", "head")),
        check_vma=False,
    )
```

profile of v0, /device:TPU:0, one launch (start us, length us, event | category | flops | bytes accessed | tf_op | source)
XLA Modules:
  0.0 901.6 jit_solution(12609812981032795139)
XLA Ops:
  9.2 2.3 copy.28
  11.6 2.6 copy.29
  14.4 45.2 %all-gather.2.cloned.1.call-done = bf16[2048,576]{0,1:T(8,128)(2,1)} async-done(((bf16[256,576]{0,1:T(8,128)(2,1)}), bf16[2048,576]{0,1:T(8,128)(2,1)}) %all-gather.2.cloned.1.call-update) | async-done | bytes 2359312 | tf_op jit(solution)/shard_map/all_gather | solution.py:40
  59.6 3.2 slice.29
  62.7 2.9 copy.33
  65.6 122.1 %while.17 = (s32[]{:T(128)}, f32[2048,576]{0,1:T(8,128)}, bf16[8,256,128]{1,2,0:T(8,128)(2,1)S(1)}, bf16[8,256,192]{1,2,0:T(8,128)(2,1)}, f32[8,512,256]{1,2,0:T...) while((s32[]{:T(128)}, f32[2048,576]{0,1:T(8,128)}, ...), condition=%wide.region_5.6_spmd.clone, body=%wide.region_1.5_spmd.clone.sunk | while | flops 2636725504 | bytes 86166800 | solution.py:97
  65.6 1.7 fusion.84
  67.4 1.5 fusion.85
  72.3 1.3 fusion.89
  73.8 1.5 fusion.92
  75.3 1.7 fusion.90
  77.0 1.7 maximum_add_fusion.2
  78.7 2.2 copy-done
  80.9 1.7 fusion.84
  82.7 1.5 fusion.85
  87.6 1.3 fusion.89
  89.0 1.5 fusion.92
  90.5 1.7 fusion.90
  92.3 1.7 maximum_add_fusion.2
  94.0 2.2 copy-done
  96.2 1.7 fusion.84
  97.9 1.5 fusion.85
  102.9 1.3 fusion.89
  104.3 1.5 fusion.92
  105.8 1.7 fusion.90
  107.5 1.7 maximum_add_fusion.2
  109.3 2.2 copy-done
  111.4 1.7 fusion.84
  113.2 1.5 fusion.85
  118.1 1.3 fusion.89
  119.5 1.5 fusion.92
  121.1 1.7 fusion.90
  122.8 1.7 maximum_add_fusion.2
  124.5 2.2 copy-done
  126.7 1.7 fusion.84
  128.4 1.5 fusion.85
  133.4 1.3 fusion.89
  134.8 1.5 fusion.92
  136.3 1.7 fusion.90
  138.1 1.7 maximum_add_fusion.2
  139.8 2.2 copy-done
  142.0 1.7 fusion.84
  143.7 1.5 fusion.85
  150.1 1.5 fusion.92
  151.6 1.7 fusion.90
  153.3 1.7 maximum_add_fusion.2
  155.1 2.2 copy-done
  157.2 1.7 fusion.84
  159.0 1.5 fusion.85
  163.9 1.3 fusion.89
  165.3 1.5 fusion.92
  166.9 1.7 fusion.90
  168.6 1.7 maximum_add_fusion.2
  170.3 2.2 copy-done
  172.5 1.7 fusion.84
  174.2 1.5 fusion.85
  180.6 1.5 fusion.92
  182.1 1.7 fusion.90
  183.9 1.7 maximum_add_fusion.2
  185.6 2.2 copy-done
  187.8 5.4 copy.39
  193.2 5.8 copy.35
  201.2 46.0 %reduce-scatter.5.cloned.1.call-done = f32[64,2048]{1,0:T(8,128)} async-done(((f32[512,2048]{1,0:T(8,128)}), f32[64,2048]{1,0:T(8,128)}) %reduce-scatter.5.cloned.1.call-update) | async-done | bytes 524304 | tf_op jit(solution)/shard_map/reduce_scatter | solution.py:102
  247.3 647.9 %reduce-scatter.3.cloned.1.call-done = f32[16,576]{1,0:T(8,128)} async-done(((f32[2048,576]{1,0:T(8,128)}), f32[16,576]{1,0:T(8,128)}) %reduce-scatter.3.cloned.1.call-update) | async-done | bytes 36880 | tf_op jit(solution)/shard_map/reduce_scatter | solution.py:101
  (162 shorter events, 35.6 us)
Async XLA Ops:
  7.2 4.4 copy-start.1
  7.2 52.4 %all-gather.2.cloned.1.call-start = ((), (), s32[]{:S(2)}) async-start(), calls=%async_computation.2 | async-start | bytes 2654208 | tf_op jit(solution)/shard_map/all_gather | solution.py:40
  7.9 239.4 %reduce-scatter.5.cloned.1.call-start = ((), (), s32[]{:S(2)}) async-start(), calls=%async_computation.4 | async-start | bytes 4718592 | tf_op jit(solution)/shard_map/reduce_scatter | solution.py:102
  11.6 2.6 copy-start.6
  11.6 2.8 copy-start.3
  11.6 2.8 copy-start.4
  11.6 2.8 copy-start.5
  62.7 2.9 slice-start.2
  73.7 3.3 slice-start
  73.7 3.3 slice-start.1
  78.7 2.2 copy-start
  88.9 3.3 slice-start
  89.0 3.3 slice-start.1
  94.0 2.2 copy-start
  104.2 3.3 slice-start
  104.3 3.3 slice-start.1
  109.2 2.2 copy-start
  119.5 3.3 slice-start
  119.5 3.3 slice-start.1
  124.5 2.2 copy-start
  134.7 3.3 slice-start
  134.8 3.3 slice-start.1
  139.8 2.2 copy-start
  150.0 3.3 slice-start
  150.0 3.3 slice-start.1
  155.1 2.2 copy-start
  165.3 3.3 slice-start
  165.3 3.3 slice-start.1
  170.3 2.2 copy-start
  180.5 3.3 slice-start
  180.6 3.3 slice-start.1
  185.6 2.2 copy-start
  193.2 702.0 %reduce-scatter.3.cloned.1.call-start = ((), (), s32[]{:S(2)}) async-start(), calls=%async_computation.3 | async-start | bytes 5283840 | tf_op jit(solution)/shard_map/reduce_scatter | solution.py:101
  199.0 1.1 copy-start.2
Sparse Core Ops, SparseCore 0:
  9.6 49.9 all-gather.1
  193.3 53.9 reduce-scatter.4
  250.2 644.8 reduce-scatter.2
where the time goes:
time: 903 us; the launch traced here: 902 us
  waiting for transfers between devices  740 us (82%)
  matrix products  81.5 us (9%)
  local copies, waits for them, and re-layouts  44.2 us (5%)
  other arithmetic  21.2 us (2%)
  between operations  13.8 us (2%)
    reduce_scatter x1, waiting for transfers between devices, local(): lax.psum_scatter(latent_terms, ('ctx', 'head'), scatter_dimension=0, tile...  648 us
    reduce_scatter x1, waiting for transfers between devices, local(): lax.psum_scatter(weight_terms, 'ctx', scatter_dimension=0, tiled=True)  46 us
    all_gather x1, waiting for transfers between devices, local(): gathered = lax.all_gather(latent, 'ctx', axis=0, tiled=True)  45.2 us
    dot_general x24, matrix products, contract_last(): lax.dot_general(former, latter, (((1,), (1,)), ((), ())), preferred_eleme...  29.5 us
    dot_general x24, matrix products, contract_first(): lax.dot_general(former, latter, (((0,), (0,)), ((), ())), preferred_eleme...  25 us
  transfers between devices with their start and end apart: 3, of which 3 were waited for; matrix products, arithmetic and copies ran while one was open for 2% of the time, Pallas kernels for 0%

commit v1 on v0

v1 whole, which is shorter than its diff:
```python
import functools, math
import jax, jax.numpy as jnp
from jax import lax
from jax.sharding import PartitionSpec as P
from jax.experimental import pallas as pl
from jax.experimental.pallas import tpu as pltpu
NOPE=128; VDIM=128; KV_RANK=512; QK=192; ROPE=64
BF=jnp.bfloat16; F32=jnp.float32
KEYS=2048; ROWS=256; LAT=576
CH=256
SCALE=QK**-0.5
C2=SCALE*math.log2(math.e)
def mm(a,b): return jnp.dot(a,b,preferred_element_type=F32)
def nt(a,b): return lax.dot_general(a,b,(((1,),(1,)),((),())),preferred_element_type=F32)
def tn(a,b): return lax.dot_general(a,b,(((0,),(0,)),((),())),preferred_element_type=F32)

def body(lat_ref,posk_ref,posq_ref,tw_ref,q_ref,g_ref,w_ref,
         out_ref,dq_ref,wg_ref,lt_ref,
         latT,bias,acc,kk,vv,ss,ee,dd,dkv):
    step=pl.program_id(0)
    @pl.when(step==0)
    def _():
        for j in range(KEYS//CH):
            r=pl.ds(j*CH,CH)
            latT[:,r]=lat_ref[r,:KV_RANK].T
            bias[r,:]=jnp.where(posk_ref[r,:]<=posq_ref[...],0.0,-jnp.inf)
            for hh in range(2):
                kk[hh,r,NOPE:]=lat_ref[r,KV_RANK:]
        acc[...]=jnp.zeros_like(acc)
    W=w_ref[...]
    q=q_ref[...]
    qT=q.T
    dout=(tw_ref[...]*g_ref[...].astype(F32)).astype(BF)
    gT=dout.T
    n=KEYS//CH
    mx=[None,None]
    for j in range(n):
        r=pl.ds(j*CH,CH)
        kv=mm(lat_ref[r,:KV_RANK],W).astype(BF)
        b=bias[r,:]
        for hh in range(2):
            kk[hh,r,:NOPE]=kv[:,hh*256:hh*256+NOPE]
            vv[hh,r,:]=kv[:,hh*256+NOPE:hh*256+256]
            s=mm(kk[hh,r,:],qT[hh*QK:(hh+1)*QK])+b
            ss[hh,r,:]=s
            m=jnp.max(s.reshape(CH//8,8,ROWS),axis=0)
            mx[hh]=m if mx[hh] is None else jnp.maximum(mx[hh],m)
    rl=[];delta=[];qs=[];gs=[];gh=[]
    for hh in range(2):
        mc=jnp.max(mx[hh],axis=0,keepdims=True)*C2
        l=jnp.zeros((8,ROWS),F32)
        for j in range(n):
            r=pl.ds(j*CH,CH)
            e=jnp.exp2(ss[hh,r,:]*C2-mc)
            l=l+jnp.sum(e.reshape(CH//8,8,ROWS),axis=0)
            ee[hh,r,:]=e.astype(BF)
        inv=1.0/jnp.sum(l,axis=0,keepdims=True)
        oT=tn(vv[hh],ee[hh])*inv
        g_h=gT[hh*VDIM:(hh+1)*VDIM]
        delta.append(jnp.sum(oT*g_h.astype(F32),axis=0,keepdims=True))
        out_ref[:,hh*VDIM:(hh+1)*VDIM]=oT.T.astype(BF)
        rl.append(inv)
        gh.append(g_h)
        qs.append((qT[hh*QK:(hh+1)*QK].astype(F32)*(inv*SCALE)).astype(BF))
        gs.append((g_h.astype(F32)*inv).astype(BF))
    for j in range(n):
        r=pl.ds(j*CH,CH)
        ropes=None
        for hh in range(2):
            e=ee[hh,r,:]
            dp=mm(vv[hh,r,:],gh[hh])
            ds=(e.astype(F32)*(dp-delta[hh])).astype(BF)
            dd[hh,r,:]=ds
            dk=nt(ds,qs[hh])
            dv=nt(e,gs[hh])
            dkv[r,hh*256:hh*256+NOPE]=dk[:,:NOPE].astype(BF)
            dkv[r,hh*256+NOPE:hh*256+256]=dv.astype(BF)
            ropes=dk[:,NOPE:] if ropes is None else ropes+dk[:,NOPE:]
        acc[r,:KV_RANK]+=nt(dkv[r,:],W)
        acc[r,KV_RANK:]+=ropes
    dqT=[tn(kk[hh],dd[hh])*(rl[hh]*SCALE) for hh in range(2)]
    dq_ref[...]=jnp.concatenate(dqT,axis=0).T.astype(BF)
    wg_ref[...]=mm(latT[...],dkv[...]).astype(BF)
    @pl.when(step==pl.num_programs(0)-1)
    def _():
        lt_ref[...]=acc[...].astype(BF)

def attn(lat,posk,posq,tw,q,g,w):
    full=lambda s: pl.BlockSpec(s,lambda i:(0,0))
    heads=q.shape[1]//QK
    return pl.pallas_call(body,grid=(heads//2,),
        in_specs=[full((KEYS,LAT)),full((KEYS,1)),full((1,ROWS)),full((ROWS,1)),
            pl.BlockSpec((ROWS,2*QK),lambda i:(0,i)),pl.BlockSpec((ROWS,2*VDIM),lambda i:(0,i)),pl.BlockSpec((KV_RANK,512),lambda i:(0,i))],
        out_specs=[pl.BlockSpec((ROWS,2*VDIM),lambda i:(0,i)),pl.BlockSpec((ROWS,2*QK),lambda i:(0,i)),pl.BlockSpec((KV_RANK,512),lambda i:(0,i)),full((KEYS,LAT))],
        out_shape=[jax.ShapeDtypeStruct((ROWS,heads*VDIM),BF),jax.ShapeDtypeStruct((ROWS,heads*QK),BF),jax.ShapeDtypeStruct((KV_RANK,heads*256),BF),jax.ShapeDtypeStruct((KEYS,LAT),BF)],
        scratch_shapes=[pltpu.VMEM((KV_RANK,KEYS),BF),pltpu.VMEM((KEYS,ROWS),F32),pltpu.VMEM((KEYS,LAT),F32),
            pltpu.VMEM((2,KEYS,QK),BF),pltpu.VMEM((2,KEYS,VDIM),BF),pltpu.VMEM((2,KEYS,ROWS),F32),pltpu.VMEM((2,KEYS,ROWS),BF),pltpu.VMEM((2,KEYS,ROWS),BF),pltpu.VMEM((KEYS,512),BF)],
        compiler_params=pltpu.CompilerParams(vmem_limit_bytes=56*2**20),
        cost_estimate=pl.CostEstimate(flops=2*heads*1300*10**6,bytes_accessed=16*2**20,transcendentals=heads*2**19),
    )(lat,posk,posq,tw,q,g,w)


AXES = ("ctx", "head")


def device_index(x, y, z, core):
    return ((y % 2) * 4 + x) * 16 + z * 4 + (y // 2) * 2 + core


def shift_pairs(steps_of_core):
    pairs = []
    for x in range(4):
        for y in range(4):
            for z in range(4):
                for core in range(2):
                    dx, dy, dz = steps_of_core[core]
                    pairs.append(
                        (
                            device_index(x, y, z, core),
                            device_index((x + dx) % 4, (y + dy) % 4, (z + dz) % 4, core),
                        )
                    )
    return pairs


def swap_cores(value):
    return lax.ppermute(value, "head", [(i, i ^ 1) for i in range(16)])


def swap_ylo(value):
    return lax.ppermute(value, "ctx", [(i, (i + 4) % 8) for i in range(8)])


def send_shift(value, first, second):
    return lax.ppermute(value, AXES, shift_pairs((first, second)))


def gather_latent(latent, z, y_hi, core):
    blocks = latent.reshape(4, 2, 2, 16, LAT)
    blocks = lax.dynamic_index_in_dim(blocks, core, 2, False)
    blocks = jnp.roll(blocks, (-z, -y_hi), (0, 1))
    own = blocks.reshape(128, LAT)
    other = swap_ylo(own)
    pair = jnp.stack([own.reshape(4, 2, 16, LAT), other.reshape(4, 2, 16, LAT)], axis=2)
    far = [pair] + [
        send_shift(pair, (-k, 0, 0), (-k, 0, 0)) for k in (1, 2, 3)
    ]
    mine = jnp.stack(far, axis=0)
    zfirst = mine.transpose(1, 0, 2, 3, 4, 5)
    mine = jnp.where(core == 0, mine, zfirst).reshape(1024, LAT)
    return jnp.concatenate([mine, swap_cores(mine)], axis=0)


def row_index(x, y, z, core):
    rel = jnp.arange(1024, dtype=jnp.int32)
    first, second = rel // 256, (rel // 64) % 4
    dyh, dyl, inner = (rel // 32) % 2, (rel // 16) % 2, rel % 16

    def rows(which):
        dx = jnp.where(which == 0, first, second)
        dz = jnp.where(which == 0, second, first)
        xx, zz = (x + dx) % 4, (z + dz) % 4
        yh, yl = (y // 2 + dyh) % 2, (y % 2 + dyl) % 2
        return ((yl * 4 + xx) * 16 + zz * 4 + yh * 2 + which) * 16 + inner

    return jnp.concatenate([rows(core), rows(1 - core)])


def reduce_latent(keep, send):
    part = keep.astype(F32) + swap_cores(send).astype(F32)
    part = part.reshape(4, 256, LAT)
    wire = part.astype(BF)
    part = part[0] + sum(
        send_shift(wire[k], (k, 0, 0), (0, 0, k)).astype(F32) for k in (1, 2, 3)
    )
    part = part.reshape(4, 64, LAT)
    wire = part.astype(BF)
    part = part[0] + sum(
        send_shift(wire[k], (0, 0, k), (k, 0, 0)).astype(F32) for k in (1, 2, 3)
    )
    part = part.reshape(4, 16, LAT)
    wire = part.astype(BF)
    return wire, part


def shift_y(value, flip_hi, flip_lo):
    pairs = []
    for c in range(8):
        for h in range(16):
            pairs.append((c * 16 + h, (c ^ (4 * flip_lo)) * 16 + (h ^ (2 * flip_hi))))
    return lax.ppermute(value, AXES, pairs)


def positions_of(rows, group_order):
    group = rows // 128
    onehot = group[:, None] == jnp.arange(16, dtype=jnp.int32)[None, :]
    return jnp.sum(jnp.where(onehot, group_order[None, :], 0), axis=1) * 128 + rows % 128


def local(
    latent, queries, up_weight, out_grad, logratio, student_logprob, teacher_logprob, group_order
):
    ctx, head = lax.axis_index("ctx"), lax.axis_index("head")
    x, y_lo = ctx % 4, ctx // 4
    z, y_hi, core = head // 4, (head // 2) % 2, head % 2
    y = y_hi * 2 + y_lo
    rows = gather_latent(latent, z, y_hi, core)
    key_pos = positions_of(row_index(x, y, z, core), group_order)
    own_pos = positions_of(ctx * 256 + jnp.arange(256, dtype=jnp.int32), group_order)
    tok_weight = jnp.clip(jnp.exp(logratio), 0.8, 1.25) * (teacher_logprob - student_logprob)
    attn_output, query_grad, weight_terms, latent_terms = attn(
        rows, key_pos[:, None], own_pos[None, :], tok_weight[:, None], queries, out_grad, up_weight
    )
    weight_grad = lax.psum_scatter(weight_terms, "ctx", scatter_dimension=0, tiled=True)
    wire, part = reduce_latent(latent_terms[:1024], latent_terms[1024:])
    latent_grad = (
        part[0]
        + shift_y(wire[1], 0, 1).astype(F32)
        + shift_y(wire[2], 1, 0).astype(F32)
        + shift_y(wire[3], 1, 1).astype(F32)
    )
    return (attn_output, query_grad, latent_grad, weight_grad.astype(F32))


def solution(mesh):
    placed = (
        P("ctx", None),
        P("ctx", "head"),
        P(None, "head"),
        P("ctx", "head"),
        P("ctx"),
        P("ctx"),
        P("ctx"),
        P(),
    )
    return jax.shard_map(
        local,
        mesh=mesh,
        in_specs=placed,
        out_specs=(P("ctx", "head"), P("ctx", "head"), P(AXES, None), P("ctx", "head")),
        check_vma=False,
    )
```

time: 903 us -> 150 us (0.17)
  waiting for transfers between devices: 740 us -> 47.5 us
  matrix products: 81.5 us -> 0 us
  Pallas kernels: 0 us -> 43.5 us
  local copies, waits for them, and re-layouts: 44.2 us -> 10.8 us
  starting transfers between devices: 0.12 us -> 22.6 us
  other arithmetic: 21.2 us -> 10.8 us
    reduce_scatter x1 -> x0, waiting for transfers between devices: 648 us -> none  [local(): lax.psum_scatter(latent_terms, ('ctx', 'head'), scatter_dimension=0, tile...]
    dot_general x72 -> x0, matrix products: 81.5 us -> none  [the longest x24 29.5 us: contract_last(): lax.dot_general(former, latter, (((1,), (1,)), ((), ())), preferred_eleme...]
    ppermute x0 -> x15, waiting for transfers between devices: none -> 47.5 us  [the longest x9 38.4 us: send_shift(): return lax.ppermute(value, AXES, shift_pairs((first, second)))]
    reduce_scatter x1, waiting for transfers between devices: 46 us -> 0.01 us  [local(): lax.psum_scatter(weight_terms, 'ctx', scatter_dimension=0, tiled=True)]
    all_gather x1 -> x0, waiting for transfers between devices: 45.2 us -> none  [local(): gathered = lax.all_gather(latent, 'ctx', axis=0, tiled=True)]
    pallas_call x0 -> x1, Pallas kernels: none -> 43.5 us  [attn(): pl.pallas_call(body, grid=(heads // 2,), in_specs=[full((KEYS, LAT)), ful...]
    while x49 -> x0, local copies, waits for them, and re-layouts: 23.2 us -> none
    ppermute x0 -> x15, starting transfers between devices: none -> 22.6 us  [the longest x9 15 us: send_shift(): return lax.ppermute(value, AXES, shift_pairs((first, second)))]
  transfers between devices with their start and end apart: 3 -> 16, of which waited for: 3 -> 12; matrix products, arithmetic and copies ran while one was open for 2% -> 8% of each run, Pallas kernels for 0% -> 0%
where the time goes in v1:
time: 150 us
  waiting for transfers between devices  47.5 us (32%)
  Pallas kernels  43.5 us (29%)
  starting transfers between devices  22.6 us (15%)
  between operations  14.4 us (10%)
  local copies, waits for them, and re-layouts  10.8 us (7%)
  other arithmetic  10.8 us (7%)
    pallas_call x1, Pallas kernels, attn(): pl.pallas_call(body, grid=(heads // 2,), in_specs=[full((KEYS, LAT)), ful...  43.5 us
    ppermute x9, waiting for transfers between devices, send_shift(): return lax.ppermute(value, AXES, shift_pairs((first, second)))  38.4 us
    ppermute x9, starting transfers between devices, send_shift(): return lax.ppermute(value, AXES, shift_pairs((first, second)))  15 us
    ppermute x3, starting transfers between devices, shift_y(): return lax.ppermute(value, AXES, pairs)  5.15 us
    ppermute x3, waiting for transfers between devices, shift_y(): return lax.ppermute(value, AXES, pairs)  4.3 us
    ppermute x2, local copies, waits for them, and re-layouts, swap_cores(): return lax.ppermute(value, 'head', [(i, i ^ 1) for i in range(16)])  3.36 us
    add x2, other arithmetic, positions_of(): jnp.sum(jnp.where(onehot, group_order[None, :], 0), axis=1) * 128  3.03 us
  transfers between devices with their start and end apart: 16, of which 12 were waited for; matrix products, arithmetic and copies ran while one was open for 8% of the time, Pallas kernels for 0%

profile of v1, /device:TPU:0, one launch (start us, length us, event | category | flops | bytes accessed | tf_op | source)
XLA Modules:
  0.0 149.7 jit_solution(16413915221367892071)
XLA Ops:
  7.2 0.0 copy-start.1
  7.2 0.0 copy-start.2
  7.2 0.0 copy-start.3
  7.2 0.0 reduce-scatter.2.cloned.1.call-start
  7.3 1.2 copy.41
  8.5 0.0 copy-start
  8.5 0.1 fusion.3
  8.7 0.1 fusion.2
  8.7 1.7 %collective-permute-start = (bf16[128,576]{1,0:T(8,128)(2,1)S(1)}, bf16[128,576]{1,0:T(8,128)(2,1)S(1)}, u32[]{:S(2)}, u32[]{:S(2)}) collective-permute-start(bf16[128,576]{1,0:T(8,128)(2,1)S(1)} %bitcast.32), channel_id=1, source_target_pairs={{0,64},{16,80},{32,96},{48,112},{64,0},{80,16},{96,32},{112,48},{1... | collective-permute-start | bytes 442376 | tf_op jit(solution)/shard_map/ppermute | solution.py:131
  10.5 0.0 copy-done.1
  10.6 0.8 copy.54.tw_ref
  11.4 1.1 copy.52
  12.5 0.1 fusion.67
  12.6 2.1 %collective-permute-done = bf16[128,576]{1,0:T(8,128)(2,1)S(1)} collective-permute-done((bf16[128,576]{1,0:T(8,128)(2,1)S(1)}, bf16[128,576]{1,0:T(8,128)(2,1)S(1)}, u32[]{:S(2)}, u32[]{:S(2)}) %collective-permute-start) | collective-permute-done | bytes 147488 | tf_op jit(solution)/shard_map/ppermute | solution.py:131
  14.7 0.8 fusion.60
  15.5 3.2 %collective-permute-start.2 = (bf16[4,2,2,16,576]{4,3,2,1,0:T(8,128)(2,1)}, bf16[4,2,2,16,576]{4,3,2,1,0:T(8,128)(2,1)S(1)}, u32[]{:S(2)}, u32[]{:S(2)}) collective-permute-start(bf16[4,2,2,16,576]{4,3,2,1,0:T(8,128)(2,1)} %get-tuple-element.27), channel_id=1, source_target_pairs={{0,32},{1,33},{4,36},{5,37},{8,40},{9,41},{12,44},{13,45},{64,96},... | collective-permute-start | bytes 884744 | tf_op jit(solution)/shard_map/ppermute | solution.py:135
  18.7 1.1 collective-permute-start.1
  19.8 0.9 collective-permute-start.3
  20.7 0.1 select_reduce_fusion
  20.8 0.4 copy.53
  21.2 0.4 copy.49
  21.5 6.3 %collective-permute-done.2 = bf16[4,2,2,16,576]{4,3,2,1,0:T(8,128)(2,1)S(1)} collective-permute-done((bf16[4,2,2,16,576]{4,3,2,1,0:T(8,128)(2,1)}, bf16[4,2,2,16,576]{4,3,2,1,0:T(8,128)(2,1)S(1)}, u32[]{:S(2)}, u32[]{:S(2)}) %collective-permute-start.2) | collective-permute-done | bytes 294944 | tf_op jit(solution)/shard_map/ppermute | solution.py:135
  27.8 5.2 %collective-permute-done.1 = bf16[4,2,2,16,576]{4,3,2,1,0:T(8,128)(2,1)S(1)} collective-permute-done((bf16[4,2,2,16,576]{4,3,2,1,0:T(8,128)(2,1)}, bf16[4,2,2,16,576]{4,3,2,1,0:T(8,128)(2,1)S(1)}, u32[]{:S(2)}, u32[]{:S(2)}) %collective-permute-start.1) | collective-permute-done | bytes 294944 | tf_op jit(solution)/shard_map/ppermute | solution.py:135
  33.1 0.0 collective-permute-done.3
  33.1 0.2 pad_maximum_fusion.1
  33.3 0.1 bitcast_select_fusion
  33.5 1.5 copy.46
  34.9 0.0 collective-permute-start.4
  34.9 0.1 select_reduce_fusion.1
  35.0 0.6 fusion.58.posq_ref
  35.6 2.4 %fusion.1.posk_ref = s32[2048,1]{1,0:T(8,128)} fusion(s32[2048,1]{1,0:T(8,128)S(1)} %copy.53, pred[2048,1]{1,0:T(8,128)(4,1)} %copy.52, s32[2048,1]{1,0:T(8,128)S(1)} %copy.49), kind=kLoop, calls=%fused_computation.8 | loop fusion | flops 22528 | bytes 26624 | tf_op jit(solution)/shard_map/add | solution.py:197
  38.1 0.1 collective-permute-done.4
  38.1 1.7 %copy.47 = bf16[1024,576]{1,0:T(8,128)(2,1)S(1)} copy(bf16[1024,576]{0,1:T(8,128)(2,1)} %collective-permute-done.4) | data formatting | bytes 2359296 | tf_op jit(solution)/shard_map/ppermute | solution.py:127
  39.8 1.8 %pad_maximum_fusion.lat_ref = bf16[2048,576]{1,0:T(8,128)(2,1)} fusion(bf16[1024,576]{1,0:T(8,128)(2,1)S(1)} %copy.47, bf16[1024,576]{1,0:T(8,128)(2,1)S(1)} %bitcast.27), kind=kLoop, calls=%fused_computation | loop fusion | flops 4718592 | bytes 4718592 | tf_op jit(solution)/shard_map/concatenate | solution.py:151
  41.6 43.5 %shard_map.111 = (bf16[256,1024]{1,0:T(8,128)(2,1)}, bf16[256,1536]{1,0:T(8,128)(2,1)}, bf16[512,2048]{1,0:T(8,128)(2,1)}, bf16[2048,576]{1,0:T(8,128)(2,1)}) custom-call(bf16[2048,576]{1,0:T(8,128)(2,1)} %pad_maximum_fusion.lat_ref, s32[2048,1]{1,0:T(8,128)} %fusion.1.posk_ref, s32[1,256]{1,0:T(1,128)} %fusion.58.posq_ref, f32[256,1]{1,0:T(8,128)} %copy.54.tw_ref, ...), custom_call_target="tpu_custom_call" | custom-call | flops 20800000000 | bytes 16777216 | tf_op jit(solution)/shard_map/pallas_call | solution.py:91
  85.1 0.0 reduce-scatter.2.cloned.1.call-update
  85.2 1.4 slice.55
  86.6 0.6 copy.55
  87.2 0.8 collective-permute-start.5
  88.0 2.6 %collective-permute-done.5 = bf16[1024,576]{0,1:T(8,128)(2,1)} collective-permute-done((bf16[1024,576]{0,1:T(8,128)(2,1)S(1)}, bf16[1024,576]{0,1:T(8,128)(2,1)}, u32[]{:S(2)}, u32[]{:S(2)}) %collective-permute-start.5) | collective-permute-done | bytes 1179680 | tf_op jit(solution)/shard_map/ppermute | solution.py:127
  90.6 1.7 %copy.56 = bf16[1024,576]{1,0:T(8,128)(2,1)S(1)} copy(bf16[1024,576]{0,1:T(8,128)(2,1)} %collective-permute-done.5) | data formatting | bytes 2359296 | tf_op jit(solution)/shard_map/ppermute | solution.py:127
  92.3 1.7 %convert_add_fusion = (f32[1024,576]{1,0:T(8,128)S(1)}, bf16[1024,576]{1,0:T(8,128)(2,1)S(1)}) fusion(bf16[1024,576]{1,0:T(8,128)(2,1)S(1)} %copy.56, bf16[2048,576]{1,0:T(8,128)(2,1)} %get-tuple-element.10), kind=kLoop, calls=%fused_computation.1 | loop fusion | flops 2359296 | bytes 5898240 | tf_op jit(solution)/shard_map/add | solution.py:170
  93.9 0.1 fusion.64
  94.0 1.5 %collective-permute-start.6 = (bf16[256,576]{1,0:T(8,128)(2,1)S(1)}, bf16[256,576]{1,0:T(8,128)(2,1)S(1)}, u32[]{:S(2)}, u32[]{:S(2)}) collective-permute-start(bf16[256,576]{1,0:T(8,128)(2,1)S(1)} %get-tuple-element.20), channel_id=1, source_target_pairs={{0,16},{1,5},{4,20},{5,9},{8,24},{9,13},{12,28},{13,1},{64,80},{65... | collective-permute-start | bytes 884744 | tf_op jit(solution)/shard_map/ppermute | solution.py:135
  95.5 1.8 %collective-permute-start.8 = (bf16[256,576]{1,0:T(8,128)(2,1)S(1)}, bf16[256,576]{1,0:T(8,128)(2,1)S(1)}, u32[]{:S(2)}, u32[]{:S(2)}) collective-permute-start(bf16[256,576]{1,0:T(8,128)(2,1)S(1)} %get-tuple-element.21), channel_id=1, source_target_pairs={{0,48},{1,13},{4,52},{5,1},{8,56},{9,5},{12,60},{13,9},{64,112},{6... | collective-permute-start | bytes 884744 | tf_op jit(solution)/shard_map/ppermute | solution.py:135
  97.3 1.7 %collective-permute-start.7 = (bf16[256,576]{1,0:T(8,128)(2,1)S(1)}, bf16[256,576]{1,0:T(8,128)(2,1)S(1)}, u32[]{:S(2)}, u32[]{:S(2)}) collective-permute-start(bf16[256,576]{1,0:T(8,128)(2,1)S(1)} %get-tuple-element.22), channel_id=1, source_target_pairs={{0,32},{1,9},{4,36},{5,13},{8,40},{9,1},{12,44},{13,5},{64,96},{65... | collective-permute-start | bytes 884744 | tf_op jit(solution)/shard_map/ppermute | solution.py:135
  99.0 9.3 %collective-permute-done.6 = bf16[256,576]{1,0:T(8,128)(2,1)S(1)} collective-permute-done((bf16[256,576]{1,0:T(8,128)(2,1)S(1)}, bf16[256,576]{1,0:T(8,128)(2,1)S(1)}, u32[]{:S(2)}, u32[]{:S(2)}) %collective-permute-start.6) | collective-permute-done | bytes 294944 | tf_op jit(solution)/shard_map/ppermute | solution.py:135
  108.3 0.0 collective-permute-done.8
  108.3 13.1 %collective-permute-done.7 = bf16[256,576]{1,0:T(8,128)(2,1)S(1)} collective-permute-done((bf16[256,576]{1,0:T(8,128)(2,1)S(1)}, bf16[256,576]{1,0:T(8,128)(2,1)S(1)}, u32[]{:S(2)}, u32[]{:S(2)}) %collective-permute-start.7) | collective-permute-done | bytes 294944 | tf_op jit(solution)/shard_map/ppermute | solution.py:135
  121.4 0.2 fusion.63
  121.6 2.1 %collective-permute-start.9 = (bf16[64,576]{1,0:T(8,128)(2,1)S(1)}, bf16[64,576]{1,0:T(8,128)(2,1)S(1)}, u32[]{:S(2)}, u32[]{:S(2)}) collective-permute-start(bf16[64,576]{1,0:T(8,128)(2,1)S(1)} %get-tuple-element.23), channel_id=1, source_target_pairs={{0,4},{1,17},{4,8},{5,21},{8,12},{9,25},{12,0},{13,29},{64,68},{65... | collective-permute-start | bytes 221192 | tf_op jit(solution)/shard_map/ppermute | solution.py:135
  123.7 1.2 collective-permute-start.11
  124.9 1.5 collective-permute-start.10
  126.4 1.0 collective-permute-done.9
  127.4 0.8 collective-permute-done.11
  128.2 2.7 %collective-permute-done.10 = bf16[64,576]{1,0:T(8,128)(2,1)S(1)} collective-permute-done((bf16[64,576]{1,0:T(8,128)(2,1)S(1)}, bf16[64,576]{1,0:T(8,128)(2,1)S(1)}, u32[]{:S(2)}, u32[]{:S(2)}) %collective-permute-start.10) | collective-permute-done | bytes 73760 | tf_op jit(solution)/shard_map/ppermute | solution.py:135
  131.0 2.5 %collective-permute-start.12 = (bf16[16,576]{1,0:T(8,128)(2,1)S(1)}, bf16[16,576]{1,0:T(8,128)(2,1)S(1)}, u32[]{:S(2)}, u32[]{:S(2)}) collective-permute-start(bf16[16,576]{1,0:T(8,128)(2,1)S(1)} %get-tuple-element.28), channel_id=1, source_target_pairs={{0,64},{1,65},{2,66},{3,67},{4,68},{5,69},{6,70},{7,71},{8,72},{9,... | collective-permute-start | bytes 55304 | tf_op jit(solution)/shard_map/ppermute | solution.py:191
  133.5 1.7 %collective-permute-start.14 = (bf16[16,576]{1,0:T(8,128)(2,1)S(1)}, bf16[16,576]{1,0:T(8,128)(2,1)S(1)}, u32[]{:S(2)}, u32[]{:S(2)}) collective-permute-start(bf16[16,576]{1,0:T(8,128)(2,1)S(1)} %get-tuple-element.29), channel_id=1, source_target_pairs={{0,66},{1,67},{2,64},{3,65},{4,70},{5,71},{6,68},{7,69},{8,74},{9,... | collective-permute-start | bytes 55304 | tf_op jit(solution)/shard_map/ppermute | solution.py:191
  135.1 1.0 collective-permute-start.13
  136.1 0.0 collective-permute-done.12
  136.1 2.3 %collective-permute-done.14 = bf16[16,576]{1,0:T(8,128)(2,1)S(1)} collective-permute-done((bf16[16,576]{1,0:T(8,128)(2,1)S(1)}, bf16[16,576]{1,0:T(8,128)(2,1)S(1)}, u32[]{:S(2)}, u32[]{:S(2)}) %collective-permute-start.14) | collective-permute-done | bytes 18464 | tf_op jit(solution)/shard_map/ppermute | solution.py:191
  138.4 2.0 %collective-permute-done.13 = bf16[16,576]{1,0:T(8,128)(2,1)S(1)} collective-permute-done((bf16[16,576]{1,0:T(8,128)(2,1)S(1)}, bf16[16,576]{1,0:T(8,128)(2,1)S(1)}, u32[]{:S(2)}, u32[]{:S(2)}) %collective-permute-start.13) | collective-permute-done | bytes 18464 | tf_op jit(solution)/shard_map/ppermute | solution.py:191
  140.4 0.6 fusion.5
  141.0 1.8 %convert_element_type.62 = f32[64,2048]{1,0:T(8,128)} convert(bf16[64,2048]{1,0:T(8,128)(2,1)} %reduce-scatter.2.cloned.1.call-done) | non-fusion elementwise | flops 131072 | bytes 786432 | tf_op jit(solution)/shard_map/convert_element_type | solution.py:222
  (15 shorter events, 0.2 us)
Async XLA Ops:
  7.2 3.4 %copy-start.1 = (f32[256]{0:T(256)S(1)}, f32[256]{0:T(256)}, u32[]{:S(2)}) copy-start(f32[256]{0:T(256)} %param.14) | copy-start | bytes 3076
  7.2 3.4 %copy-start.2 = (f32[256]{0:T(256)S(1)}, f32[256]{0:T(256)}, u32[]{:S(2)}) copy-start(f32[256]{0:T(256)} %param.13) | copy-start | bytes 3076
  7.2 3.4 %copy-start.3 = (f32[256]{0:T(256)S(1)}, f32[256]{0:T(256)}, u32[]{:S(2)}) copy-start(f32[256]{0:T(256)} %param.12) | copy-start | bytes 3076
  7.2 133.8 %reduce-scatter.2.cloned.1.call-start = ((), (), s32[]{:S(2)}) async-start(), calls=%async_computation.1 | async-start | bytes 2359296 | tf_op jit(solution)/shard_map/reduce_scatter | solution.py:214
  8.5 12.2 %copy-start = (s32[16]{0:T(128)S(1)}, s32[16]{0:T(128)}, u32[]{:S(2)}) copy-start(s32[16]{0:T(128)} %param.15) | copy-start | bytes 196
  8.7 5.9 %collective-permute-start = (bf16[128,576]{1,0:T(8,128)(2,1)S(1)}, bf16[128,576]{1,0:T(8,128)(2,1)S(1)}, u32[]{:S(2)}, u32[]{:S(2)}) collective-permute-start(bf16[128,576]{1,0:T(8,128)(2,1)S(1)} %bitcast.32), channel_id=1, source_target_pairs={{0,64},{16,80},{32,96},{48,112},{64,0},{80,16},{96,32},{112,48},{1... | collective-permute-start | bytes 442376 | tf_op jit(solution)/shard_map/ppermute | solution.py:131
  15.5 12.4 %collective-permute-start.2 = (bf16[4,2,2,16,576]{4,3,2,1,0:T(8,128)(2,1)}, bf16[4,2,2,16,576]{4,3,2,1,0:T(8,128)(2,1)S(1)}, u32[]{:S(2)}, u32[]{:S(2)}) collective-permute-start(bf16[4,2,2,16,576]{4,3,2,1,0:T(8,128)(2,1)} %get-tuple-element.27), channel_id=1, source_target_pairs={{0,32},{1,33},{4,36},{5,37},{8,40},{9,41},{12,44},{13,45},{64,96},... | collective-permute-start | bytes 884744 | tf_op jit(solution)/shard_map/ppermute | solution.py:135
  18.7 14.4 %collective-permute-start.1 = (bf16[4,2,2,16,576]{4,3,2,1,0:T(8,128)(2,1)}, bf16[4,2,2,16,576]{4,3,2,1,0:T(8,128)(2,1)S(1)}, u32[]{:S(2)}, u32[]{:S(2)}) collective-permute-start(bf16[4,2,2,16,576]{4,3,2,1,0:T(8,128)(2,1)} %get-tuple-element.27), channel_id=1, source_target_pairs={{0,48},{1,49},{4,52},{5,53},{8,56},{9,57},{12,60},{13,61},{64,112}... | collective-permute-start | bytes 884744 | tf_op jit(solution)/shard_map/ppermute | solution.py:135
  19.8 13.3 %collective-permute-start.3 = (bf16[4,2,2,16,576]{4,3,2,1,0:T(8,128)(2,1)}, bf16[4,2,2,16,576]{4,3,2,1,0:T(8,128)(2,1)S(1)}, u32[]{:S(2)}, u32[]{:S(2)}) collective-permute-start(bf16[4,2,2,16,576]{4,3,2,1,0:T(8,128)(2,1)} %get-tuple-element.27), channel_id=1, source_target_pairs={{0,16},{1,17},{4,20},{5,21},{8,24},{9,25},{12,28},{13,29},{64,80},... | collective-permute-start | bytes 884744 | tf_op jit(solution)/shard_map/ppermute | solution.py:135
  34.9 3.2 %collective-permute-start.4 = (bf16[1024,576]{0,1:T(8,128)(2,1)}, bf16[1024,576]{0,1:T(8,128)(2,1)}, u32[]{:S(2)}, u32[]{:S(2)}) collective-permute-start(bf16[1024,576]{0,1:T(8,128)(2,1)} %copy.46), channel_id=1, source_target_pairs={{0,1},{1,0},{2,3},{3,2},{4,5},{5,4},{6,7},{7,6},{8,9},{9,8},{10,11... | collective-permute-start | bytes 3538952 | tf_op jit(solution)/shard_map/ppermute | solution.py:127
  87.2 3.4 %collective-permute-start.5 = (bf16[1024,576]{0,1:T(8,128)(2,1)S(1)}, bf16[1024,576]{0,1:T(8,128)(2,1)}, u32[]{:S(2)}, u32[]{:S(2)}) collective-permute-start(bf16[1024,576]{0,1:T(8,128)(2,1)S(1)} %copy.55), channel_id=1, source_target_pairs={{0,1},{1,0},{2,3},{3,2},{4,5},{5,4},{6,7},{7,6},{8,9},{9,8},{10,11... | collective-permute-start | bytes 3538952 | tf_op jit(solution)/shard_map/ppermute | solution.py:127
  94.0 14.3 %collective-permute-start.6 = (bf16[256,576]{1,0:T(8,128)(2,1)S(1)}, bf16[256,576]{1,0:T(8,128)(2,1)S(1)}, u32[]{:S(2)}, u32[]{:S(2)}) collective-permute-start(bf16[256,576]{1,0:T(8,128)(2,1)S(1)} %get-tuple-element.20), channel_id=1, source_target_pairs={{0,16},{1,5},{4,20},{5,9},{8,24},{9,13},{12,28},{13,1},{64,80},{65... | collective-permute-start | bytes 884744 | tf_op jit(solution)/shard_map/ppermute | solution.py:135
  95.5 12.8 %collective-permute-start.8 = (bf16[256,576]{1,0:T(8,128)(2,1)S(1)}, bf16[256,576]{1,0:T(8,128)(2,1)S(1)}, u32[]{:S(2)}, u32[]{:S(2)}) collective-permute-start(bf16[256,576]{1,0:T(8,128)(2,1)S(1)} %get-tuple-element.21), channel_id=1, source_target_pairs={{0,48},{1,13},{4,52},{5,1},{8,56},{9,5},{12,60},{13,9},{64,112},{6... | collective-permute-start | bytes 884744 | tf_op jit(solution)/shard_map/ppermute | solution.py:135
  97.3 24.1 %collective-permute-start.7 = (bf16[256,576]{1,0:T(8,128)(2,1)S(1)}, bf16[256,576]{1,0:T(8,128)(2,1)S(1)}, u32[]{:S(2)}, u32[]{:S(2)}) collective-permute-start(bf16[256,576]{1,0:T(8,128)(2,1)S(1)} %get-tuple-element.22), channel_id=1, source_target_pairs={{0,32},{1,9},{4,36},{5,13},{8,40},{9,1},{12,44},{13,5},{64,96},{65... | collective-permute-start | bytes 884744 | tf_op jit(solution)/shard_map/ppermute | solution.py:135
  121.6 5.7 %collective-permute-start.9 = (bf16[64,576]{1,0:T(8,128)(2,1)S(1)}, bf16[64,576]{1,0:T(8,128)(2,1)S(1)}, u32[]{:S(2)}, u32[]{:S(2)}) collective-permute-start(bf16[64,576]{1,0:T(8,128)(2,1)S(1)} %get-tuple-element.23), channel_id=1, source_target_pairs={{0,4},{1,17},{4,8},{5,21},{8,12},{9,25},{12,0},{13,29},{64,68},{65... | collective-permute-start | bytes 221192 | tf_op jit(solution)/shard_map/ppermute | solution.py:135
  123.7 4.4 %collective-permute-start.11 = (bf16[64,576]{1,0:T(8,128)(2,1)S(1)}, bf16[64,576]{1,0:T(8,128)(2,1)S(1)}, u32[]{:S(2)}, u32[]{:S(2)}) collective-permute-start(bf16[64,576]{1,0:T(8,128)(2,1)S(1)} %get-tuple-element.24), channel_id=1, source_target_pairs={{0,12},{1,49},{4,0},{5,53},{8,4},{9,57},{12,8},{13,61},{64,76},{65... | collective-permute-start | bytes 221192 | tf_op jit(solution)/shard_map/ppermute | solution.py:135
  124.9 5.9 %collective-permute-start.10 = (bf16[64,576]{1,0:T(8,128)(2,1)S(1)}, bf16[64,576]{1,0:T(8,128)(2,1)S(1)}, u32[]{:S(2)}, u32[]{:S(2)}) collective-permute-start(bf16[64,576]{1,0:T(8,128)(2,1)S(1)} %get-tuple-element.25), channel_id=1, source_target_pairs={{0,8},{1,33},{4,12},{5,37},{8,0},{9,41},{12,4},{13,45},{64,72},{65... | collective-permute-start | bytes 221192 | tf_op jit(solution)/shard_map/ppermute | solution.py:135
  131.0 5.2 %collective-permute-start.12 = (bf16[16,576]{1,0:T(8,128)(2,1)S(1)}, bf16[16,576]{1,0:T(8,128)(2,1)S(1)}, u32[]{:S(2)}, u32[]{:S(2)}) collective-permute-start(bf16[16,576]{1,0:T(8,128)(2,1)S(1)} %get-tuple-element.28), channel_id=1, source_target_pairs={{0,64},{1,65},{2,66},{3,67},{4,68},{5,69},{6,70},{7,71},{8,72},{9,... | collective-permute-start | bytes 55304 | tf_op jit(solution)/shard_map/ppermute | solution.py:191
  133.5 5.0 %collective-permute-start.14 = (bf16[16,576]{1,0:T(8,128)(2,1)S(1)}, bf16[16,576]{1,0:T(8,128)(2,1)S(1)}, u32[]{:S(2)}, u32[]{:S(2)}) collective-permute-start(bf16[16,576]{1,0:T(8,128)(2,1)S(1)} %get-tuple-element.29), channel_id=1, source_target_pairs={{0,66},{1,67},{2,64},{3,65},{4,70},{5,71},{6,68},{7,69},{8,74},{9,... | collective-permute-start | bytes 55304 | tf_op jit(solution)/shard_map/ppermute | solution.py:191
  135.1 5.3 %collective-permute-start.13 = (bf16[16,576]{1,0:T(8,128)(2,1)S(1)}, bf16[16,576]{1,0:T(8,128)(2,1)S(1)}, u32[]{:S(2)}, u32[]{:S(2)}) collective-permute-start(bf16[16,576]{1,0:T(8,128)(2,1)S(1)} %get-tuple-element.30), channel_id=1, source_target_pairs={{0,2},{1,3},{2,0},{3,1},{4,6},{5,7},{6,4},{7,5},{8,10},{9,11},{10,... | collective-permute-start | bytes 55304 | tf_op jit(solution)/shard_map/ppermute | solution.py:191
Sparse Core Ops, SparseCore 0:
  85.3 48.2 reduce-scatter.1

commit v2 on v0

v2 whole, which is shorter than its diff:
```python
import math

import jax
import jax.numpy as jnp
from jax import lax
from jax.experimental import pallas as pl
from jax.experimental.pallas import tpu as pltpu
from jax.sharding import PartitionSpec as P

NOPE = 128
VDIM = 128
KV_RANK = 512
QK = 192
LAT = 576
KEYS = 2048
ROWS = 256
BF = jnp.bfloat16
F32 = jnp.float32
SCALE = QK ** -0.5
SCALE_LOG2 = SCALE * math.log2(math.e)
AT_QUERY, AT_X, AT_YLO, AT_CORE = 128, 130, 131, 132


def mm(a, b):
    return jnp.dot(a, b, preferred_element_type=F32)


def mm_last(a, b):
    return lax.dot_general(a, b, (((1,), (1,)), ((), ())), preferred_element_type=F32)


def mm_first(a, b):
    return lax.dot_general(a, b, (((0,), (0,)), ((), ())), preferred_element_type=F32)


def prepare(ints, pieces, lat, lat_t, bias, keys):
    for i, piece in enumerate(pieces):
        rows = pl.ds(i * 256, 256)
        lat[rows, :] = piece[:, :KV_RANK]
        for hh in range(2):
            keys[hh, rows, NOPE:] = piece[:, KV_RANK:]
    for block in range(8):
        far = (block // 4 + ints[AT_YLO]) % 2
        slot = far * 4 + (block % 4 - ints[AT_X] + 4) % 4
        start = pl.multiple_of(slot * 64, 64)
        lat_t[pl.ds(start, 64), :] = lat[:, block * 64 : block * 64 + 64].T
    lane = lax.broadcasted_iota(jnp.int32, (16, ROWS), 1)
    query_pos = lane % 128 + jnp.where(lane < 128, ints[AT_QUERY], ints[AT_QUERY + 1])
    query_pos = query_pos - lax.broadcasted_iota(jnp.int32, (16, ROWS), 0)
    for i in range(128):
        bias[i * 16 : i * 16 + 16, :] = jnp.where(ints[i] <= query_pos, 0.0, -jnp.inf)


def head_pair(tw, q, g, w, out, dq, wg_keep, wg_send, lat, lat_t, bias, acc, keys, vals, scores, exps, dscores, dkv):
    q_t = q[...].T
    g_t = (g[...].T.astype(F32) * tw[...]).astype(BF)
    kv = mm(lat[...], w[...]).astype(BF)
    top = []
    for hh in range(2):
        keys[hh, :, :NOPE] = kv[:, hh * 256 : hh * 256 + NOPE]
        vals[hh] = kv[:, hh * 256 + NOPE : hh * 256 + 256]
        s = mm(keys[hh], q_t[hh * QK : hh * QK + QK]) + bias[...]
        scores[hh] = s
        top.append(jnp.max(s, axis=0, keepdims=True) * SCALE_LOG2)
    inverse, delta, q_s, g_s, g_h = [], [], [], [], []
    for hh in range(2):
        e = jnp.exp2(scores[hh] * SCALE_LOG2 - top[hh])
        exps[hh] = e.astype(BF)
        inv = 1.0 / jnp.sum(e, axis=0, keepdims=True)
        o_t = mm_first(vals[hh], exps[hh]) * inv
        gh = g_t[hh * VDIM : hh * VDIM + VDIM]
        delta.append(jnp.sum(o_t * gh.astype(F32), axis=0, keepdims=True))
        out[:, hh * VDIM : hh * VDIM + VDIM] = o_t.T.astype(BF)
        inverse.append(inv)
        g_h.append(gh)
        q_s.append((q_t[hh * QK : hh * QK + QK].astype(F32) * (inv * SCALE)).astype(BF))
        g_s.append((gh.astype(F32) * inv).astype(BF))
    rope = None
    for hh in range(2):
        dp = mm(vals[hh], g_h[hh])
        dscores[hh] = (exps[hh].astype(F32) * (dp - delta[hh])).astype(BF)
        dk = mm_last(dscores[hh], q_s[hh])
        dv = mm_last(exps[hh], g_s[hh])
        dkv[:, hh * 256 : hh * 256 + NOPE] = dk[:, :NOPE].astype(BF)
        dkv[:, hh * 256 + NOPE : hh * 256 + 256] = dv.astype(BF)
        rope = dk[:, NOPE:] if rope is None else rope + dk[:, NOPE:]
    acc[:, :KV_RANK] += mm_last(dkv[...], w[...])
    acc[:, KV_RANK:] += rope
    dq_t = [mm_first(keys[hh], dscores[hh]) * (inverse[hh] * SCALE) for hh in range(2)]
    dq[...] = jnp.concatenate(dq_t, axis=0).T.astype(BF)
    wg = mm(lat_t[...], dkv[...]).astype(BF)
    wg_keep[...] = wg[:256]
    wg_send[...] = wg[256:]


def first_body(ints, *refs):
    pieces, (tw, q, g, w, out, dq, wg_keep, wg_send, partial) = refs[:8], refs[8:17]
    scratch = refs[17:]
    lat, lat_t, bias, acc, keys = scratch[:5]

    @pl.when(pl.program_id(0) == 0)
    def _():
        prepare(ints, pieces, lat, lat_t, bias, keys)
        acc[...] = jnp.zeros_like(acc)

    head_pair(tw, q, g, w, out, dq, wg_keep, wg_send, *scratch)

    @pl.when(pl.program_id(0) == pl.num_programs(0) - 1)
    def _():
        partial[...] = acc[...].astype(BF)


def second_body(ints, *refs):
    pieces, (partial, tw, q, g, w, out, dq, wg_keep, wg_send, keep, send) = refs[:8], refs[10:21]
    scratch = refs[21:]
    lat, lat_t, bias, acc, keys = scratch[:5]

    @pl.when(pl.program_id(0) == 0)
    def _():
        prepare(ints, pieces, lat, lat_t, bias, keys)
        acc[...] = partial[...].astype(F32)

    head_pair(tw, q, g, w, out, dq, wg_keep, wg_send, *scratch)

    @pl.when(pl.program_id(0) == pl.num_programs(0) - 1)
    def _():
        core = ints[AT_CORE]
        for a in range(4):
            for b in range(4):
                x_first, z_first = a * 4 + b, b * 4 + a
                rows = pl.ds(x_first * 64, 64)
                keep[jnp.where(core == 0, x_first, z_first)] = acc[rows, :].astype(BF)
                rows = pl.ds(1024 + x_first * 64, 64)
                send[jnp.where(core == 0, z_first, x_first)] = acc[rows, :].astype(BF)


def attention(ints, pieces, tok_weight, queries, out_grad, up_weight, first_pair, pairs, before=None):
    def whole(shape):
        return pl.BlockSpec(shape, lambda i: (0,) * len(shape))

    def part(rows, columns):
        return pl.BlockSpec((rows, columns), lambda i: (0, i + first_pair))

    def made(rows, columns):
        return pl.BlockSpec((rows, columns), lambda i: (0, i))

    def shape(*dims):
        return jax.ShapeDtypeStruct(dims, BF)

    last = before is not None
    in_specs = [pl.BlockSpec(memory_space=pltpu.SMEM)] + [whole((256, LAT))] * 8
    if last:
        in_specs += [pl.BlockSpec(memory_space=pl.ANY)] * 2 + [whole((KEYS, LAT))]
    in_specs += [whole((1, ROWS)), part(ROWS, 2 * QK), part(ROWS, 2 * VDIM), part(KV_RANK, 512)]
    out_specs = [part(ROWS, 2 * VDIM), part(ROWS, 2 * QK), made(256, 512), made(256, 512)]
    out_shape = [
        shape(*out_grad.shape),
        shape(*queries.shape),
        shape(256, pairs * 512),
        shape(256, pairs * 512),
    ]
    if last:
        out_specs += [whole((16, 64, LAT))] * 2
        out_shape += [shape(16, 64, LAT)] * 2
    else:
        out_specs += [whole((KEYS, LAT))]
        out_shape += [shape(KEYS, LAT)]
    operands = [ints, *pieces] + (list(before) if last else [])
    return pl.pallas_call(
        second_body if last else first_body,
        grid=(pairs,),
        in_specs=in_specs,
        out_specs=out_specs,
        out_shape=out_shape,
        input_output_aliases={9: 0, 10: 1} if last else {},
        scratch_shapes=[
            pltpu.VMEM((KEYS, KV_RANK), BF),
            pltpu.VMEM((KV_RANK, KEYS), BF),
            pltpu.VMEM((KEYS, ROWS), F32),
            pltpu.VMEM((KEYS, LAT), F32),
            pltpu.VMEM((2, KEYS, QK), BF),
            pltpu.VMEM((2, KEYS, VDIM), BF),
            pltpu.VMEM((2, KEYS, ROWS), F32),
            pltpu.VMEM((2, KEYS, ROWS), BF),
            pltpu.VMEM((2, KEYS, ROWS), BF),
            pltpu.VMEM((KEYS, 512), BF),
        ],
        compiler_params=pltpu.CompilerParams(vmem_limit_bytes=56 * 2**20),
        cost_estimate=pl.CostEstimate(
            flops=2 * pairs * 3200 * 10**6, bytes_accessed=8 * 2**20, transcendentals=pairs * 2**20
        ),
    )(*operands, tok_weight, queries, out_grad, up_weight)


AXES = ("ctx", "head")


def device_index(x, y, z, core):
    return ((y % 2) * 4 + x) * 16 + z * 4 + (y // 2) * 2 + core


def send_shift(value, first, second):
    pairs = []
    for x in range(4):
        for y in range(4):
            for z in range(4):
                for core, (dx, dy, dz) in enumerate((first, second)):
                    target = device_index((x + dx) % 4, (y + dy) % 4, (z + dz) % 4, core)
                    pairs.append((device_index(x, y, z, core), target))
    return lax.ppermute(value, AXES, pairs)


def swap_cores(value):
    return lax.ppermute(value, "head", [(i, i ^ 1) for i in range(16)])


def swap_ylo(value):
    return lax.ppermute(value, "ctx", [(i, i ^ 4) for i in range(8)])


def swap_y(value, flip_hi, flip_lo):
    pairs = [
        (c * 16 + h, (c ^ (4 * flip_lo)) * 16 + (h ^ (2 * flip_hi)))
        for c in range(8)
        for h in range(16)
    ]
    return lax.ppermute(value, AXES, pairs)


def gather_latent(latent, z, y_hi, core):
    blocks = lax.dynamic_index_in_dim(latent.reshape(4, 2, 2, 16, LAT), core, 2, False)
    own = jnp.roll(blocks, (-z, -y_hi), (0, 1))
    pair = jnp.stack([own, swap_ylo(own)], axis=2)
    mine = [pair] + [send_shift(pair, (-k, 0, 0), (-k, 0, 0)) for k in (1, 2, 3)]
    other = [swap_cores(piece) for piece in mine]
    return [piece.reshape(256, LAT) for piece in mine + other]


def kernel_ints(x, y_lo, z, y_hi, core, group_order):
    block = jnp.arange(128, dtype=jnp.int32)
    which = core ^ (block // 64)
    far_x, far_z = (x + (block // 16) % 4) % 4, (z + (block // 4) % 4) % 4
    far_hi, far_lo = y_hi ^ ((block // 2) % 2), y_lo ^ (block % 2)
    row = ((far_lo * 4 + far_x) * 16 + far_z * 4 + far_hi * 2 + which) * 16
    groups = jnp.concatenate([row // 128, (y_lo * 4 + x) * 2 + jnp.arange(2, dtype=jnp.int32)])
    onehot = groups[:, None] == jnp.arange(16, dtype=jnp.int32)[None, :]
    starts = jnp.sum(jnp.where(onehot, group_order[None, :], 0), axis=1) * 128
    starts = starts + jnp.concatenate([row % 128, jnp.zeros((2,), jnp.int32)])
    return jnp.concatenate([starts, jnp.stack([x, y_lo, core])])


def sum_terms(first, others):
    total = first.astype(F32)
    for other in others:
        total = total + other.astype(F32)
    return total


def reduce_latent(keep, send):
    part = sum_terms(keep, [swap_cores(send)])
    wire = part.astype(BF)
    part = sum_terms(
        part[:4], [send_shift(wire[4 * k : 4 * k + 4], (k, 0, 0), (0, 0, k)) for k in (2, 1, 3)]
    )
    wire = part.astype(BF)
    part = sum_terms(part[0], [send_shift(wire[k], (0, 0, k), (k, 0, 0)) for k in (2, 1, 3)])
    part = part.reshape(4, 16, LAT)
    wire = part.astype(BF)
    return sum_terms(part[0], [swap_y(wire[k], k // 2, k % 2) for k in (3, 2, 1)])


def local(
    latent, queries, up_weight, out_grad, logratio, student_logprob, teacher_logprob, group_order
):
    ctx, head = lax.axis_index("ctx"), lax.axis_index("head")
    x, y_lo = ctx % 4, ctx // 4
    z, y_hi, core = head // 4, (head // 2) % 2, head % 2
    pieces = gather_latent(latent, z, y_hi, core)
    ints = kernel_ints(x, y_lo, z, y_hi, core, group_order)
    tok_weight = jnp.clip(jnp.exp(logratio), 0.8, 1.25) * (teacher_logprob - student_logprob)
    operands = (ints, pieces, tok_weight[None, :], queries, out_grad, up_weight)
    out_1, dq_1, wg_keep_1, wg_send_1, partial = attention(*operands, 0, 2)
    wg_1 = sum_terms(wg_keep_1, [swap_ylo(wg_send_1)])
    before = (out_1, dq_1, partial)
    attn_output, query_grad, wg_keep_2, wg_send_2, keep, send = attention(*operands, 2, 2, before)
    latent_grad = reduce_latent(keep, send)
    wg_2 = sum_terms(wg_keep_2, [swap_ylo(wg_send_2)])
    wg = jnp.concatenate([wg_1, wg_2], axis=1).reshape(4, 64, 2048)
    wire = wg.astype(BF)
    weight_grad = sum_terms(wg[0], [send_shift(wire[k], (k, 0, 0), (k, 0, 0)) for k in (2, 1, 3)])
    return (attn_output, query_grad, latent_grad, weight_grad)


def solution(mesh):
    placed = (
        P("ctx", None),
        P("ctx", "head"),
        P(None, "head"),
        P("ctx", "head"),
        P("ctx"),
        P("ctx"),
        P("ctx"),
        P(),
    )
    return jax.shard_map(
        local,
        mesh=mesh,
        in_specs=placed,
        out_specs=(P("ctx", "head"), P("ctx", "head"), P(AXES, None), P("ctx", "head")),
        check_vma=False,
    )
```

time: 903 us -> 124 us (0.14)
  waiting for transfers between devices: 740 us -> 39.3 us
  matrix products: 81.5 us -> 0 us
  Pallas kernels: 0 us -> 43.9 us
  local copies, waits for them, and re-layouts: 44.2 us -> 2.15 us
  starting transfers between devices: 0.12 us -> 32 us
  other arithmetic: 21.2 us -> 5.36 us
  between operations: 13.8 us -> 1.06 us
    reduce_scatter x2 -> x0, waiting for transfers between devices: 694 us -> none  [the longest x1 648 us: local(): lax.psum_scatter(latent_terms, ('ctx', 'head'), scatter_dimension=0, tile...]
    dot_general x72 -> x0, matrix products: 81.5 us -> none  [the longest x24 29.5 us: contract_last(): lax.dot_general(former, latter, (((1,), (1,)), ((), ())), preferred_eleme...]
    all_gather x1 -> x0, waiting for transfers between devices: 45.2 us -> none  [local(): gathered = lax.all_gather(latent, 'ctx', axis=0, tiled=True)]
    pallas_call x0 -> x2, Pallas kernels: none -> 43.9 us  [attention(): pl.pallas_call(second_body if last else first_body, grid=(pairs,), in_spe...]
    ppermute x0 -> x23, waiting for transfers between devices: none -> 39.3 us  [the longest x3 21.2 us: swap_ylo(): return lax.ppermute(value, 'ctx', [(i, i ^ 4) for i in range(8)])]
    ppermute x0 -> x23, starting transfers between devices: none -> 32 us  [the longest x12 20.9 us: send_shift(): return lax.ppermute(value, AXES, pairs)]
    while x49 -> x0, local copies, waits for them, and re-layouts: 23.2 us -> none
    add x9 -> x7, other arithmetic: 13.6 us -> 3.34 us  [the longest x5 3.33 us: sum_terms(): total = total + other.astype(F32)]
  transfers between devices with their start and end apart: 3 -> 23, of which waited for: 3 -> 10; matrix products, arithmetic and copies ran while one was open for 2% -> 4% of each run, Pallas kernels for 0% -> 0%
where the time goes in v2:
time: 124 us
  Pallas kernels  43.9 us (35%)
  waiting for transfers between devices  39.3 us (32%)
  starting transfers between devices  32 us (26%)
  other arithmetic  5.36 us (4%)
  local copies, waits for them, and re-layouts  2.15 us (2%)
    pallas_call x2, Pallas kernels, attention(): pl.pallas_call(second_body if last else first_body, grid=(pairs,), in_spe...  43.9 us
    ppermute x3, waiting for transfers between devices, swap_ylo(): return lax.ppermute(value, 'ctx', [(i, i ^ 4) for i in range(8)])  21.2 us
    ppermute x12, starting transfers between devices, send_shift(): return lax.ppermute(value, AXES, pairs)  20.9 us
    ppermute x12, waiting for transfers between devices, send_shift(): return lax.ppermute(value, AXES, pairs)  16.6 us
    ppermute x3, starting transfers between devices, swap_y(): return lax.ppermute(value, AXES, pairs)  6.42 us
    ppermute x3, starting transfers between devices, swap_ylo(): return lax.ppermute(value, 'ctx', [(i, i ^ 4) for i in range(8)])  3.76 us
    add x5, other arithmetic, sum_terms(): total = total + other.astype(F32)  3.33 us
  transfers between devices with their start and end apart: 23, of which 10 were waited for; matrix products, arithmetic and copies ran while one was open for 4% of the time, Pallas kernels for 0%

profile of v2, /device:TPU:0, one launch (start us, length us, event | category | flops | bytes accessed | tf_op | source)
XLA Modules:
  0.0 123.7 jit_solution(10878742684071831977)
XLA Ops:
  0.8 1.2 copy.16
  2.0 0.1 fusion.8
  2.1 0.1 fusion.7
  2.2 1.7 %collective-permute-start = (bf16[4,2,16,576]{3,2,1,0:T(8,128)(2,1)S(1)}, bf16[4,2,16,576]{3,2,1,0:T(8,128)(2,1)S(1)}, u32[]{:S(2)}, u32[]{:S(2)}) collective-permute-start(bf16[4,2,16,576]{3,2,1,0:T(8,128)(2,1)S(1)} %fusion.7), channel_id=1, source_target_pairs={{0,64},{16,80},{32,96},{48,112},{64,0},{80,16},{96,32},{112,48},{1... | collective-permute-start | bytes 442376 | tf_op jit(solution)/shard_map/ppermute | solution.py:218
  4.0 0.1 fusion.43
  4.1 4.0 %collective-permute-done = bf16[4,2,16,576]{3,2,1,0:T(8,128)(2,1)S(1)} collective-permute-done((bf16[4,2,16,576]{3,2,1,0:T(8,128)(2,1)S(1)}, bf16[4,2,16,576]{3,2,1,0:T(8,128)(2,1)S(1)}, u32[]{:S(2)}, u32[]{:S(2)}) %collective-permute-start) | collective-permute-done | bytes 147488 | tf_op jit(solution)/shard_map/ppermute | solution.py:218
  8.1 0.1 pad_maximum_fusion.1
  8.2 1.7 %collective-permute-start.3 = (bf16[4,2,2,16,576]{4,3,2,1,0:T(8,128)(2,1)S(1)}, bf16[4,2,2,16,576]{4,3,2,1,0:T(8,128)(2,1)S(1)}, u32[]{:S(2)}, u32[]{:S(2)}) collective-permute-start(bf16[4,2,2,16,576]{4,3,2,1,0:T(8,128)(2,1)S(1)} %pad_maximum_fusion.1), channel_id=1, source_target_pairs={{0,16},{1,17},{4,20},{5,21},{8,24},{9,25},{12,28},{13,29},{64,80},... | collective-permute-start | bytes 884744 | tf_op jit(solution)/shard_map/ppermute | solution.py:210
  9.9 2.7 %collective-permute-start.2 = (bf16[4,2,2,16,576]{4,3,2,1,0:T(8,128)(2,1)S(1)}, bf16[4,2,2,16,576]{4,3,2,1,0:T(8,128)(2,1)S(1)}, u32[]{:S(2)}, u32[]{:S(2)}) collective-permute-start(bf16[4,2,2,16,576]{4,3,2,1,0:T(8,128)(2,1)S(1)} %pad_maximum_fusion.1), channel_id=1, source_target_pairs={{0,32},{1,33},{4,36},{5,37},{8,40},{9,41},{12,44},{13,45},{64,96},... | collective-permute-start | bytes 884744 | tf_op jit(solution)/shard_map/ppermute | solution.py:210
  12.6 1.4 %collective-permute-start.1 = (bf16[4,2,2,16,576]{4,3,2,1,0:T(8,128)(2,1)S(1)}, bf16[4,2,2,16,576]{4,3,2,1,0:T(8,128)(2,1)S(1)}, u32[]{:S(2)}, u32[]{:S(2)}) collective-permute-start(bf16[4,2,2,16,576]{4,3,2,1,0:T(8,128)(2,1)S(1)} %pad_maximum_fusion.1), channel_id=1, source_target_pairs={{0,48},{1,49},{4,52},{5,53},{8,56},{9,57},{12,60},{13,61},{64,112}... | collective-permute-start | bytes 884744 | tf_op jit(solution)/shard_map/ppermute | solution.py:210
  14.1 0.1 select_reduce_fusion
  14.2 0.1 collective-permute-start.4
  14.3 4.6 %collective-permute-done.3 = bf16[4,2,2,16,576]{4,3,2,1,0:T(8,128)(2,1)S(1)} collective-permute-done((bf16[4,2,2,16,576]{4,3,2,1,0:T(8,128)(2,1)S(1)}, bf16[4,2,2,16,576]{4,3,2,1,0:T(8,128)(2,1)S(1)}, u32[]{:S(2)}, u32[]{:S(2)}) %collective-permute-start.3) | collective-permute-done | bytes 294944 | tf_op jit(solution)/shard_map/ppermute | solution.py:210
  18.9 7.3 %collective-permute-done.2 = bf16[4,2,2,16,576]{4,3,2,1,0:T(8,128)(2,1)S(1)} collective-permute-done((bf16[4,2,2,16,576]{4,3,2,1,0:T(8,128)(2,1)S(1)}, bf16[4,2,2,16,576]{4,3,2,1,0:T(8,128)(2,1)S(1)}, u32[]{:S(2)}, u32[]{:S(2)}) %collective-permute-start.2) | collective-permute-done | bytes 294944 | tf_op jit(solution)/shard_map/ppermute | solution.py:210
  26.2 0.0 collective-permute-start.6
  26.2 0.5 collective-permute-start.5
  26.7 0.6 pad_add_fusion.1.ints
  27.4 0.6 subtract_multiply_fusion
  28.0 0.0 collective-permute-done.7
  28.0 0.0 collective-permute-done.6
  28.0 0.3 collective-permute-done.5
  28.3 0.4 copy-done.11
  28.7 0.1 copy-done.12
  28.8 0.1 copy-done.13
  28.9 0.1 copy-done.14
  29.1 21.3 %shard_map.111 = (bf16[256,1024]{1,0:T(8,128)(2,1)}, bf16[256,1536]{1,0:T(8,128)(2,1)}, bf16[256,1024]{1,0:T(8,128)(2,1)}, bf16[256,1024]{1,0:T(8,128)(2,1)}, bf16[2048,576]{1,0:T(8,128)(2,1)}) custom-call(s32[133]{0:T(256)} %pad_add_fusion.1.ints, bf16[256,576]{1,0:T(8,128)(2,1)} %bitcast.34, bf16[256,576]{1,0:T(8,128)(2,1)} %bitcast.43, ...), custom_call_target="tpu_custom_call" | custom-call | flops 12800000000 | bytes 8388608 | tf_op jit(solution)/shard_map/pallas_call | solution.py:169
  50.4 22.6 %shard_map.112 = (bf16[256,1024]{1,0:T(8,128)(2,1)}, bf16[256,1536]{1,0:T(8,128)(2,1)}, bf16[256,1024]{1,0:T(8,128)(2,1)}, bf16[256,1024]{1,0:T(8,128)(2,1)}, bf...) custom-call(s32[133]{0:T(256)} %pad_add_fusion.1.ints, ...), custom_call_target="tpu_custom_call", output_to_operand_aliasing={{0}: (9, {}), {1}: (10, {})} | custom-call | flops 12800000000 | bytes 8388608 | tf_op jit(solution)/shard_map/pallas_call | solution.py:169
  73.0 0.4 collective-permute-start.8
  73.3 1.6 %collective-permute-start.19 = (bf16[256,1024]{1,0:T(8,128)(2,1)}, bf16[256,1024]{1,0:T(8,128)(2,1)S(1)}, u32[]{:S(2)}, u32[]{:S(2)}) collective-permute-start(bf16[256,1024]{1,0:T(8,128)(2,1)} %get-tuple-element.25), channel_id=1, source_target_pairs={{0,64},{16,80},{32,96},{48,112},{64,0},{80,16},{96,32},{112,48},{1... | collective-permute-start | bytes 1572872 | tf_op jit(solution)/shard_map/ppermute | solution.py:218
  74.9 0.4 collective-permute-start.18
  75.4 12.9 %collective-permute-done.19 = bf16[256,1024]{1,0:T(8,128)(2,1)S(1)} collective-permute-done((bf16[256,1024]{1,0:T(8,128)(2,1)}, bf16[256,1024]{1,0:T(8,128)(2,1)S(1)}, u32[]{:S(2)}, u32[]{:S(2)}) %collective-permute-start.19) | collective-permute-done | bytes 524320 | tf_op jit(solution)/shard_map/ppermute | solution.py:218
  88.3 1.2 convert_add_fusion.1
  89.5 0.0 collective-permute-done.8
  89.5 0.4 convert_add_fusion
  90.0 0.0 copy-start.1
  90.0 0.1 fusion.40
  90.1 2.5 %collective-permute-start.9 = (bf16[4,64,576]{2,1,0:T(8,128)(2,1)S(1)}, bf16[4,64,576]{2,1,0:T(8,128)(2,1)S(1)}, u32[]{:S(2)}, u32[]{:S(2)}) collective-permute-start(bf16[4,64,576]{2,1,0:T(8,128)(2,1)S(1)} %get-tuple-element.34), channel_id=1, source_target_pairs={{0,32},{1,9},{4,36},{5,13},{8,40},{9,1},{12,44},{13,5},{64,96},{65... | collective-permute-start | bytes 884744 | tf_op jit(solution)/shard_map/ppermute | solution.py:210
  92.5 1.3 %collective-permute-start.11 = (bf16[4,64,576]{2,1,0:T(8,128)(2,1)S(1)}, bf16[4,64,576]{2,1,0:T(8,128)(2,1)S(1)}, u32[]{:S(2)}, u32[]{:S(2)}) collective-permute-start(bf16[4,64,576]{2,1,0:T(8,128)(2,1)S(1)} %get-tuple-element.35), channel_id=1, source_target_pairs={{0,48},{1,13},{4,52},{5,1},{8,56},{9,5},{12,60},{13,9},{64,112},{6... | collective-permute-start | bytes 884744 | tf_op jit(solution)/shard_map/ppermute | solution.py:210
  93.8 0.8 collective-permute-start.10
  94.6 4.3 %collective-permute-done.18 = bf16[256,1024]{1,0:T(8,128)(2,1)S(1)} collective-permute-done((bf16[256,1024]{1,0:T(8,128)(2,1)S(1)}, bf16[256,1024]{1,0:T(8,128)(2,1)S(1)}, u32[]{:S(2)}, u32[]{:S(2)}) %collective-permute-start.18) | collective-permute-done | bytes 524320 | tf_op jit(solution)/shard_map/ppermute | solution.py:218
  98.8 0.2 convert_add_fusion.2
  99.0 0.1 fusion
  99.1 0.0 collective-permute-done.9
  99.2 2.3 %collective-permute-done.11 = bf16[4,64,576]{2,1,0:T(8,128)(2,1)S(1)} collective-permute-done((bf16[4,64,576]{2,1,0:T(8,128)(2,1)S(1)}, bf16[4,64,576]{2,1,0:T(8,128)(2,1)S(1)}, u32[]{:S(2)}, u32[]{:S(2)}) %collective-permute-start.11) | collective-permute-done | bytes 294944 | tf_op jit(solution)/shard_map/ppermute | solution.py:210
  101.5 0.7 collective-permute-done.10
  102.2 0.1 fusion.37
  102.4 4.0 %collective-permute-start.12 = (bf16[64,576]{1,0:T(8,128)(2,1)S(1)}, bf16[64,576]{1,0:T(8,128)(2,1)S(1)}, u32[]{:S(2)}, u32[]{:S(2)}) collective-permute-start(bf16[64,576]{1,0:T(8,128)(2,1)S(1)} %get-tuple-element.40), channel_id=1, source_target_pairs={{0,8},{1,33},{4,12},{5,37},{8,0},{9,41},{12,4},{13,45},{64,72},{65... | collective-permute-start | bytes 221192 | tf_op jit(solution)/shard_map/ppermute | solution.py:210
  106.4 0.7 collective-permute-start.14
  107.1 1.3 %collective-permute-start.13 = (bf16[64,576]{1,0:T(8,128)(2,1)S(1)}, bf16[64,576]{1,0:T(8,128)(2,1)S(1)}, u32[]{:S(2)}, u32[]{:S(2)}) collective-permute-start(bf16[64,576]{1,0:T(8,128)(2,1)S(1)} %get-tuple-element.42), channel_id=1, source_target_pairs={{0,4},{1,17},{4,8},{5,21},{8,12},{9,25},{12,0},{13,29},{64,68},{65... | collective-permute-start | bytes 221192 | tf_op jit(solution)/shard_map/ppermute | solution.py:210
  108.4 0.1 fusion.41
  108.5 2.5 %collective-permute-start.20 = (bf16[64,2048]{1,0:T(8,128)(2,1)S(1)}, bf16[64,2048]{1,0:T(8,128)(2,1)S(1)}, u32[]{:S(2)}, u32[]{:S(2)}) collective-permute-start(bf16[64,2048]{1,0:T(8,128)(2,1)S(1)} %get-tuple-element.37), channel_id=1, source_target_pairs={{0,32},{1,33},{4,36},{5,37},{8,40},{9,41},{12,44},{13,45},{64,96},... | collective-permute-start | bytes 786440 | tf_op jit(solution)/shard_map/ppermute | solution.py:210
  110.9 1.4 %collective-permute-start.22 = (bf16[64,2048]{1,0:T(8,128)(2,1)S(1)}, bf16[64,2048]{1,0:T(8,128)(2,1)S(1)}, u32[]{:S(2)}, u32[]{:S(2)}) collective-permute-start(bf16[64,2048]{1,0:T(8,128)(2,1)S(1)} %get-tuple-element.38), channel_id=1, source_target_pairs={{0,48},{1,49},{4,52},{5,53},{8,56},{9,57},{12,60},{13,61},{64,112}... | collective-permute-start | bytes 786440 | tf_op jit(solution)/shard_map/ppermute | solution.py:210
  112.3 0.0 collective-permute-done.12
  112.3 0.7 collective-permute-start.21
  113.0 0.0 collective-permute-done.14
  113.0 0.0 collective-permute-done.13
  113.0 3.1 %collective-permute-start.15 = (bf16[16,576]{1,0:T(8,128)(2,1)S(1)}, bf16[16,576]{1,0:T(8,128)(2,1)S(1)}, u32[]{:S(2)}, u32[]{:S(2)}) collective-permute-start(bf16[16,576]{1,0:T(8,128)(2,1)S(1)} %get-tuple-element.43), channel_id=1, source_target_pairs={{0,66},{1,67},{2,64},{3,65},{4,70},{5,71},{6,68},{7,69},{8,74},{9,... | collective-permute-start | bytes 55304 | tf_op jit(solution)/shard_map/ppermute | solution.py:227
  116.1 0.1 collective-permute-start.17
  116.3 1.5 %collective-permute-done.20 = bf16[64,2048]{1,0:T(8,128)(2,1)S(1)} collective-permute-done((bf16[64,2048]{1,0:T(8,128)(2,1)S(1)}, bf16[64,2048]{1,0:T(8,128)(2,1)S(1)}, u32[]{:S(2)}, u32[]{:S(2)}) %collective-permute-start.20) | collective-permute-done | bytes 262176 | tf_op jit(solution)/shard_map/ppermute | solution.py:210
  117.8 3.2 %collective-permute-start.16 = (bf16[16,576]{1,0:T(8,128)(2,1)S(1)}, bf16[16,576]{1,0:T(8,128)(2,1)S(1)}, u32[]{:S(2)}, u32[]{:S(2)}) collective-permute-start(bf16[16,576]{1,0:T(8,128)(2,1)S(1)} %get-tuple-element.45), channel_id=1, source_target_pairs={{0,2},{1,3},{2,0},{3,1},{4,6},{5,7},{6,4},{7,5},{8,10},{9,11},{10,... | collective-permute-start | bytes 55304 | tf_op jit(solution)/shard_map/ppermute | solution.py:227
  121.0 0.0 collective-permute-done.22
  121.0 0.9 fusion.6
  121.9 1.2 collective-permute-done.16
  123.1 0.6 fusion.13
  (40 shorter events, 0.2 us)
Async XLA Ops:
  0.6 13.4 %copy-start.6 = (s32[16]{0:T(128)S(1)}, s32[16]{0:T(128)}, u32[]{:S(2)}) copy-start(s32[16]{0:T(128)} %param.15) | copy-start | bytes 196
  0.6 26.7 %copy-start.3 = (f32[256]{0:T(256)S(1)}, f32[256]{0:T(256)}, u32[]{:S(2)}) copy-start(f32[256]{0:T(256)} %param.14) | copy-start | bytes 3076
  0.7 26.7 %copy-start.4 = (f32[256]{0:T(256)S(1)}, f32[256]{0:T(256)}, u32[]{:S(2)}) copy-start(f32[256]{0:T(256)} %param.13) | copy-start | bytes 3076
  0.7 26.7 %copy-start.5 = (f32[256]{0:T(256)S(1)}, f32[256]{0:T(256)}, u32[]{:S(2)}) copy-start(f32[256]{0:T(256)} %param.12) | copy-start | bytes 3076
  2.2 5.9 %collective-permute-start = (bf16[4,2,16,576]{3,2,1,0:T(8,128)(2,1)S(1)}, bf16[4,2,16,576]{3,2,1,0:T(8,128)(2,1)S(1)}, u32[]{:S(2)}, u32[]{:S(2)}) collective-permute-start(bf16[4,2,16,576]{3,2,1,0:T(8,128)(2,1)S(1)} %fusion.7), channel_id=1, source_target_pairs={{0,64},{16,80},{32,96},{48,112},{64,0},{80,16},{96,32},{112,48},{1... | collective-permute-start | bytes 442376 | tf_op jit(solution)/shard_map/ppermute | solution.py:218
  8.2 20.1 %copy-start.2 = (bf16[4,2,2,16,576]{4,3,2,1,0:T(8,128)(2,1)}, bf16[4,2,2,16,576]{4,3,2,1,0:T(8,128)(2,1)S(1)}, u32[]{:S(2)}) copy-start(bf16[4,2,2,16,576]{4,3,2,1,0:T(8,128)(2,1)S(1)} %pad_maximum_fusion.1) | copy-start | bytes 884740
  8.2 10.7 %collective-permute-start.3 = (bf16[4,2,2,16,576]{4,3,2,1,0:T(8,128)(2,1)S(1)}, bf16[4,2,2,16,576]{4,3,2,1,0:T(8,128)(2,1)S(1)}, u32[]{:S(2)}, u32[]{:S(2)}) collective-permute-start(bf16[4,2,2,16,576]{4,3,2,1,0:T(8,128)(2,1)S(1)} %pad_maximum_fusion.1), channel_id=1, source_target_pairs={{0,16},{1,17},{4,20},{5,21},{8,24},{9,25},{12,28},{13,29},{64,80},... | collective-permute-start | bytes 884744 | tf_op jit(solution)/shard_map/ppermute | solution.py:210
  9.9 16.3 %collective-permute-start.2 = (bf16[4,2,2,16,576]{4,3,2,1,0:T(8,128)(2,1)S(1)}, bf16[4,2,2,16,576]{4,3,2,1,0:T(8,128)(2,1)S(1)}, u32[]{:S(2)}, u32[]{:S(2)}) collective-permute-start(bf16[4,2,2,16,576]{4,3,2,1,0:T(8,128)(2,1)S(1)} %pad_maximum_fusion.1), channel_id=1, source_target_pairs={{0,32},{1,33},{4,36},{5,37},{8,40},{9,41},{12,44},{13,45},{64,96},... | collective-permute-start | bytes 884744 | tf_op jit(solution)/shard_map/ppermute | solution.py:210
  12.6 13.6 %collective-permute-start.1 = (bf16[4,2,2,16,576]{4,3,2,1,0:T(8,128)(2,1)S(1)}, bf16[4,2,2,16,576]{4,3,2,1,0:T(8,128)(2,1)S(1)}, u32[]{:S(2)}, u32[]{:S(2)}) collective-permute-start(bf16[4,2,2,16,576]{4,3,2,1,0:T(8,128)(2,1)S(1)} %pad_maximum_fusion.1), channel_id=1, source_target_pairs={{0,48},{1,49},{4,52},{5,53},{8,56},{9,57},{12,60},{13,61},{64,112}... | collective-permute-start | bytes 884744 | tf_op jit(solution)/shard_map/ppermute | solution.py:210
  14.2 13.8 %collective-permute-start.4 = (bf16[4,2,2,16,576]{4,3,2,1,0:T(8,128)(2,1)S(1)}, bf16[4,2,2,16,576]{4,3,2,1,0:T(8,128)(2,1)S(1)}, u32[]{:S(2)}, u32[]{:S(2)}) collective-permute-start(bf16[4,2,2,16,576]{4,3,2,1,0:T(8,128)(2,1)S(1)} %pad_maximum_fusion.1), channel_id=1, source_target_pairs={{0,1},{1,0},{2,3},{3,2},{4,5},{5,4},{6,7},{7,6},{8,9},{9,8},{10,11... | collective-permute-start | bytes 884744 | tf_op jit(solution)/shard_map/ppermute | solution.py:214
  18.9 9.4 %copy-start.8 = (bf16[4,2,2,16,576]{4,3,2,1,0:T(8,128)(2,1)}, bf16[4,2,2,16,576]{4,3,2,1,0:T(8,128)(2,1)S(1)}, u32[]{:S(2)}) copy-start(bf16[4,2,2,16,576]{4,3,2,1,0:T(8,128)(2,1)S(1)} %collective-permute-done.3) | copy-start | bytes 884740
  18.9 9.1 %collective-permute-start.7 = (bf16[4,2,2,16,576]{4,3,2,1,0:T(8,128)(2,1)S(1)}, bf16[4,2,2,16,576]{4,3,2,1,0:T(8,128)(2,1)S(1)}, u32[]{:S(2)}, u32[]{:S(2)}) collective-permute-start(bf16[4,2,2,16,576]{4,3,2,1,0:T(8,128)(2,1)S(1)} %collective-permute-done.3), channel_id=1, source_target_pairs={{0,1},{1,0},{2,3},{3,2},{4,5},{5,4},{6,7},{7,6},{8,9},{9,8},{10,11... | collective-permute-start | bytes 884744 | tf_op jit(solution)/shard_map/ppermute | solution.py:214
  26.2 2.1 %copy-start.9 = (bf16[4,2,2,16,576]{4,3,2,1,0:T(8,128)(2,1)}, bf16[4,2,2,16,576]{4,3,2,1,0:T(8,128)(2,1)S(1)}, u32[]{:S(2)}) copy-start(bf16[4,2,2,16,576]{4,3,2,1,0:T(8,128)(2,1)S(1)} %collective-permute-done.2) | copy-start | bytes 884740
  26.2 1.8 %collective-permute-start.6 = (bf16[4,2,2,16,576]{4,3,2,1,0:T(8,128)(2,1)S(1)}, bf16[4,2,2,16,576]{4,3,2,1,0:T(8,128)(2,1)S(1)}, u32[]{:S(2)}, u32[]{:S(2)}) collective-permute-start(bf16[4,2,2,16,576]{4,3,2,1,0:T(8,128)(2,1)S(1)} %collective-permute-done.2), channel_id=1, source_target_pairs={{0,1},{1,0},{2,3},{3,2},{4,5},{5,4},{6,7},{7,6},{8,9},{9,8},{10,11... | collective-permute-start | bytes 884744 | tf_op jit(solution)/shard_map/ppermute | solution.py:214
  26.2 2.1 %copy-start.10 = (bf16[4,2,2,16,576]{4,3,2,1,0:T(8,128)(2,1)}, bf16[4,2,2,16,576]{4,3,2,1,0:T(8,128)(2,1)S(1)}, u32[]{:S(2)}) copy-start(bf16[4,2,2,16,576]{4,3,2,1,0:T(8,128)(2,1)S(1)} %collective-permute-done.1) | copy-start | bytes 884740
  26.2 2.1 %collective-permute-start.5 = (bf16[4,2,2,16,576]{4,3,2,1,0:T(8,128)(2,1)S(1)}, bf16[4,2,2,16,576]{4,3,2,1,0:T(8,128)(2,1)S(1)}, u32[]{:S(2)}, u32[]{:S(2)}) collective-permute-start(bf16[4,2,2,16,576]{4,3,2,1,0:T(8,128)(2,1)S(1)} %collective-permute-done.1), channel_id=1, source_target_pairs={{0,1},{1,0},{2,3},{3,2},{4,5},{5,4},{6,7},{7,6},{8,9},{9,8},{10,11... | collective-permute-start | bytes 884744 | tf_op jit(solution)/shard_map/ppermute | solution.py:214
  28.0 0.8 copy-start.11
  28.0 0.9 copy-start.12
  28.0 0.9 copy-start.13
  28.3 0.8 copy-start.14
  50.4 24.6 %copy-start.7 = (bf16[256,1024]{1,0:T(8,128)(2,1)S(1)}, bf16[256,1024]{1,0:T(8,128)(2,1)}, u32[]{:S(2)}) copy-start(bf16[256,1024]{1,0:T(8,128)(2,1)} %get-tuple-element.23) | copy-start | bytes 1572868
  72.9 16.6 %copy-start = (bf16[16,64,576]{2,1,0:T(8,128)(2,1)S(1)}, bf16[16,64,576]{2,1,0:T(8,128)(2,1)}, u32[]{:S(2)}) copy-start(bf16[16,64,576]{2,1,0:T(8,128)(2,1)} %get-tuple-element.20) | copy-start | bytes 3538948
  73.0 16.6 %collective-permute-start.8 = (bf16[16,64,576]{2,1,0:T(8,128)(2,1)}, bf16[16,64,576]{2,1,0:T(8,128)(2,1)S(1)}, u32[]{:S(2)}, u32[]{:S(2)}) collective-permute-start(bf16[16,64,576]{2,1,0:T(8,128)(2,1)} %get-tuple-element.21), channel_id=1, source_target_pairs={{0,1},{1,0},{2,3},{3,2},{4,5},{5,4},{6,7},{7,6},{8,9},{9,8},{10,11... | collective-permute-start | bytes 3538952 | tf_op jit(solution)/shard_map/ppermute | solution.py:214
  73.3 15.0 %collective-permute-start.19 = (bf16[256,1024]{1,0:T(8,128)(2,1)}, bf16[256,1024]{1,0:T(8,128)(2,1)S(1)}, u32[]{:S(2)}, u32[]{:S(2)}) collective-permute-start(bf16[256,1024]{1,0:T(8,128)(2,1)} %get-tuple-element.25), channel_id=1, source_target_pairs={{0,64},{16,80},{32,96},{48,112},{64,0},{80,16},{96,32},{112,48},{1... | collective-permute-start | bytes 1572872 | tf_op jit(solution)/shard_map/ppermute | solution.py:218
  74.9 23.9 %collective-permute-start.18 = (bf16[256,1024]{1,0:T(8,128)(2,1)S(1)}, bf16[256,1024]{1,0:T(8,128)(2,1)S(1)}, u32[]{:S(2)}, u32[]{:S(2)}) collective-permute-start(bf16[256,1024]{1,0:T(8,128)(2,1)S(1)} %copy-done.7), channel_id=1, source_target_pairs={{0,64},{16,80},{32,96},{48,112},{64,0},{80,16},{96,32},{112,48},{1... | collective-permute-start | bytes 1572872 | tf_op jit(solution)/shard_map/ppermute | solution.py:218
  90.0 8.9 %copy-start.1 = (bf16[256,1024]{1,0:T(8,128)(2,1)S(1)}, bf16[256,1024]{1,0:T(8,128)(2,1)}, u32[]{:S(2)}) copy-start(bf16[256,1024]{1,0:T(8,128)(2,1)} %get-tuple-element.22) | copy-start | bytes 1572868
  90.1 9.1 %collective-permute-start.9 = (bf16[4,64,576]{2,1,0:T(8,128)(2,1)S(1)}, bf16[4,64,576]{2,1,0:T(8,128)(2,1)S(1)}, u32[]{:S(2)}, u32[]{:S(2)}) collective-permute-start(bf16[4,64,576]{2,1,0:T(8,128)(2,1)S(1)} %get-tuple-element.34), channel_id=1, source_target_pairs={{0,32},{1,9},{4,36},{5,13},{8,40},{9,1},{12,44},{13,5},{64,96},{65... | collective-permute-start | bytes 884744 | tf_op jit(solution)/shard_map/ppermute | solution.py:210
  92.5 9.0 %collective-permute-start.11 = (bf16[4,64,576]{2,1,0:T(8,128)(2,1)S(1)}, bf16[4,64,576]{2,1,0:T(8,128)(2,1)S(1)}, u32[]{:S(2)}, u32[]{:S(2)}) collective-permute-start(bf16[4,64,576]{2,1,0:T(8,128)(2,1)S(1)} %get-tuple-element.35), channel_id=1, source_target_pairs={{0,48},{1,13},{4,52},{5,1},{8,56},{9,5},{12,60},{13,9},{64,112},{6... | collective-permute-start | bytes 884744 | tf_op jit(solution)/shard_map/ppermute | solution.py:210
  93.8 8.4 %collective-permute-start.10 = (bf16[4,64,576]{2,1,0:T(8,128)(2,1)S(1)}, bf16[4,64,576]{2,1,0:T(8,128)(2,1)S(1)}, u32[]{:S(2)}, u32[]{:S(2)}) collective-permute-start(bf16[4,64,576]{2,1,0:T(8,128)(2,1)S(1)} %get-tuple-element.36), channel_id=1, source_target_pairs={{0,16},{1,5},{4,20},{5,9},{8,24},{9,13},{12,28},{13,1},{64,80},{65... | collective-permute-start | bytes 884744 | tf_op jit(solution)/shard_map/ppermute | solution.py:210
  102.4 9.9 %collective-permute-start.12 = (bf16[64,576]{1,0:T(8,128)(2,1)S(1)}, bf16[64,576]{1,0:T(8,128)(2,1)S(1)}, u32[]{:S(2)}, u32[]{:S(2)}) collective-permute-start(bf16[64,576]{1,0:T(8,128)(2,1)S(1)} %get-tuple-element.40), channel_id=1, source_target_pairs={{0,8},{1,33},{4,12},{5,37},{8,0},{9,41},{12,4},{13,45},{64,72},{65... | collective-permute-start | bytes 221192 | tf_op jit(solution)/shard_map/ppermute | solution.py:210
  106.4 6.6 %collective-permute-start.14 = (bf16[64,576]{1,0:T(8,128)(2,1)S(1)}, bf16[64,576]{1,0:T(8,128)(2,1)S(1)}, u32[]{:S(2)}, u32[]{:S(2)}) collective-permute-start(bf16[64,576]{1,0:T(8,128)(2,1)S(1)} %get-tuple-element.41), channel_id=1, source_target_pairs={{0,12},{1,49},{4,0},{5,53},{8,4},{9,57},{12,8},{13,61},{64,76},{65... | collective-permute-start | bytes 221192 | tf_op jit(solution)/shard_map/ppermute | solution.py:210
  107.1 5.9 %collective-permute-start.13 = (bf16[64,576]{1,0:T(8,128)(2,1)S(1)}, bf16[64,576]{1,0:T(8,128)(2,1)S(1)}, u32[]{:S(2)}, u32[]{:S(2)}) collective-permute-start(bf16[64,576]{1,0:T(8,128)(2,1)S(1)} %get-tuple-element.42), channel_id=1, source_target_pairs={{0,4},{1,17},{4,8},{5,21},{8,12},{9,25},{12,0},{13,29},{64,68},{65... | collective-permute-start | bytes 221192 | tf_op jit(solution)/shard_map/ppermute | solution.py:210
  108.5 9.3 %collective-permute-start.20 = (bf16[64,2048]{1,0:T(8,128)(2,1)S(1)}, bf16[64,2048]{1,0:T(8,128)(2,1)S(1)}, u32[]{:S(2)}, u32[]{:S(2)}) collective-permute-start(bf16[64,2048]{1,0:T(8,128)(2,1)S(1)} %get-tuple-element.37), channel_id=1, source_target_pairs={{0,32},{1,33},{4,36},{5,37},{8,40},{9,41},{12,44},{13,45},{64,96},... | collective-permute-start | bytes 786440 | tf_op jit(solution)/shard_map/ppermute | solution.py:210
  110.9 10.1 %collective-permute-start.22 = (bf16[64,2048]{1,0:T(8,128)(2,1)S(1)}, bf16[64,2048]{1,0:T(8,128)(2,1)S(1)}, u32[]{:S(2)}, u32[]{:S(2)}) collective-permute-start(bf16[64,2048]{1,0:T(8,128)(2,1)S(1)} %get-tuple-element.38), channel_id=1, source_target_pairs={{0,48},{1,49},{4,52},{5,53},{8,56},{9,57},{12,60},{13,61},{64,112}... | collective-permute-start | bytes 786440 | tf_op jit(solution)/shard_map/ppermute | solution.py:210
  112.3 8.7 %collective-permute-start.21 = (bf16[64,2048]{1,0:T(8,128)(2,1)S(1)}, bf16[64,2048]{1,0:T(8,128)(2,1)S(1)}, u32[]{:S(2)}, u32[]{:S(2)}) collective-permute-start(bf16[64,2048]{1,0:T(8,128)(2,1)S(1)} %get-tuple-element.39), channel_id=1, source_target_pairs={{0,16},{1,17},{4,20},{5,21},{8,24},{9,25},{12,28},{13,29},{64,80},... | collective-permute-start | bytes 786440 | tf_op jit(solution)/shard_map/ppermute | solution.py:210
  113.0 8.9 %collective-permute-start.15 = (bf16[16,576]{1,0:T(8,128)(2,1)S(1)}, bf16[16,576]{1,0:T(8,128)(2,1)S(1)}, u32[]{:S(2)}, u32[]{:S(2)}) collective-permute-start(bf16[16,576]{1,0:T(8,128)(2,1)S(1)} %get-tuple-element.43), channel_id=1, source_target_pairs={{0,66},{1,67},{2,64},{3,65},{4,70},{5,71},{6,68},{7,69},{8,74},{9,... | collective-permute-start | bytes 55304 | tf_op jit(solution)/shard_map/ppermute | solution.py:227
  116.1 5.8 %collective-permute-start.17 = (bf16[16,576]{1,0:T(8,128)(2,1)S(1)}, bf16[16,576]{1,0:T(8,128)(2,1)S(1)}, u32[]{:S(2)}, u32[]{:S(2)}) collective-permute-start(bf16[16,576]{1,0:T(8,128)(2,1)S(1)} %get-tuple-element.44), channel_id=1, source_target_pairs={{0,64},{1,65},{2,66},{3,67},{4,68},{5,69},{6,70},{7,71},{8,72},{9,... | collective-permute-start | bytes 55304 | tf_op jit(solution)/shard_map/ppermute | solution.py:227
  117.8 5.3 %collective-permute-start.16 = (bf16[16,576]{1,0:T(8,128)(2,1)S(1)}, bf16[16,576]{1,0:T(8,128)(2,1)S(1)}, u32[]{:S(2)}, u32[]{:S(2)}) collective-permute-start(bf16[16,576]{1,0:T(8,128)(2,1)S(1)} %get-tuple-element.45), channel_id=1, source_target_pairs={{0,2},{1,3},{2,0},{3,1},{4,6},{5,7},{6,4},{7,5},{8,10},{9,11},{10,... | collective-permute-start | bytes 55304 | tf_op jit(solution)/shard_map/ppermute | solution.py:227

commit v3 on v2

v3 whole, which is shorter than its diff:
```python
import math

import jax
import jax.numpy as jnp
from jax import lax
from jax.experimental import pallas as pl
from jax.experimental.pallas import tpu as pltpu
from jax.sharding import PartitionSpec as P

NOPE = 128
VDIM = 128
KV_RANK = 512
QK = 192
LAT = 576
KEYS = 2048
ROWS = 256
BF = jnp.bfloat16
F32 = jnp.float32
SCALE = QK ** -0.5
SCALE_LOG2 = SCALE * math.log2(math.e)
AT_QUERY, AT_X, AT_YLO, AT_Z, AT_CORE = 128, 130, 131, 132, 133


def mm(a, b):
    return jnp.dot(a, b, preferred_element_type=F32)


def mm_last(a, b):
    return lax.dot_general(a, b, (((1,), (1,)), ((), ())), preferred_element_type=F32)


def mm_first(a, b):
    return lax.dot_general(a, b, (((0,), (0,)), ((), ())), preferred_element_type=F32)


def prepare(ints, pieces, lat, lat_t, bias, keys):
    for i, piece in enumerate(pieces):
        rows = pl.ds(i * 256, 256)
        lat[rows, :] = piece[:, :KV_RANK]
        for hh in range(2):
            keys[hh, rows, NOPE:] = piece[:, KV_RANK:]
    for block in range(8):
        far = (block // 4 + ints[AT_YLO]) % 2
        slot = far * 4 + (block % 4 - ints[AT_X] + 4) % 4
        start = pl.multiple_of(slot * 64, 64)
        lat_t[pl.ds(start, 64), :] = lat[:, block * 64 : block * 64 + 64].T
    lane = lax.broadcasted_iota(jnp.int32, (16, ROWS), 1)
    query_pos = lane % 128 + jnp.where(lane < 128, ints[AT_QUERY], ints[AT_QUERY + 1])
    query_pos = query_pos - lax.broadcasted_iota(jnp.int32, (16, ROWS), 0)
    for i in range(128):
        bias[i * 16 : i * 16 + 16, :] = jnp.where(ints[i] <= query_pos, 0.0, -jnp.inf)


def head_pair(tw, q, g, w, out, dq, lat, lat_t, bias, acc, keys, vals, scores, exps, dscores, dkv):
    q_t = q[...].T
    g_t = (g[...].T.astype(F32) * tw[...]).astype(BF)
    kv = mm(lat[...], w[...]).astype(BF)
    top = []
    for hh in range(2):
        keys[hh, :, :NOPE] = kv[:, hh * 256 : hh * 256 + NOPE]
        vals[hh] = kv[:, hh * 256 + NOPE : hh * 256 + 256]
        s = mm(keys[hh], q_t[hh * QK : hh * QK + QK]) + bias[...]
        scores[hh] = s
        top.append(jnp.max(s, axis=0, keepdims=True) * SCALE_LOG2)
    inverse, delta, q_s, g_s, g_h = [], [], [], [], []
    for hh in range(2):
        e = jnp.exp2(scores[hh] * SCALE_LOG2 - top[hh])
        exps[hh] = e.astype(BF)
        inv = 1.0 / jnp.sum(e, axis=0, keepdims=True)
        o_t = mm_first(vals[hh], exps[hh]) * inv
        gh = g_t[hh * VDIM : hh * VDIM + VDIM]
        delta.append(jnp.sum(o_t * gh.astype(F32), axis=0, keepdims=True))
        out[:, hh * VDIM : hh * VDIM + VDIM] = o_t.T.astype(BF)
        inverse.append(inv)
        g_h.append(gh)
        q_s.append((q_t[hh * QK : hh * QK + QK].astype(F32) * (inv * SCALE)).astype(BF))
        g_s.append((gh.astype(F32) * inv).astype(BF))
    rope = None
    for hh in range(2):
        dp = mm(vals[hh], g_h[hh])
        dscores[hh] = (exps[hh].astype(F32) * (dp - delta[hh])).astype(BF)
        dk = mm_last(dscores[hh], q_s[hh])
        dv = mm_last(exps[hh], g_s[hh])
        dkv[:, hh * 256 : hh * 256 + NOPE] = dk[:, :NOPE].astype(BF)
        dkv[:, hh * 256 + NOPE : hh * 256 + 256] = dv.astype(BF)
        rope = dk[:, NOPE:] if rope is None else rope + dk[:, NOPE:]
    acc[:, :KV_RANK] += mm_last(dkv[...], w[...])
    acc[:, KV_RANK:] += rope
    dq_t = [mm_first(keys[hh], dscores[hh]) * (inverse[hh] * SCALE) for hh in range(2)]
    dq[...] = jnp.concatenate(dq_t, axis=0).T.astype(BF)
    return mm(lat_t[...], dkv[...]).astype(BF)


def body(ints, *refs):
    pieces, (tw, q, g, w, out, dq, wg_1, wg_2, keep, send) = refs[:8], refs[8:18]
    scratch = refs[18:]
    lat, lat_t, bias, acc, keys = scratch[:5]
    step = pl.program_id(0)

    @pl.when(step == 0)
    def _():
        prepare(ints, pieces, lat, lat_t, bias, keys)
        acc[...] = jnp.zeros_like(acc)

    wg = head_pair(tw, q, g, w, out, dq, *scratch)

    @pl.when(step < 2)
    def _():
        for slot in range(2):
            wg_1[slot] = wg[slot * 256 : slot * 256 + 256]

    @pl.when(step >= 2)
    def _():
        for slot in range(4):
            for near in range(2):
                rows = near * 256 + slot * 64
                wg_2[slot, near * 64 : near * 64 + 64, :] = wg[rows : rows + 64]

    @pl.when(step == pl.num_programs(0) - 1)
    def _():
        core = ints[AT_CORE]
        for dx in range(4):
            for z in range(4):
                x_first = dx * 4 + z
                z_first = (z - ints[AT_Z] + 4) % 4 * 4 + (dx + ints[AT_X]) % 4
                rows = pl.ds(x_first * 64, 64)
                keep[jnp.where(core == 0, x_first, z_first)] = acc[rows, :].astype(BF)
                rows = pl.ds(1024 + x_first * 64, 64)
                send[jnp.where(core == 0, z_first, x_first)] = acc[rows, :].astype(BF)


def attention(ints, pieces, tok_weight, queries, out_grad, up_weight):
    def whole(shape):
        return pl.BlockSpec(shape, lambda i: (0,) * len(shape))

    def columns(rows, width):
        return pl.BlockSpec((rows, width), lambda i: (0, i))

    def shape(*dims):
        return jax.ShapeDtypeStruct(dims, BF)

    return pl.pallas_call(
        body,
        grid=(4,),
        in_specs=[pl.BlockSpec(memory_space=pltpu.SMEM)]
        + [whole((256, LAT))] * 8
        + [whole((1, ROWS)), columns(ROWS, 2 * QK), columns(ROWS, 2 * VDIM), columns(KV_RANK, 512)],
        out_specs=[
            columns(ROWS, 2 * VDIM),
            columns(ROWS, 2 * QK),
            pl.BlockSpec((2, 256, 512), lambda i: (0, 0, jnp.minimum(i, 1))),
            pl.BlockSpec((4, 128, 512), lambda i: (0, 0, jnp.maximum(i - 2, 0))),
            whole((16, 64, LAT)),
            whole((16, 64, LAT)),
        ],
        out_shape=[
            shape(*out_grad.shape),
            shape(*queries.shape),
            shape(2, 256, 1024),
            shape(4, 128, 1024),
            shape(16, 64, LAT),
            shape(16, 64, LAT),
        ],
        scratch_shapes=[
            pltpu.VMEM((KEYS, KV_RANK), BF),
            pltpu.VMEM((KV_RANK, KEYS), BF),
            pltpu.VMEM((KEYS, ROWS), F32),
            pltpu.VMEM((KEYS, LAT), F32),
            pltpu.VMEM((2, KEYS, QK), BF),
            pltpu.VMEM((2, KEYS, VDIM), BF),
            pltpu.VMEM((2, KEYS, ROWS), F32),
            pltpu.VMEM((2, KEYS, ROWS), BF),
            pltpu.VMEM((2, KEYS, ROWS), BF),
            pltpu.VMEM((KEYS, 512), BF),
        ],
        compiler_params=pltpu.CompilerParams(vmem_limit_bytes=56 * 2**20),
        cost_estimate=pl.CostEstimate(
            flops=26 * 10**9, bytes_accessed=16 * 2**20, transcendentals=2**22
        ),
    )(ints, *pieces, tok_weight, queries, out_grad, up_weight)


AXES = ("ctx", "head")


def device_index(x, y, z, core):
    return ((y % 2) * 4 + x) * 16 + z * 4 + (y // 2) * 2 + core


def send_shift(value, first, second):
    pairs = []
    for x in range(4):
        for y in range(4):
            for z in range(4):
                for core, (dx, dy, dz) in enumerate((first, second)):
                    target = device_index((x + dx) % 4, (y + dy) % 4, (z + dz) % 4, core)
                    pairs.append((device_index(x, y, z, core), target))
    return lax.ppermute(value, AXES, pairs)


def swap_cores(value):
    return lax.ppermute(value, "head", [(i, i ^ 1) for i in range(16)])


def swap_ylo(value):
    return lax.ppermute(value, "ctx", [(i, i ^ 4) for i in range(8)])


def exchange_rest(value):
    groups = [
        [device_index(x, yh * 2 + yl, z, 0) for z in range(4) for yh in range(2) for yl in range(2)]
        for x in range(4)
    ] + [
        [device_index(x, yh * 2 + yl, z, 1) for x in range(4) for yh in range(2) for yl in range(2)]
        for z in range(4)
    ]
    return lax.all_to_all(value, AXES, 0, 0, tiled=True, axis_index_groups=groups)


def gather_latent(latent, y_lo, core):
    own = lax.dynamic_index_in_dim(latent.reshape(4, 2, 2, 16, LAT), core, 2, False)
    other = swap_ylo(own)
    low, high = jnp.where(y_lo == 0, own, other), jnp.where(y_lo == 0, other, own)
    pair = jnp.stack([low, high], axis=2)
    mine = [pair] + [send_shift(pair, (-k, 0, 0), (-k, 0, 0)) for k in (1, 2, 3)]
    other = [swap_cores(piece) for piece in mine]
    return [piece.reshape(256, LAT) for piece in mine + other]


def kernel_ints(x, y_lo, z, core, group_order):
    block = jnp.arange(128, dtype=jnp.int32)
    which = core ^ (block // 64)
    far_x = (x + (block // 16) % 4) % 4
    row = ((block % 2 * 4 + far_x) * 16 + (block // 4) % 4 * 4 + block // 2 % 2 * 2 + which) * 16
    groups = jnp.concatenate([row // 128, (y_lo * 4 + x) * 2 + jnp.arange(2, dtype=jnp.int32)])
    onehot = groups[:, None] == jnp.arange(16, dtype=jnp.int32)[None, :]
    starts = jnp.sum(jnp.where(onehot, group_order[None, :], 0), axis=1) * 128
    starts = starts + jnp.concatenate([row % 128, jnp.zeros((2,), jnp.int32)])
    return jnp.concatenate([starts, jnp.stack([x, y_lo, z, core])])


def sum_terms(first, others):
    total = first.astype(F32)
    for other in others:
        total = total + other.astype(F32)
    return total


def after(value, *earlier):
    return lax.optimization_barrier((value, *earlier))[0]


def reduce_terms(keep, send, wg_1, wg_2):
    def along_x(value):
        return [send_shift(value[k], (k, 0, 0), (k, 0, 0)) for k in (2, 1, 3)]

    swapped = swap_cores(send)
    near_1 = swap_ylo(wg_1[1])
    part = sum_terms(keep, [swapped])
    wire = part.astype(BF)
    terms = [send_shift(wire[4 * k : 4 * k + 4], (k, 0, 0), (0, 0, k)) for k in (2, 1, 3)]
    wg_2 = after(wg_2, wire)
    half_2 = sum_terms(wg_2[0], along_x(wg_2))
    near_2 = swap_ylo(half_2[64:].astype(BF))
    half_1 = sum_terms(wg_1[0], [near_1]).reshape(4, 64, 1024)
    far_1 = along_x(half_1.astype(BF))
    part = sum_terms(part[:4], terms).astype(BF)
    moved = exchange_rest(part.reshape(16, 16, LAT))
    latent_grad = sum_terms(moved[0], [moved[i] for i in range(1, 16)])
    weight_grad = [sum_terms(half_1[0], far_1), sum_terms(half_2[:64], [near_2])]
    return latent_grad, jnp.concatenate(weight_grad, axis=1)


def local(
    latent, queries, up_weight, out_grad, logratio, student_logprob, teacher_logprob, group_order
):
    ctx, head = lax.axis_index("ctx"), lax.axis_index("head")
    x, y_lo, z, core = ctx % 4, ctx // 4, head // 4, head % 2
    pieces = gather_latent(latent, y_lo, core)
    ints = kernel_ints(x, y_lo, z, core, group_order)
    tok_weight = jnp.clip(jnp.exp(logratio), 0.8, 1.25) * (teacher_logprob - student_logprob)
    attn_output, query_grad, wg_1, wg_2, keep, send = attention(
        ints, pieces, tok_weight[None, :], queries, out_grad, up_weight
    )
    latent_grad, weight_grad = reduce_terms(keep, send, wg_1, wg_2)
    return (attn_output, query_grad, latent_grad, weight_grad)


def solution(mesh):
    placed = (
        P("ctx", None),
        P("ctx", "head"),
        P(None, "head"),
        P("ctx", "head"),
        P("ctx"),
        P("ctx"),
        P("ctx"),
        P(),
    )
    return jax.shard_map(
        local,
        mesh=mesh,
        in_specs=placed,
        out_specs=(P("ctx", "head"), P("ctx", "head"), P(AXES, None), P("ctx", "head")),
        check_vma=False,
    )
```

time: 124 us -> 129 us (1.040)
  waiting for transfers between devices: 39.3 us -> 48.7 us
  Pallas kernels: 43.9 us -> 36.9 us
  local copies, waits for them, and re-layouts: 2.15 us -> 4.69 us
  other arithmetic: 5.36 us -> 4.06 us
    all_to_all x0 -> x1, waiting for transfers between devices: none -> 8.18 us  [exchange_rest(): lax.all_to_all(value, AXES, 0, 0, tiled=True, axis_index_groups=groups)]
    all_to_all x0 -> x1, starting transfers between devices: none -> 8.16 us  [exchange_rest(): lax.all_to_all(value, AXES, 0, 0, tiled=True, axis_index_groups=groups)]
    pallas_call x2 -> x1, Pallas kernels: 43.9 us -> 36.9 us  [attention(): pl.pallas_call(body, grid=(4,), in_specs=[pl.BlockSpec(memory_space=pltpu...]
    ppermute x12, waiting for transfers between devices: 16.6 us -> 23.5 us  [send_shift(): return lax.ppermute(value, AXES, pairs)]
    ppermute x3 -> x0, starting transfers between devices: 6.42 us -> none  [swap_y(): return lax.ppermute(value, AXES, pairs)]
    ppermute x3, waiting for transfers between devices: 21.2 us -> 16.7 us  [swap_ylo(): return lax.ppermute(value, 'ctx', [(i, i ^ 4) for i in range(8)])]
    add x5 -> x4, other arithmetic: 3.33 us -> 0.91 us  [sum_terms(): total = total + other.astype(F32)]
    ppermute x12, starting transfers between devices: 20.9 us -> 18.9 us  [send_shift(): return lax.ppermute(value, AXES, pairs)]
  transfers between devices with their start and end apart: 23 -> 21, of which waited for: 10 -> 11; matrix products, arithmetic and copies ran while one was open for 4% -> 4% of each run, Pallas kernels for 0% -> 0%
where the time goes in v3:
time: 129 us; the launch traced here: 128 us
  waiting for transfers between devices  48.7 us (38%)
  Pallas kernels  36.9 us (29%)
  starting transfers between devices  33.1 us (26%)
  local copies, waits for them, and re-layouts  4.69 us (4%)
  other arithmetic  4.06 us (3%)
    pallas_call x1, Pallas kernels, attention(): pl.pallas_call(body, grid=(4,), in_specs=[pl.BlockSpec(memory_space=pltpu...  36.9 us
    ppermute x12, waiting for transfers between devices, send_shift(): return lax.ppermute(value, AXES, pairs)  23.5 us
    ppermute x12, starting transfers between devices, send_shift(): return lax.ppermute(value, AXES, pairs)  18.9 us
    ppermute x3, waiting for transfers between devices, swap_ylo(): return lax.ppermute(value, 'ctx', [(i, i ^ 4) for i in range(8)])  16.7 us
    all_to_all x1, waiting for transfers between devices, exchange_rest(): lax.all_to_all(value, AXES, 0, 0, tiled=True, axis_index_groups=groups)  8.18 us
    all_to_all x1, starting transfers between devices, exchange_rest(): lax.all_to_all(value, AXES, 0, 0, tiled=True, axis_index_groups=groups)  8.16 us
    ppermute x3, starting transfers between devices, swap_ylo(): return lax.ppermute(value, 'ctx', [(i, i ^ 4) for i in range(8)])  5.06 us
    unnamed x31, local copies, waits for them, and re-layouts  2.76 us
  transfers between devices with their start and end apart: 21, of which 11 were waited for; matrix products, arithmetic and copies ran while one was open for 4% of the time, Pallas kernels for 0%

profile of v3, /device:TPU:0, one launch (start us, length us, event | category | flops | bytes accessed | tf_op | source)
XLA Modules:
  0.0 128.3 jit_solution(7437769802208053053)
XLA Ops:
  0.7 1.2 copy.16
  1.9 1.7 %collective-permute-start = (bf16[4,2,16,576]{3,2,1,0:T(8,128)(2,1)S(1)}, bf16[4,2,16,576]{3,2,1,0:T(8,128)(2,1)S(1)}, u32[]{:S(2)}, u32[]{:S(2)}) collective-permute-start(bf16[4,2,16,576]{3,2,1,0:T(8,128)(2,1)S(1)} %dynamic-slice_bitcast_fusion), channel_id=1, source_target_pairs={{0,64},{16,80},{32,96},{48,112},{64,0},{80,16},{96,32},{112,48},{1... | collective-permute-start | bytes 442376 | tf_op jit(solution)/shard_map/ppermute | solution.py:206
  3.7 4.2 %collective-permute-done = bf16[4,2,16,576]{3,2,1,0:T(8,128)(2,1)S(1)} collective-permute-done((bf16[4,2,16,576]{3,2,1,0:T(8,128)(2,1)S(1)}, bf16[4,2,16,576]{3,2,1,0:T(8,128)(2,1)S(1)}, u32[]{:S(2)}, u32[]{:S(2)}) %collective-permute-start) | collective-permute-done | bytes 147488 | tf_op jit(solution)/shard_map/ppermute | solution.py:206
  7.9 0.1 pad_maximum_fusion.1
  7.9 0.0 copy-start.3
  7.9 1.7 %collective-permute-start.3 = (bf16[4,2,2,16,576]{4,3,2,1,0:T(8,128)(2,1)S(1)}, bf16[4,2,2,16,576]{4,3,2,1,0:T(8,128)(2,1)S(1)}, u32[]{:S(2)}, u32[]{:S(2)}) collective-permute-start(bf16[4,2,2,16,576]{4,3,2,1,0:T(8,128)(2,1)S(1)} %pad_maximum_fusion.1), channel_id=1, source_target_pairs={{0,16},{1,17},{4,20},{5,21},{8,24},{9,25},{12,28},{13,29},{64,80},... | collective-permute-start | bytes 884744 | tf_op jit(solution)/shard_map/ppermute | solution.py:198
  9.7 2.7 %collective-permute-start.2 = (bf16[4,2,2,16,576]{4,3,2,1,0:T(8,128)(2,1)S(1)}, bf16[4,2,2,16,576]{4,3,2,1,0:T(8,128)(2,1)S(1)}, u32[]{:S(2)}, u32[]{:S(2)}) collective-permute-start(bf16[4,2,2,16,576]{4,3,2,1,0:T(8,128)(2,1)S(1)} %pad_maximum_fusion.1), channel_id=1, source_target_pairs={{0,32},{1,33},{4,36},{5,37},{8,40},{9,41},{12,44},{13,45},{64,96},... | collective-permute-start | bytes 884744 | tf_op jit(solution)/shard_map/ppermute | solution.py:198
  12.4 1.4 %collective-permute-start.1 = (bf16[4,2,2,16,576]{4,3,2,1,0:T(8,128)(2,1)S(1)}, bf16[4,2,2,16,576]{4,3,2,1,0:T(8,128)(2,1)S(1)}, u32[]{:S(2)}, u32[]{:S(2)}) collective-permute-start(bf16[4,2,2,16,576]{4,3,2,1,0:T(8,128)(2,1)S(1)} %pad_maximum_fusion.1), channel_id=1, source_target_pairs={{0,48},{1,49},{4,52},{5,53},{8,56},{9,57},{12,60},{13,61},{64,112}... | collective-permute-start | bytes 884744 | tf_op jit(solution)/shard_map/ppermute | solution.py:198
  13.9 0.1 select_reduce_fusion
  13.9 0.1 collective-permute-start.4
  14.0 4.6 %collective-permute-done.3 = bf16[4,2,2,16,576]{4,3,2,1,0:T(8,128)(2,1)S(1)} collective-permute-done((bf16[4,2,2,16,576]{4,3,2,1,0:T(8,128)(2,1)S(1)}, bf16[4,2,2,16,576]{4,3,2,1,0:T(8,128)(2,1)S(1)}, u32[]{:S(2)}, u32[]{:S(2)}) %collective-permute-start.3) | collective-permute-done | bytes 294944 | tf_op jit(solution)/shard_map/ppermute | solution.py:198
  18.7 0.0 collective-permute-start.7
  18.7 7.3 %collective-permute-done.2 = bf16[4,2,2,16,576]{4,3,2,1,0:T(8,128)(2,1)S(1)} collective-permute-done((bf16[4,2,2,16,576]{4,3,2,1,0:T(8,128)(2,1)S(1)}, bf16[4,2,2,16,576]{4,3,2,1,0:T(8,128)(2,1)S(1)}, u32[]{:S(2)}, u32[]{:S(2)}) %collective-permute-start.2) | collective-permute-done | bytes 294944 | tf_op jit(solution)/shard_map/ppermute | solution.py:198
  26.0 0.0 collective-permute-start.6
  26.0 0.0 collective-permute-done.1
  26.0 0.5 collective-permute-start.5
  26.5 0.7 concatenate.14.ints
  27.2 0.6 subtract_multiply_fusion
  27.7 0.0 collective-permute-done.4
  27.8 0.0 collective-permute-done.7
  27.8 0.0 collective-permute-done.6
  27.8 0.3 collective-permute-done.5
  28.1 0.4 copy-done.11
  28.5 0.1 copy-done.12
  28.6 0.1 copy-done.13
  28.7 0.1 copy-done.14
  28.8 36.9 %shard_map.111 = (bf16[256,1024]{1,0:T(8,128)(2,1)}, bf16[256,1536]{1,0:T(8,128)(2,1)}, bf16[2,256,1024]{2,1,0:T(8,128)(2,1)}, bf16[4,128,1024]{2,1,0:T(8,128)(2...) custom-call(s32[134]{0:T(256)} %concatenate.14.ints, bf16[256,576]{1,0:T(8,128)(2,1)} %bitcast.50, ...), custom_call_target="tpu_custom_call" | custom-call | flops 25999998976 | bytes 16777216 | tf_op jit(solution)/shard_map/pallas_call | solution.py:142
  65.7 0.4 collective-permute-start.8
  66.1 1.1 slice_bitcast_fusion
  67.2 1.7 %collective-permute-start.12 = (bf16[256,1024]{1,0:T(8,128)(2,1)S(1)}, bf16[256,1024]{1,0:T(8,128)(2,1)S(1)}, u32[]{:S(2)}, u32[]{:S(2)}) collective-permute-start(bf16[256,1024]{1,0:T(8,128)(2,1)S(1)} %slice_bitcast_fusion), channel_id=1, source_target_pairs={{0,64},{16,80},{32,96},{48,112},{64,0},{80,16},{96,32},{112,48},{1... | collective-permute-start | bytes 1572872 | tf_op jit(solution)/shard_map/ppermute | solution.py:206
  68.9 12.5 %collective-permute-done.12 = bf16[256,1024]{1,0:T(8,128)(2,1)S(1)} collective-permute-done((bf16[256,1024]{1,0:T(8,128)(2,1)S(1)}, bf16[256,1024]{1,0:T(8,128)(2,1)S(1)}, u32[]{:S(2)}, u32[]{:S(2)}) %collective-permute-start.12) | collective-permute-done | bytes 524320 | tf_op jit(solution)/shard_map/ppermute | solution.py:206
  81.3 0.2 fusion.23
  81.6 2.3 %collective-permute-start.13 = (bf16[64,1024]{1,0:T(8,128)(2,1)S(1)}, bf16[64,1024]{1,0:T(8,128)(2,1)S(1)}, u32[]{:S(2)}, u32[]{:S(2)}) collective-permute-start(bf16[64,1024]{1,0:T(8,128)(2,1)S(1)} %get-tuple-element.28), channel_id=1, source_target_pairs={{0,32},{1,33},{4,36},{5,37},{8,40},{9,41},{12,44},{13,45},{64,96},... | collective-permute-start | bytes 393224 | tf_op jit(solution)/shard_map/ppermute | solution.py:198
  83.9 0.0 collective-permute-done.8
  83.9 0.4 fusion.24
  84.3 0.8 copy-done.2
  85.1 0.1 slice_bitcast_fusion.3
  85.2 1.4 %collective-permute-start.16 = (bf16[128,1024]{1,0:T(8,128)(2,1)S(1)}, bf16[128,1024]{1,0:T(8,128)(2,1)S(1)}, u32[]{:S(2)}, u32[]{:S(2)}) collective-permute-start(bf16[128,1024]{1,0:T(8,128)(2,1)S(1)} %get-tuple-element.25), channel_id=1, source_target_pairs={{0,32},{1,33},{4,36},{5,37},{8,40},{9,41},{12,44},{13,45},{64,96},... | collective-permute-start | bytes 786440 | tf_op jit(solution)/shard_map/ppermute | solution.py:198
  86.6 1.7 %collective-permute-start.15 = (bf16[64,1024]{1,0:T(8,128)(2,1)S(1)}, bf16[64,1024]{1,0:T(8,128)(2,1)S(1)}, u32[]{:S(2)}, u32[]{:S(2)}) collective-permute-start(bf16[64,1024]{1,0:T(8,128)(2,1)S(1)} %get-tuple-element.29), channel_id=1, source_target_pairs={{0,48},{1,49},{4,52},{5,53},{8,56},{9,57},{12,60},{13,61},{64,112}... | collective-permute-start | bytes 393224 | tf_op jit(solution)/shard_map/ppermute | solution.py:198
  88.3 0.3 collective-permute-start.14
  88.6 3.0 %collective-permute-start.18 = (bf16[128,1024]{1,0:T(8,128)(2,1)S(1)}, bf16[128,1024]{1,0:T(8,128)(2,1)S(1)}, u32[]{:S(2)}, u32[]{:S(2)}) collective-permute-start(bf16[128,1024]{1,0:T(8,128)(2,1)S(1)} %get-tuple-element.26), channel_id=1, source_target_pairs={{0,48},{1,49},{4,52},{5,53},{8,56},{9,57},{12,60},{13,61},{64,112}... | collective-permute-start | bytes 786440 | tf_op jit(solution)/shard_map/ppermute | solution.py:198
  91.6 0.0 collective-permute-done.13
  91.6 0.0 collective-permute-start.17
  91.6 0.1 fusion.25
  91.7 5.8 %collective-permute-done.15 = bf16[64,1024]{1,0:T(8,128)(2,1)S(1)} collective-permute-done((bf16[64,1024]{1,0:T(8,128)(2,1)S(1)}, bf16[64,1024]{1,0:T(8,128)(2,1)S(1)}, u32[]{:S(2)}, u32[]{:S(2)}) %collective-permute-start.15) | collective-permute-done | bytes 131104 | tf_op jit(solution)/shard_map/ppermute | solution.py:198
  97.5 2.4 %collective-permute-start.9 = (bf16[4,64,576]{2,1,0:T(8,128)(2,1)S(1)}, bf16[4,64,576]{2,1,0:T(8,128)(2,1)S(1)}, u32[]{:S(2)}, u32[]{:S(2)}) collective-permute-start(bf16[4,64,576]{2,1,0:T(8,128)(2,1)S(1)} %get-tuple-element.22), channel_id=1, source_target_pairs={{0,32},{1,9},{4,36},{5,13},{8,40},{9,1},{12,44},{13,5},{64,96},{65... | collective-permute-start | bytes 884744 | tf_op jit(solution)/shard_map/ppermute | solution.py:198
  99.8 0.0 collective-permute-done.14
  99.8 0.3 collective-permute-start.11
  100.2 0.0 collective-permute-done.16
  100.2 1.7 %collective-permute-start.10 = (bf16[4,64,576]{2,1,0:T(8,128)(2,1)S(1)}, bf16[4,64,576]{2,1,0:T(8,128)(2,1)S(1)}, u32[]{:S(2)}, u32[]{:S(2)}) collective-permute-start(bf16[4,64,576]{2,1,0:T(8,128)(2,1)S(1)} %get-tuple-element.24), channel_id=1, source_target_pairs={{0,16},{1,5},{4,20},{5,9},{8,24},{9,13},{12,28},{13,1},{64,80},{65... | collective-permute-start | bytes 884744 | tf_op jit(solution)/shard_map/ppermute | solution.py:198
  101.8 0.1 fusion.6
  101.9 0.0 collective-permute-done.18
  101.9 0.5 collective-permute-done.17
  102.4 0.2 fusion.4
  102.6 1.7 %collective-permute-start.19 = (bf16[64,1024]{1,0:T(8,128)(2,1)S(1)}, bf16[64,1024]{1,0:T(8,128)(2,1)S(1)}, u32[]{:S(2)}, u32[]{:S(2)}) collective-permute-start(bf16[64,1024]{1,0:T(8,128)(2,1)S(1)} %slice.199), channel_id=1, source_target_pairs={{0,64},{16,80},{32,96},{48,112},{64,0},{80,16},{96,32},{112,48},{1... | collective-permute-start | bytes 393224 | tf_op jit(solution)/shard_map/ppermute | solution.py:206
  104.3 1.9 %collective-permute-done.9 = bf16[4,64,576]{2,1,0:T(8,128)(2,1)S(1)} collective-permute-done((bf16[4,64,576]{2,1,0:T(8,128)(2,1)S(1)}, bf16[4,64,576]{2,1,0:T(8,128)(2,1)S(1)}, u32[]{:S(2)}, u32[]{:S(2)}) %collective-permute-start.9) | collective-permute-done | bytes 294944 | tf_op jit(solution)/shard_map/ppermute | solution.py:198
  106.1 2.2 %collective-permute-done.11 = bf16[4,64,576]{2,1,0:T(8,128)(2,1)S(1)} collective-permute-done((bf16[4,64,576]{2,1,0:T(8,128)(2,1)S(1)}, bf16[4,64,576]{2,1,0:T(8,128)(2,1)S(1)}, u32[]{:S(2)}, u32[]{:S(2)}) %collective-permute-start.11) | collective-permute-done | bytes 294944 | tf_op jit(solution)/shard_map/ppermute | solution.py:198
  108.4 1.2 collective-permute-done.10
  109.5 0.9 fusion.2
  110.4 8.2 %all-to-all-start = ((bf16[16,16,576]{2,1,0:T(8,128)(2,1)}), bf16[16,16,576]{2,1,0:T(8,128)(2,1)S(1)}, u32[]{:S(2)}, u32[]{:S(2)}) async-start(bf16[16,16,576]{2,1,0:T(8,128)(2,1)} %bitcast.18), calls=%async_computation | async-start | bytes 655360 | tf_op jit(solution)/shard_map/all_to_all | solution.py:217
  118.6 0.0 collective-permute-done.19
  118.7 0.8 pad_maximum_fusion
  119.5 8.2 %all-to-all-done = bf16[16,16,576]{2,1,0:T(8,128)(2,1)S(1)} async-done(((bf16[16,16,576]{2,1,0:T(8,128)(2,1)}), bf16[16,16,576]{2,1,0:T(8,128)(2,1)S(1)}, u32[]{:S(2)}, u32[]{:S(2)}) %all-to-all-start) | async-done | bytes 294944 | tf_op jit(solution)/shard_map/all_to_all | solution.py:217
  127.7 0.7 convert_add_fusion.3
  (33 shorter events, 0.2 us)
Async XLA Ops:
  0.6 13.2 %copy-start.7 = (s32[16]{0:T(128)S(1)}, s32[16]{0:T(128)}, u32[]{:S(2)}) copy-start(s32[16]{0:T(128)} %param.15) | copy-start | bytes 196
  0.6 26.5 %copy-start.4 = (f32[256]{0:T(256)S(1)}, f32[256]{0:T(256)}, u32[]{:S(2)}) copy-start(f32[256]{0:T(256)} %param.14) | copy-start | bytes 3076
  0.7 26.5 %copy-start.5 = (f32[256]{0:T(256)S(1)}, f32[256]{0:T(256)}, u32[]{:S(2)}) copy-start(f32[256]{0:T(256)} %param.13) | copy-start | bytes 3076
  0.7 26.5 %copy-start.6 = (f32[256]{0:T(256)S(1)}, f32[256]{0:T(256)}, u32[]{:S(2)}) copy-start(f32[256]{0:T(256)} %param.12) | copy-start | bytes 3076
  1.9 5.9 %collective-permute-start = (bf16[4,2,16,576]{3,2,1,0:T(8,128)(2,1)S(1)}, bf16[4,2,16,576]{3,2,1,0:T(8,128)(2,1)S(1)}, u32[]{:S(2)}, u32[]{:S(2)}) collective-permute-start(bf16[4,2,16,576]{3,2,1,0:T(8,128)(2,1)S(1)} %dynamic-slice_bitcast_fusion), channel_id=1, source_target_pairs={{0,64},{16,80},{32,96},{48,112},{64,0},{80,16},{96,32},{112,48},{1... | collective-permute-start | bytes 442376 | tf_op jit(solution)/shard_map/ppermute | solution.py:206
  7.9 20.1 %copy-start.3 = (bf16[4,2,2,16,576]{4,3,2,1,0:T(8,128)(2,1)}, bf16[4,2,2,16,576]{4,3,2,1,0:T(8,128)(2,1)S(1)}, u32[]{:S(2)}) copy-start(bf16[4,2,2,16,576]{4,3,2,1,0:T(8,128)(2,1)S(1)} %pad_maximum_fusion.1) | copy-start | bytes 884740
  7.9 10.7 %collective-permute-start.3 = (bf16[4,2,2,16,576]{4,3,2,1,0:T(8,128)(2,1)S(1)}, bf16[4,2,2,16,576]{4,3,2,1,0:T(8,128)(2,1)S(1)}, u32[]{:S(2)}, u32[]{:S(2)}) collective-permute-start(bf16[4,2,2,16,576]{4,3,2,1,0:T(8,128)(2,1)S(1)} %pad_maximum_fusion.1), channel_id=1, source_target_pairs={{0,16},{1,17},{4,20},{5,21},{8,24},{9,25},{12,28},{13,29},{64,80},... | collective-permute-start | bytes 884744 | tf_op jit(solution)/shard_map/ppermute | solution.py:198
  9.7 16.3 %collective-permute-start.2 = (bf16[4,2,2,16,576]{4,3,2,1,0:T(8,128)(2,1)S(1)}, bf16[4,2,2,16,576]{4,3,2,1,0:T(8,128)(2,1)S(1)}, u32[]{:S(2)}, u32[]{:S(2)}) collective-permute-start(bf16[4,2,2,16,576]{4,3,2,1,0:T(8,128)(2,1)S(1)} %pad_maximum_fusion.1), channel_id=1, source_target_pairs={{0,32},{1,33},{4,36},{5,37},{8,40},{9,41},{12,44},{13,45},{64,96},... | collective-permute-start | bytes 884744 | tf_op jit(solution)/shard_map/ppermute | solution.py:198
  12.4 13.6 %collective-permute-start.1 = (bf16[4,2,2,16,576]{4,3,2,1,0:T(8,128)(2,1)S(1)}, bf16[4,2,2,16,576]{4,3,2,1,0:T(8,128)(2,1)S(1)}, u32[]{:S(2)}, u32[]{:S(2)}) collective-permute-start(bf16[4,2,2,16,576]{4,3,2,1,0:T(8,128)(2,1)S(1)} %pad_maximum_fusion.1), channel_id=1, source_target_pairs={{0,48},{1,49},{4,52},{5,53},{8,56},{9,57},{12,60},{13,61},{64,112}... | collective-permute-start | bytes 884744 | tf_op jit(solution)/shard_map/ppermute | solution.py:198
  13.9 13.8 %collective-permute-start.4 = (bf16[4,2,2,16,576]{4,3,2,1,0:T(8,128)(2,1)S(1)}, bf16[4,2,2,16,576]{4,3,2,1,0:T(8,128)(2,1)S(1)}, u32[]{:S(2)}, u32[]{:S(2)}) collective-permute-start(bf16[4,2,2,16,576]{4,3,2,1,0:T(8,128)(2,1)S(1)} %pad_maximum_fusion.1), channel_id=1, source_target_pairs={{0,1},{1,0},{2,3},{3,2},{4,5},{5,4},{6,7},{7,6},{8,9},{9,8},{10,11... | collective-permute-start | bytes 884744 | tf_op jit(solution)/shard_map/ppermute | solution.py:202
  18.7 9.4 %copy-start.8 = (bf16[4,2,2,16,576]{4,3,2,1,0:T(8,128)(2,1)}, bf16[4,2,2,16,576]{4,3,2,1,0:T(8,128)(2,1)S(1)}, u32[]{:S(2)}) copy-start(bf16[4,2,2,16,576]{4,3,2,1,0:T(8,128)(2,1)S(1)} %collective-permute-done.3) | copy-start | bytes 884740
  18.7 9.1 %collective-permute-start.7 = (bf16[4,2,2,16,576]{4,3,2,1,0:T(8,128)(2,1)S(1)}, bf16[4,2,2,16,576]{4,3,2,1,0:T(8,128)(2,1)S(1)}, u32[]{:S(2)}, u32[]{:S(2)}) collective-permute-start(bf16[4,2,2,16,576]{4,3,2,1,0:T(8,128)(2,1)S(1)} %collective-permute-done.3), channel_id=1, source_target_pairs={{0,1},{1,0},{2,3},{3,2},{4,5},{5,4},{6,7},{7,6},{8,9},{9,8},{10,11... | collective-permute-start | bytes 884744 | tf_op jit(solution)/shard_map/ppermute | solution.py:202
  26.0 2.1 %copy-start.9 = (bf16[4,2,2,16,576]{4,3,2,1,0:T(8,128)(2,1)}, bf16[4,2,2,16,576]{4,3,2,1,0:T(8,128)(2,1)S(1)}, u32[]{:S(2)}) copy-start(bf16[4,2,2,16,576]{4,3,2,1,0:T(8,128)(2,1)S(1)} %collective-permute-done.2) | copy-start | bytes 884740
  26.0 1.8 %collective-permute-start.6 = (bf16[4,2,2,16,576]{4,3,2,1,0:T(8,128)(2,1)S(1)}, bf16[4,2,2,16,576]{4,3,2,1,0:T(8,128)(2,1)S(1)}, u32[]{:S(2)}, u32[]{:S(2)}) collective-permute-start(bf16[4,2,2,16,576]{4,3,2,1,0:T(8,128)(2,1)S(1)} %collective-permute-done.2), channel_id=1, source_target_pairs={{0,1},{1,0},{2,3},{3,2},{4,5},{5,4},{6,7},{7,6},{8,9},{9,8},{10,11... | collective-permute-start | bytes 884744 | tf_op jit(solution)/shard_map/ppermute | solution.py:202
  26.0 2.1 %copy-start.10 = (bf16[4,2,2,16,576]{4,3,2,1,0:T(8,128)(2,1)}, bf16[4,2,2,16,576]{4,3,2,1,0:T(8,128)(2,1)S(1)}, u32[]{:S(2)}) copy-start(bf16[4,2,2,16,576]{4,3,2,1,0:T(8,128)(2,1)S(1)} %collective-permute-done.1) | copy-start | bytes 884740
  26.0 2.1 %collective-permute-start.5 = (bf16[4,2,2,16,576]{4,3,2,1,0:T(8,128)(2,1)S(1)}, bf16[4,2,2,16,576]{4,3,2,1,0:T(8,128)(2,1)S(1)}, u32[]{:S(2)}, u32[]{:S(2)}) collective-permute-start(bf16[4,2,2,16,576]{4,3,2,1,0:T(8,128)(2,1)S(1)} %collective-permute-done.1), channel_id=1, source_target_pairs={{0,1},{1,0},{2,3},{3,2},{4,5},{5,4},{6,7},{7,6},{8,9},{9,8},{10,11... | collective-permute-start | bytes 884744 | tf_op jit(solution)/shard_map/ppermute | solution.py:202
  27.8 0.7 copy-start.11
  27.8 0.8 copy-start.12
  27.8 0.9 copy-start.13
  28.1 0.8 copy-start.14
  65.7 15.6 %copy-start.1 = (bf16[2,256,1024]{2,1,0:T(8,128)(2,1)S(1)}, bf16[2,256,1024]{2,1,0:T(8,128)(2,1)}, u32[]{:S(2)}) copy-start(bf16[2,256,1024]{2,1,0:T(8,128)(2,1)} %get-tuple-element.15) | copy-start | bytes 3145732
  65.7 18.2 %collective-permute-start.8 = (bf16[16,64,576]{2,1,0:T(8,128)(2,1)}, bf16[16,64,576]{2,1,0:T(8,128)(2,1)S(1)}, u32[]{:S(2)}, u32[]{:S(2)}) collective-permute-start(bf16[16,64,576]{2,1,0:T(8,128)(2,1)} %get-tuple-element.14), channel_id=1, source_target_pairs={{0,1},{1,0},{2,3},{3,2},{4,5},{5,4},{6,7},{7,6},{8,9},{9,8},{10,11... | collective-permute-start | bytes 3538952 | tf_op jit(solution)/shard_map/ppermute | solution.py:202
  67.2 16.7 %copy-start = (bf16[16,64,576]{2,1,0:T(8,128)(2,1)S(1)}, bf16[16,64,576]{2,1,0:T(8,128)(2,1)}, u32[]{:S(2)}) copy-start(bf16[16,64,576]{2,1,0:T(8,128)(2,1)} %get-tuple-element.13) | copy-start | bytes 3538948
  67.2 14.1 %collective-permute-start.12 = (bf16[256,1024]{1,0:T(8,128)(2,1)S(1)}, bf16[256,1024]{1,0:T(8,128)(2,1)S(1)}, u32[]{:S(2)}, u32[]{:S(2)}) collective-permute-start(bf16[256,1024]{1,0:T(8,128)(2,1)S(1)} %slice_bitcast_fusion), channel_id=1, source_target_pairs={{0,64},{16,80},{32,96},{48,112},{64,0},{80,16},{96,32},{112,48},{1... | collective-permute-start | bytes 1572872 | tf_op jit(solution)/shard_map/ppermute | solution.py:206
  81.6 10.0 %collective-permute-start.13 = (bf16[64,1024]{1,0:T(8,128)(2,1)S(1)}, bf16[64,1024]{1,0:T(8,128)(2,1)S(1)}, u32[]{:S(2)}, u32[]{:S(2)}) collective-permute-start(bf16[64,1024]{1,0:T(8,128)(2,1)S(1)} %get-tuple-element.28), channel_id=1, source_target_pairs={{0,32},{1,33},{4,36},{5,37},{8,40},{9,41},{12,44},{13,45},{64,96},... | collective-permute-start | bytes 393224 | tf_op jit(solution)/shard_map/ppermute | solution.py:198
  83.9 1.2 copy-start.2
  85.2 15.0 %collective-permute-start.16 = (bf16[128,1024]{1,0:T(8,128)(2,1)S(1)}, bf16[128,1024]{1,0:T(8,128)(2,1)S(1)}, u32[]{:S(2)}, u32[]{:S(2)}) collective-permute-start(bf16[128,1024]{1,0:T(8,128)(2,1)S(1)} %get-tuple-element.25), channel_id=1, source_target_pairs={{0,32},{1,33},{4,36},{5,37},{8,40},{9,41},{12,44},{13,45},{64,96},... | collective-permute-start | bytes 786440 | tf_op jit(solution)/shard_map/ppermute | solution.py:198
  86.6 10.9 %collective-permute-start.15 = (bf16[64,1024]{1,0:T(8,128)(2,1)S(1)}, bf16[64,1024]{1,0:T(8,128)(2,1)S(1)}, u32[]{:S(2)}, u32[]{:S(2)}) collective-permute-start(bf16[64,1024]{1,0:T(8,128)(2,1)S(1)} %get-tuple-element.29), channel_id=1, source_target_pairs={{0,48},{1,49},{4,52},{5,53},{8,56},{9,57},{12,60},{13,61},{64,112}... | collective-permute-start | bytes 393224 | tf_op jit(solution)/shard_map/ppermute | solution.py:198
  88.3 11.5 %collective-permute-start.14 = (bf16[64,1024]{1,0:T(8,128)(2,1)S(1)}, bf16[64,1024]{1,0:T(8,128)(2,1)S(1)}, u32[]{:S(2)}, u32[]{:S(2)}) collective-permute-start(bf16[64,1024]{1,0:T(8,128)(2,1)S(1)} %get-tuple-element.30), channel_id=1, source_target_pairs={{0,16},{1,17},{4,20},{5,21},{8,24},{9,25},{12,28},{13,29},{64,80},... | collective-permute-start | bytes 393224 | tf_op jit(solution)/shard_map/ppermute | solution.py:198
  88.6 13.3 %collective-permute-start.18 = (bf16[128,1024]{1,0:T(8,128)(2,1)S(1)}, bf16[128,1024]{1,0:T(8,128)(2,1)S(1)}, u32[]{:S(2)}, u32[]{:S(2)}) collective-permute-start(bf16[128,1024]{1,0:T(8,128)(2,1)S(1)} %get-tuple-element.26), channel_id=1, source_target_pairs={{0,48},{1,49},{4,52},{5,53},{8,56},{9,57},{12,60},{13,61},{64,112}... | collective-permute-start | bytes 786440 | tf_op jit(solution)/shard_map/ppermute | solution.py:198
  91.6 10.9 %collective-permute-start.17 = (bf16[128,1024]{1,0:T(8,128)(2,1)S(1)}, bf16[128,1024]{1,0:T(8,128)(2,1)S(1)}, u32[]{:S(2)}, u32[]{:S(2)}) collective-permute-start(bf16[128,1024]{1,0:T(8,128)(2,1)S(1)} %get-tuple-element.27), channel_id=1, source_target_pairs={{0,16},{1,17},{4,20},{5,21},{8,24},{9,25},{12,28},{13,29},{64,80},... | collective-permute-start | bytes 786440 | tf_op jit(solution)/shard_map/ppermute | solution.py:198
  97.5 8.7 %collective-permute-start.9 = (bf16[4,64,576]{2,1,0:T(8,128)(2,1)S(1)}, bf16[4,64,576]{2,1,0:T(8,128)(2,1)S(1)}, u32[]{:S(2)}, u32[]{:S(2)}) collective-permute-start(bf16[4,64,576]{2,1,0:T(8,128)(2,1)S(1)} %get-tuple-element.22), channel_id=1, source_target_pairs={{0,32},{1,9},{4,36},{5,13},{8,40},{9,1},{12,44},{13,5},{64,96},{65... | collective-permute-start | bytes 884744 | tf_op jit(solution)/shard_map/ppermute | solution.py:198
  99.8 8.6 %collective-permute-start.11 = (bf16[4,64,576]{2,1,0:T(8,128)(2,1)S(1)}, bf16[4,64,576]{2,1,0:T(8,128)(2,1)S(1)}, u32[]{:S(2)}, u32[]{:S(2)}) collective-permute-start(bf16[4,64,576]{2,1,0:T(8,128)(2,1)S(1)} %get-tuple-element.23), channel_id=1, source_target_pairs={{0,48},{1,13},{4,52},{5,1},{8,56},{9,5},{12,60},{13,9},{64,112},{6... | collective-permute-start | bytes 884744 | tf_op jit(solution)/shard_map/ppermute | solution.py:198
  100.2 9.4 %collective-permute-start.10 = (bf16[4,64,576]{2,1,0:T(8,128)(2,1)S(1)}, bf16[4,64,576]{2,1,0:T(8,128)(2,1)S(1)}, u32[]{:S(2)}, u32[]{:S(2)}) collective-permute-start(bf16[4,64,576]{2,1,0:T(8,128)(2,1)S(1)} %get-tuple-element.24), channel_id=1, source_target_pairs={{0,16},{1,5},{4,20},{5,9},{8,24},{9,13},{12,28},{13,1},{64,80},{65... | collective-permute-start | bytes 884744 | tf_op jit(solution)/shard_map/ppermute | solution.py:198
  102.6 16.0 %collective-permute-start.19 = (bf16[64,1024]{1,0:T(8,128)(2,1)S(1)}, bf16[64,1024]{1,0:T(8,128)(2,1)S(1)}, u32[]{:S(2)}, u32[]{:S(2)}) collective-permute-start(bf16[64,1024]{1,0:T(8,128)(2,1)S(1)} %slice.199), channel_id=1, source_target_pairs={{0,64},{16,80},{32,96},{48,112},{64,0},{80,16},{96,32},{112,48},{1... | collective-permute-start | bytes 393224 | tf_op jit(solution)/shard_map/ppermute | solution.py:206
  110.4 17.2 %all-to-all-start = ((bf16[16,16,576]{2,1,0:T(8,128)(2,1)}), bf16[16,16,576]{2,1,0:T(8,128)(2,1)S(1)}, u32[]{:S(2)}, u32[]{:S(2)}) async-start(bf16[16,16,576]{2,1,0:T(8,128)(2,1)} %bitcast.18), calls=%async_computation | async-start | bytes 655360 | tf_op jit(solution)/shard_map/all_to_all | solution.py:217

commit v4 on v3

v4 whole, which is shorter than its diff:
```python
import math

import jax
import jax.numpy as jnp
from jax import lax
from jax.experimental import pallas as pl
from jax.experimental.pallas import tpu as pltpu
from jax.sharding import PartitionSpec as P

NOPE = 128
VDIM = 128
KV_RANK = 512
QK = 192
LAT = 576
KEYS = 2048
ROWS = 512
BF = jnp.bfloat16
F32 = jnp.float32
SCALE = QK ** -0.5
SCALE_LOG2 = SCALE * math.log2(math.e)
AT_QUERY, AT_X, AT_YLO, AT_Z, AT_CORE = 128, 132, 133, 134, 135


def mm(a, b):
    return jnp.dot(a, b, preferred_element_type=F32)


def mm_last(a, b):
    return lax.dot_general(a, b, (((1,), (1,)), ((), ())), preferred_element_type=F32)


def mm_first(a, b):
    return lax.dot_general(a, b, (((0,), (0,)), ((), ())), preferred_element_type=F32)


def prepare(ints, pieces, lat, lat_t, bias, keys):
    for i, piece in enumerate(pieces):
        rows = pl.ds(i * 256, 256)
        lat[rows, :] = piece[:, :KV_RANK]
        for hh in range(2):
            keys[hh, rows, NOPE:] = piece[:, KV_RANK:]
    for block in range(8):
        near = (block // 4 + ints[AT_YLO]) % 2
        start = pl.multiple_of((block % 4 - ints[AT_X] + 4) % 4 * 128 + near * 64, 64)
        lat_t[pl.ds(start, 64), :] = lat[:, block * 64 : block * 64 + 64].T
    lane = lax.broadcasted_iota(jnp.int32, (16, ROWS), 1)
    query_pos = lane % 128 - lax.broadcasted_iota(jnp.int32, (16, ROWS), 0)
    for group in range(4):
        query_pos = query_pos + jnp.where(lane // 128 == group, ints[AT_QUERY + group], 0)
    for i in range(128):
        bias[i * 16 : i * 16 + 16, :] = jnp.where(ints[i] <= query_pos, 0.0, -jnp.inf)


def head_pair(q_t, g_t, w, lat, lat_t, bias, acc, keys, vals, scores, exps, dscores, dkv):
    kv = mm(lat[...], w[...]).astype(BF)
    top = []
    for hh in range(2):
        keys[hh, :, :NOPE] = kv[:, hh * 256 : hh * 256 + NOPE]
        vals[hh] = kv[:, hh * 256 + NOPE : hh * 256 + 256]
        s = mm(keys[hh], q_t[hh * QK : hh * QK + QK]) + bias[...]
        scores[hh] = s
        top.append(jnp.max(s, axis=0, keepdims=True) * SCALE_LOG2)
    out, inverse, delta, q_s, g_s, g_h = [], [], [], [], [], []
    for hh in range(2):
        e = jnp.exp2(scores[hh] * SCALE_LOG2 - top[hh])
        exps[hh] = e.astype(BF)
        inv = 1.0 / jnp.sum(e, axis=0, keepdims=True)
        o_t = mm_first(vals[hh], exps[hh]) * inv
        gh = g_t[hh * VDIM : hh * VDIM + VDIM]
        delta.append(jnp.sum(o_t * gh.astype(F32), axis=0, keepdims=True))
        out.append(o_t)
        inverse.append(inv)
        g_h.append(gh)
        q_s.append((q_t[hh * QK : hh * QK + QK].astype(F32) * (inv * SCALE)).astype(BF))
        g_s.append((gh.astype(F32) * inv).astype(BF))
    rope = None
    for hh in range(2):
        dp = mm(vals[hh], g_h[hh])
        dscores[hh] = (exps[hh].astype(F32) * (dp - delta[hh])).astype(BF)
        dk = mm_last(dscores[hh], q_s[hh])
        dv = mm_last(exps[hh], g_s[hh])
        dkv[:, hh * 256 : hh * 256 + NOPE] = dk[:, :NOPE].astype(BF)
        dkv[:, hh * 256 + NOPE : hh * 256 + 256] = dv.astype(BF)
        rope = dk[:, NOPE:] if rope is None else rope + dk[:, NOPE:]
    acc[:, :KV_RANK] += mm_last(dkv[...], w[...])
    acc[:, KV_RANK:] += rope
    dq_t = [mm_first(keys[hh], dscores[hh]) * (inverse[hh] * SCALE) for hh in range(2)]
    out = jnp.concatenate(out, axis=0).T.astype(BF)
    dq = jnp.concatenate(dq_t, axis=0).T.astype(BF)
    return out, dq, mm(lat_t[...], dkv[...]).astype(BF)


def body(ints, *refs):
    pieces, (q, g, far_q, far_g, w, out, dq, far_out, wg_0, wg_1, wg_2, wg_3, keep, send) = (
        refs[:8],
        refs[8:22],
    )
    scratch = refs[22:]
    lat, lat_t, bias, acc, keys = scratch[:5]
    step = pl.program_id(0)

    @pl.when(step == 0)
    def _():
        prepare(ints, pieces, lat, lat_t, bias, keys)
        acc[...] = jnp.zeros_like(acc)

    q_t = jnp.concatenate([q[...].T, far_q[...].T], axis=1)
    g_t = jnp.concatenate([g[...].T, far_g[...].T], axis=1)
    out_pair, dq_pair, wg = head_pair(q_t, g_t, w, *scratch)
    out[...] = out_pair[:256]
    dq[...] = dq_pair[:256]
    for k, ref in enumerate((wg_0, wg_1, wg_2, wg_3)):
        ref[...] = wg[k * 128 : k * 128 + 128]
    for i in range(2):

        @pl.when(step == i)
        def _():
            far_out[:, i * 2 * QK : (i + 1) * 2 * QK] = dq_pair[256:]
            far_out[:, 4 * QK + i * 2 * VDIM : 4 * QK + (i + 1) * 2 * VDIM] = out_pair[256:]

    @pl.when(step == pl.num_programs(0) - 1)
    def _():
        core = ints[AT_CORE]
        for dx in range(4):
            for z in range(4):
                x_first = dx * 4 + z
                z_first = (z - ints[AT_Z] + 4) % 4 * 4 + (dx + ints[AT_X]) % 4
                rows = pl.ds(x_first * 64, 64)
                keep[jnp.where(core == 0, x_first, z_first)] = acc[rows, :].astype(BF)
                rows = pl.ds(1024 + x_first * 64, 64)
                send[jnp.where(core == 0, z_first, x_first)] = acc[rows, :].astype(BF)


def attention(ints, pieces, queries, out_grad, far, up_weight):
    def whole(*dims):
        return pl.BlockSpec(dims, lambda i, n: (0,) * len(dims))

    def once(*dims):
        return pl.BlockSpec(dims, lambda i, n: (0,) * len(dims), pipeline_mode=pl.Buffered(1))

    def mine(rows, width):
        return pl.BlockSpec((rows, width), lambda i, n: (0, i + 2 * n[AT_YLO]))

    def columns(rows, width, first=0):
        return pl.BlockSpec((rows, width), lambda i, n: (0, i + first))

    def shape(*dims):
        return jax.ShapeDtypeStruct(dims, BF)

    return pl.pallas_call(
        body,
        grid_spec=pltpu.PrefetchScalarGridSpec(
            num_scalar_prefetch=1,
            grid=(2,),
            in_specs=[once(256, LAT)] * 8
            + [
                mine(256, 2 * QK),
                mine(256, 2 * VDIM),
                columns(256, 2 * QK),
                columns(256, 2 * VDIM, 3),
                mine(KV_RANK, 512),
            ],
            out_specs=[
                columns(256, 2 * VDIM),
                columns(256, 2 * QK),
                whole(256, 4 * (QK + VDIM)),
                columns(128, 512),
                columns(128, 512),
                columns(128, 512),
                columns(128, 512),
                whole(16, 64, LAT),
                whole(16, 64, LAT),
            ],
            scratch_shapes=[
                pltpu.VMEM((KEYS, KV_RANK), BF),
                pltpu.VMEM((KV_RANK, KEYS), BF),
                pltpu.VMEM((KEYS, ROWS), F32),
                pltpu.VMEM((KEYS, LAT), F32),
                pltpu.VMEM((2, KEYS, QK), BF),
                pltpu.VMEM((2, KEYS, VDIM), BF),
                pltpu.VMEM((2, KEYS, ROWS), F32),
                pltpu.VMEM((2, KEYS, ROWS), BF),
                pltpu.VMEM((2, KEYS, ROWS), BF),
                pltpu.VMEM((KEYS, 512), BF),
            ],
        ),
        out_shape=[
            shape(256, 4 * VDIM),
            shape(256, 4 * QK),
            shape(256, 4 * (QK + VDIM)),
            shape(128, 1024),
            shape(128, 1024),
            shape(128, 1024),
            shape(128, 1024),
            shape(16, 64, LAT),
            shape(16, 64, LAT),
        ],
        compiler_params=pltpu.CompilerParams(vmem_limit_bytes=60 * 2**20),
        cost_estimate=pl.CostEstimate(
            flops=20 * 10**9, bytes_accessed=16 * 2**20, transcendentals=2**22
        ),
    )(ints, *pieces, queries, out_grad, far, far, up_weight)


AXES = ("ctx", "head")


def device_index(x, y, z, core):
    return ((y % 2) * 4 + x) * 16 + z * 4 + (y // 2) * 2 + core


def send_shift(value, first, second):
    pairs = []
    for x in range(4):
        for y in range(4):
            for z in range(4):
                for core, (dx, dy, dz) in enumerate((first, second)):
                    target = device_index((x + dx) % 4, (y + dy) % 4, (z + dz) % 4, core)
                    pairs.append((device_index(x, y, z, core), target))
    return lax.ppermute(value, AXES, pairs)


def swap_cores(value):
    return lax.ppermute(value, "head", [(i, i ^ 1) for i in range(16)])


def swap_ylo(value):
    return lax.ppermute(value, "ctx", [(i, i ^ 4) for i in range(8)])


def exchange_rest(value):
    groups = [
        [device_index(x, yh * 2 + yl, z, 0) for z in range(4) for yh in range(2) for yl in range(2)]
        for x in range(4)
    ] + [
        [device_index(x, yh * 2 + yl, z, 1) for x in range(4) for yh in range(2) for yl in range(2)]
        for z in range(4)
    ]
    return lax.all_to_all(value, AXES, 0, 0, tiled=True, axis_index_groups=groups)


def gather_latent(latent, y_lo, core):
    own = lax.dynamic_index_in_dim(latent.reshape(4, 2, 2, 16, LAT), core, 2, False)
    other = swap_ylo(own)
    low, high = jnp.where(y_lo == 0, own, other), jnp.where(y_lo == 0, other, own)
    pair = jnp.stack([low, high], axis=2)
    mine = [pair] + [send_shift(pair, (-k, 0, 0), (-k, 0, 0)) for k in (1, 2, 3)]
    other = [swap_cores(piece) for piece in mine]
    return [piece.reshape(256, LAT) for piece in mine + other]


def kernel_ints(x, y_lo, z, core, group_order):
    block = jnp.arange(128, dtype=jnp.int32)
    which = core ^ (block // 64)
    far_x = (x + (block // 16) % 4) % 4
    row = ((block % 2 * 4 + far_x) * 16 + (block // 4) % 4 * 4 + block // 2 % 2 * 2 + which) * 16
    query = jnp.arange(4, dtype=jnp.int32)
    query = ((y_lo ^ (query // 2)) * 4 + x) * 2 + query % 2
    groups = jnp.concatenate([row // 128, query])
    onehot = groups[:, None] == jnp.arange(16, dtype=jnp.int32)[None, :]
    starts = jnp.sum(jnp.where(onehot, group_order[None, :], 0), axis=1) * 128
    starts = starts + jnp.concatenate([row % 128, jnp.zeros((4,), jnp.int32)])
    return jnp.concatenate([starts, jnp.stack([x, y_lo, z, core])])


def sum_terms(first, others):
    total = first.astype(F32)
    for other in others:
        total = total + other.astype(F32)
    return total


def halves(y_lo, near, far, axis=1):
    low, high = jnp.where(y_lo == 0, near, far), jnp.where(y_lo == 0, far, near)
    return jnp.concatenate([low, high], axis=axis)


def other_half(y_lo, value):
    width = value.shape[1] // 2
    return jnp.where(y_lo == 0, value[:, width:], value[:, :width])


def reduce_terms(y_lo, keep, send, wg, far_out):
    swapped = swap_cores(send)
    far_out = swap_ylo(far_out)
    part = sum_terms(keep, [swapped])
    wire = part.astype(BF)
    terms = [send_shift(wire[4 * k : 4 * k + 4], (k, 0, 0), (0, 0, k)) for k in (2, 1, 3)]
    parts = lax.optimization_barrier((wire, wg[1], wg[2], wg[3]))
    wg_terms = [send_shift(parts[k], (k, 0, 0), (k, 0, 0)) for k in (2, 1, 3)]
    part = sum_terms(part[:4], terms).astype(BF)
    far_out, *wg_terms = lax.optimization_barrier((part, far_out, *wg_terms))[1:]
    wg_sum = sum_terms(wg[0], wg_terms)
    wg_far = swap_ylo(wg_sum[64:].astype(BF))
    moved = exchange_rest(part.reshape(16, 16, LAT))
    latent_grad = sum_terms(moved[0], [moved[i] for i in range(1, 16)])
    return latent_grad, halves(y_lo, wg_sum[:64], wg_far.astype(F32)), far_out


def local(
    latent, queries, up_weight, out_grad, logratio, student_logprob, teacher_logprob, group_order
):
    ctx, head = lax.axis_index("ctx"), lax.axis_index("head")
    x, y_lo, z, core = ctx % 4, ctx // 4, head // 4, head % 2
    pieces = gather_latent(latent, y_lo, core)
    tok_weight = jnp.clip(jnp.exp(logratio), 0.8, 1.25) * (teacher_logprob - student_logprob)
    dout = (tok_weight[:, None] * out_grad.astype(F32)).astype(BF)
    far = swap_ylo(jnp.concatenate([other_half(y_lo, queries), other_half(y_lo, dout)], axis=1))
    ints = kernel_ints(x, y_lo, z, core, group_order)
    out, dq, far_out, wg_0, wg_1, wg_2, wg_3, keep, send = attention(
        ints, pieces, queries, dout, far, up_weight
    )
    latent_grad, weight_grad, far_out = reduce_terms(
        y_lo, keep, send, (wg_0, wg_1, wg_2, wg_3), far_out
    )
    query_grad = halves(y_lo, dq, far_out[:, : 4 * QK])
    attn_output = halves(y_lo, out, far_out[:, 4 * QK :])
    return (attn_output, query_grad, latent_grad, weight_grad)


def solution(mesh):
    placed = (
        P("ctx", None),
        P("ctx", "head"),
        P(None, "head"),
        P("ctx", "head"),
        P("ctx"),
        P("ctx"),
        P("ctx"),
        P(),
    )
    return jax.shard_map(
        local,
        mesh=mesh,
        in_specs=placed,
        out_specs=(P("ctx", "head"), P("ctx", "head"), P(AXES, None), P("ctx", "head")),
        check_vma=False,
    )
```

time: 129 us -> 105 us (0.81)
  waiting for transfers between devices: 48.7 us -> 35.4 us
  Pallas kernels: 36.9 us -> 30.3 us
  starting transfers between devices: 33.1 us -> 29.5 us
  other arithmetic: 4.06 us -> 6.75 us
  local copies, waits for them, and re-layouts: 4.69 us -> 2.12 us
    ppermute x3 -> x4, waiting for transfers between devices: 16.7 us -> 7.32 us  [swap_ylo(): return lax.ppermute(value, 'ctx', [(i, i ^ 4) for i in range(8)])]
    all_to_all x1, waiting for transfers between devices: 8.18 us -> 1.35 us  [exchange_rest(): lax.all_to_all(value, AXES, 0, 0, tiled=True, axis_index_groups=groups)]
    pallas_call x1, Pallas kernels: 36.9 us -> 30.3 us  [attention(): pl.pallas_call(body, grid_spec=pltpu.PrefetchScalarGridSpec(num_scalar_pr...]
    ppermute x12 -> x9, starting transfers between devices: 18.9 us -> 14.9 us  [send_shift(): return lax.ppermute(value, AXES, pairs)]
    ppermute x5, waiting for transfers between devices: 0.29 us -> 2.45 us  [swap_cores(): return lax.ppermute(value, 'head', [(i, i ^ 1) for i in range(16)])]
    concatenate x2 -> x5, other arithmetic: 0.84 us -> 2.68 us  [the longest x3 2.63 us: halves(): return jnp.concatenate([low, high], axis=axis)]
    unnamed x31 -> x39, local copies, waits for them, and re-layouts: 2.76 us -> 1.34 us
    convert_element_type x1, other arithmetic: 0.41 us -> 1.75 us  [reduce_terms(): wire = part.astype(BF)]
  transfers between devices with their start and end apart: 21 -> 19, of which waited for: 11 -> 13; matrix products, arithmetic and copies ran while one was open for 4% -> 7% of each run, Pallas kernels for 0% -> 0%
where the time goes in v4:
time: 105 us
  waiting for transfers between devices  35.4 us (34%)
  Pallas kernels  30.3 us (29%)
  starting transfers between devices  29.5 us (28%)
  other arithmetic  6.75 us (6%)
  local copies, waits for them, and re-layouts  2.12 us (2%)
    pallas_call x1, Pallas kernels, attention(): pl.pallas_call(body, grid_spec=pltpu.PrefetchScalarGridSpec(num_scalar_pr...  30.3 us
    ppermute x9, waiting for transfers between devices, send_shift(): return lax.ppermute(value, AXES, pairs)  24.3 us
    ppermute x9, starting transfers between devices, send_shift(): return lax.ppermute(value, AXES, pairs)  14.9 us
    all_to_all x1, starting transfers between devices, exchange_rest(): lax.all_to_all(value, AXES, 0, 0, tiled=True, axis_index_groups=groups)  8.05 us
    ppermute x4, waiting for transfers between devices, swap_ylo(): return lax.ppermute(value, 'ctx', [(i, i ^ 4) for i in range(8)])  7.32 us
    ppermute x4, starting transfers between devices, swap_ylo(): return lax.ppermute(value, 'ctx', [(i, i ^ 4) for i in range(8)])  5.78 us
    concatenate x3, other arithmetic, halves(): return jnp.concatenate([low, high], axis=axis)  2.63 us
    ppermute x5, waiting for transfers between devices, swap_cores(): return lax.ppermute(value, 'head', [(i, i ^ 1) for i in range(16)])  2.45 us
  transfers between devices with their start and end apart: 19, of which 13 were waited for; matrix products, arithmetic and copies ran while one was open for 7% of the time, Pallas kernels for 0%

profile of v4, /device:TPU:0, one launch (start us, length us, event | category | flops | bytes accessed | tf_op | source)
XLA Modules:
  0.0 105.1 jit_solution(12924366666526673341)
XLA Ops:
  0.6 0.0 copy-start.1
  0.6 0.0 copy-start.7
  0.7 0.0 copy-start.8
  0.7 0.0 copy-start.9
  0.7 0.0 copy-start.2
  0.7 1.3 %copy.16 = bf16[256,576]{1,0:T(8,128)(2,1)S(1)} copy(bf16[256,576]{0,1:T(8,128)(2,1)} %param.8) | data formatting | bytes 589824 | tf_op args[0]
  2.0 1.7 %collective-permute-start = (bf16[4,2,16,576]{3,2,1,0:T(8,128)(2,1)S(1)}, bf16[4,2,16,576]{3,2,1,0:T(8,128)(2,1)S(1)}, u32[]{:S(2)}, u32[]{:S(2)}) collective-permute-start(bf16[4,2,16,576]{3,2,1,0:T(8,128)(2,1)S(1)} %dynamic-slice_bitcast_fusion), channel_id=1, source_target_pairs={{0,64},{16,80},{32,96},{48,112},{64,0},{80,16},{96,32},{112,48},{1... | collective-permute-start | bytes 442376 | tf_op jit(solution)/shard_map/ppermute | solution.py:228
  3.8 0.2 multiply_convert_fusion.refs_9_
  4.0 0.0 copy-start
  4.0 0.0 copy-start.10
  4.1 0.4 collective-permute-start.8
  4.5 4.6 %collective-permute-done = bf16[4,2,16,576]{3,2,1,0:T(8,128)(2,1)S(1)} collective-permute-done((bf16[4,2,16,576]{3,2,1,0:T(8,128)(2,1)S(1)}, bf16[4,2,16,576]{3,2,1,0:T(8,128)(2,1)S(1)}, u32[]{:S(2)}, u32[]{:S(2)}) %collective-permute-start) | collective-permute-done | bytes 147488 | tf_op jit(solution)/shard_map/ppermute | solution.py:228
  9.2 0.1 pad_maximum_fusion.4
  9.3 0.0 copy-start.4
  9.3 1.6 %collective-permute-start.3 = (bf16[4,2,2,16,576]{4,3,2,1,0:T(8,128)(2,1)S(1)}, bf16[4,2,2,16,576]{4,3,2,1,0:T(8,128)(2,1)S(1)}, u32[]{:S(2)}, u32[]{:S(2)}) collective-permute-start(bf16[4,2,2,16,576]{4,3,2,1,0:T(8,128)(2,1)S(1)} %pad_maximum_fusion.4), channel_id=1, source_target_pairs={{0,16},{1,17},{4,20},{5,21},{8,24},{9,25},{12,28},{13,29},{64,80},... | collective-permute-start | bytes 884744 | tf_op jit(solution)/shard_map/ppermute | solution.py:220
  10.9 2.7 %collective-permute-start.2 = (bf16[4,2,2,16,576]{4,3,2,1,0:T(8,128)(2,1)S(1)}, bf16[4,2,2,16,576]{4,3,2,1,0:T(8,128)(2,1)S(1)}, u32[]{:S(2)}, u32[]{:S(2)}) collective-permute-start(bf16[4,2,2,16,576]{4,3,2,1,0:T(8,128)(2,1)S(1)} %pad_maximum_fusion.4), channel_id=1, source_target_pairs={{0,32},{1,33},{4,36},{5,37},{8,40},{9,41},{12,44},{13,45},{64,96},... | collective-permute-start | bytes 884744 | tf_op jit(solution)/shard_map/ppermute | solution.py:220
  13.6 1.4 %collective-permute-start.1 = (bf16[4,2,2,16,576]{4,3,2,1,0:T(8,128)(2,1)S(1)}, bf16[4,2,2,16,576]{4,3,2,1,0:T(8,128)(2,1)S(1)}, u32[]{:S(2)}, u32[]{:S(2)}) collective-permute-start(bf16[4,2,2,16,576]{4,3,2,1,0:T(8,128)(2,1)S(1)} %pad_maximum_fusion.4), channel_id=1, source_target_pairs={{0,48},{1,49},{4,52},{5,53},{8,56},{9,57},{12,60},{13,61},{64,112}... | collective-permute-start | bytes 884744 | tf_op jit(solution)/shard_map/ppermute | solution.py:220
  15.1 0.1 collective-permute-start.4
  15.2 4.7 %collective-permute-done.3 = bf16[4,2,2,16,576]{4,3,2,1,0:T(8,128)(2,1)S(1)} collective-permute-done((bf16[4,2,2,16,576]{4,3,2,1,0:T(8,128)(2,1)S(1)}, bf16[4,2,2,16,576]{4,3,2,1,0:T(8,128)(2,1)S(1)}, u32[]{:S(2)}, u32[]{:S(2)}) %collective-permute-start.3) | collective-permute-done | bytes 294944 | tf_op jit(solution)/shard_map/ppermute | solution.py:220
  19.9 0.0 collective-permute-start.7
  19.9 6.2 %collective-permute-done.2 = bf16[4,2,2,16,576]{4,3,2,1,0:T(8,128)(2,1)S(1)} collective-permute-done((bf16[4,2,2,16,576]{4,3,2,1,0:T(8,128)(2,1)S(1)}, bf16[4,2,2,16,576]{4,3,2,1,0:T(8,128)(2,1)S(1)}, u32[]{:S(2)}, u32[]{:S(2)}) %collective-permute-start.2) | collective-permute-done | bytes 294944 | tf_op jit(solution)/shard_map/ppermute | solution.py:220
  26.1 0.0 collective-permute-start.6
  26.1 0.0 collective-permute-done.1
  26.1 0.5 collective-permute-start.5
  26.6 0.1 select_reduce_fusion
  26.7 0.7 concatenate.23.ints
  27.4 0.0 collective-permute-done.4
  27.4 0.0 collective-permute-done.8.refs_10_.refs_11_
  27.4 0.0 copy-start.11
  27.4 0.0 collective-permute-done.7
  27.4 0.5 collective-permute-done.6
  27.8 0.5 collective-permute-done.5
  28.3 0.0 copy-done.4
  28.4 30.3 %shard_map.111 = (bf16[256,512]{1,0:T(8,128)(2,1)}, bf16[256,768]{1,0:T(8,128)(2,1)}, bf16[256,1280]{1,0:T(8,128)(2,1)}, bf16[128,1024]{1,0:T(8,128)(2,1)}, bf16...) custom-call(s32[136]{0:T(256)} %concatenate.23.ints, ...), custom_call_target="tpu_custom_call" | custom-call | flops 20000000000 | bytes 16777216 | tf_op jit(solution)/shard_map/pallas_call | solution.py:150
  58.7 0.2 collective-permute-start.9
  58.9 1.6 %collective-permute-start.13 = (bf16[256,1280]{1,0:T(8,128)(2,1)}, bf16[256,1280]{1,0:T(8,128)(2,1)S(1)}, u32[]{:S(2)}, u32[]{:S(2)}) collective-permute-start(bf16[256,1280]{1,0:T(8,128)(2,1)} %get-tuple-element.23), channel_id=1, source_target_pairs={{0,64},{16,80},{32,96},{48,112},{64,0},{80,16},{96,32},{112,48},{1... | collective-permute-start | bytes 1966088 | tf_op jit(solution)/shard_map/ppermute | solution.py:228
  60.5 1.5 %collective-permute-done.9 = bf16[16,64,576]{2,1,0:T(8,128)(2,1)S(1)} collective-permute-done((bf16[16,64,576]{2,1,0:T(8,128)(2,1)}, bf16[16,64,576]{2,1,0:T(8,128)(2,1)S(1)}, u32[]{:S(2)}, u32[]{:S(2)}) %collective-permute-start.9) | collective-permute-done | bytes 1179680 | tf_op jit(solution)/shard_map/ppermute | solution.py:224
  62.0 1.7 %fusion.24 = (bf16[16,64,576]{2,1,0:T(8,128)(2,1)S(1)}, f32[16,64,576]{2,1,0:T(8,128)S(1)}) fusion(bf16[16,64,576]{2,1,0:T(8,128)(2,1)S(1)} %collective-permute-done.9, bf16[16,64,576]{2,1,0:T(8,128)(2,1)} %get-tuple-element.21), kind=kLoop, calls=%fused_computation.86 | loop fusion | flops 2359296 | bytes 5898240 | tf_op jit(solution)/shard_map/convert_element_type | solution.py:287
  63.8 0.1 fusion.25
  63.9 2.3 %collective-permute-start.10 = (bf16[4,64,576]{2,1,0:T(8,128)(2,1)S(1)}, bf16[4,64,576]{2,1,0:T(8,128)(2,1)S(1)}, u32[]{:S(2)}, u32[]{:S(2)}) collective-permute-start(bf16[4,64,576]{2,1,0:T(8,128)(2,1)S(1)} %get-tuple-element.38), channel_id=1, source_target_pairs={{0,32},{1,9},{4,36},{5,13},{8,40},{9,1},{12,44},{13,5},{64,96},{65... | collective-permute-start | bytes 884744 | tf_op jit(solution)/shard_map/ppermute | solution.py:220
  66.2 1.3 %collective-permute-start.12 = (bf16[4,64,576]{2,1,0:T(8,128)(2,1)S(1)}, bf16[4,64,576]{2,1,0:T(8,128)(2,1)S(1)}, u32[]{:S(2)}, u32[]{:S(2)}) collective-permute-start(bf16[4,64,576]{2,1,0:T(8,128)(2,1)S(1)} %get-tuple-element.39), channel_id=1, source_target_pairs={{0,48},{1,13},{4,52},{5,1},{8,56},{9,5},{12,60},{13,9},{64,112},{6... | collective-permute-start | bytes 884744 | tf_op jit(solution)/shard_map/ppermute | solution.py:220
  67.4 0.8 collective-permute-start.11
  68.2 1.3 %collective-permute-start.14 = (bf16[128,1024]{1,0:T(8,128)(2,1)S(1)}, bf16[128,1024]{1,0:T(8,128)(2,1)S(1)}, u32[]{:S(2)}, u32[]{:S(2)}) collective-permute-start(bf16[128,1024]{1,0:T(8,128)(2,1)S(1)} %copy-done.18), channel_id=1, source_target_pairs={{0,32},{1,33},{4,36},{5,37},{8,40},{9,41},{12,44},{13,45},{64,96},... | collective-permute-start | bytes 786440 | tf_op jit(solution)/shard_map/ppermute | solution.py:220
  69.5 3.1 %collective-permute-done.10 = bf16[4,64,576]{2,1,0:T(8,128)(2,1)S(1)} collective-permute-done((bf16[4,64,576]{2,1,0:T(8,128)(2,1)S(1)}, bf16[4,64,576]{2,1,0:T(8,128)(2,1)S(1)}, u32[]{:S(2)}, u32[]{:S(2)}) %collective-permute-start.10) | collective-permute-done | bytes 294944 | tf_op jit(solution)/shard_map/ppermute | solution.py:220
  72.6 0.9 collective-permute-start.15
  73.4 4.1 %collective-permute-done.12 = bf16[4,64,576]{2,1,0:T(8,128)(2,1)S(1)} collective-permute-done((bf16[4,64,576]{2,1,0:T(8,128)(2,1)S(1)}, bf16[4,64,576]{2,1,0:T(8,128)(2,1)S(1)}, u32[]{:S(2)}, u32[]{:S(2)}) %collective-permute-start.12) | collective-permute-done | bytes 294944 | tf_op jit(solution)/shard_map/ppermute | solution.py:220
  77.6 2.6 %collective-permute-start.16 = (bf16[128,1024]{1,0:T(8,128)(2,1)S(1)}, bf16[128,1024]{1,0:T(8,128)(2,1)S(1)}, u32[]{:S(2)}, u32[]{:S(2)}) collective-permute-start(bf16[128,1024]{1,0:T(8,128)(2,1)S(1)} %copy-done.16), channel_id=1, source_target_pairs={{0,48},{1,49},{4,52},{5,53},{8,56},{9,57},{12,60},{13,61},{64,112}... | collective-permute-start | bytes 786440 | tf_op jit(solution)/shard_map/ppermute | solution.py:220
  80.1 1.2 %collective-permute-done.11 = bf16[4,64,576]{2,1,0:T(8,128)(2,1)S(1)} collective-permute-done((bf16[4,64,576]{2,1,0:T(8,128)(2,1)S(1)}, bf16[4,64,576]{2,1,0:T(8,128)(2,1)S(1)}, u32[]{:S(2)}, u32[]{:S(2)}) %collective-permute-start.11) | collective-permute-done | bytes 294944 | tf_op jit(solution)/shard_map/ppermute | solution.py:220
  81.3 0.9 fusion.2
  82.2 0.0 collective-permute-done.13
  82.2 2.1 %collective-permute-done.14 = bf16[128,1024]{1,0:T(8,128)(2,1)S(1)} collective-permute-done((bf16[128,1024]{1,0:T(8,128)(2,1)S(1)}, bf16[128,1024]{1,0:T(8,128)(2,1)S(1)}, u32[]{:S(2)}, u32[]{:S(2)}) %collective-permute-start.14) | collective-permute-done | bytes 262176 | tf_op jit(solution)/shard_map/ppermute | solution.py:220
  84.4 2.9 %collective-permute-done.15 = bf16[128,1024]{1,0:T(8,128)(2,1)S(1)} collective-permute-done((bf16[128,1024]{1,0:T(8,128)(2,1)S(1)}, bf16[128,1024]{1,0:T(8,128)(2,1)S(1)}, u32[]{:S(2)}, u32[]{:S(2)}) %collective-permute-start.15) | collective-permute-done | bytes 262176 | tf_op jit(solution)/shard_map/ppermute | solution.py:220
  87.3 0.0 collective-permute-done.16
  87.3 8.1 %all-to-all-start = ((bf16[16,16,576]{2,1,0:T(8,128)(2,1)}), bf16[16,16,576]{2,1,0:T(8,128)(2,1)S(1)}, u32[]{:S(2)}, u32[]{:S(2)}) async-start(bf16[16,16,576]{2,1,0:T(8,128)(2,1)} %bitcast.17), calls=%async_computation | async-start | bytes 655360 | tf_op jit(solution)/shard_map/all_to_all | solution.py:239
  95.4 0.0 copy-start.3
  95.4 0.2 convert_add_fusion.1
  95.6 2.0 %collective-permute-start.17 = (bf16[64,1024]{1,0:T(8,128)(2,1)S(1)}, bf16[64,1024]{1,0:T(8,128)(2,1)S(1)}, u32[]{:S(2)}, u32[]{:S(2)}) collective-permute-start(bf16[64,1024]{1,0:T(8,128)(2,1)S(1)} %slice.173), channel_id=1, source_target_pairs={{0,64},{16,80},{32,96},{48,112},{64,0},{80,16},{96,32},{112,48},{1... | collective-permute-start | bytes 393224 | tf_op jit(solution)/shard_map/ppermute | solution.py:228
  97.6 0.1 broadcast_select_fusion.1
  97.7 0.9 pad_maximum_fusion
  98.6 0.9 pad_maximum_fusion.2
  99.5 2.7 %collective-permute-done.17 = bf16[64,1024]{1,0:T(8,128)(2,1)S(1)} collective-permute-done((bf16[64,1024]{1,0:T(8,128)(2,1)S(1)}, bf16[64,1024]{1,0:T(8,128)(2,1)S(1)}, u32[]{:S(2)}, u32[]{:S(2)}) %collective-permute-start.17) | collective-permute-done | bytes 131104 | tf_op jit(solution)/shard_map/ppermute | solution.py:228
  102.2 0.8 pad_maximum_fusion.3
  103.1 1.4 %all-to-all-done = bf16[16,16,576]{2,1,0:T(8,128)(2,1)S(1)} async-done(((bf16[16,16,576]{2,1,0:T(8,128)(2,1)}), bf16[16,16,576]{2,1,0:T(8,128)(2,1)S(1)}, u32[]{:S(2)}, u32[]{:S(2)}) %all-to-all-start) | async-done | bytes 294944 | tf_op jit(solution)/shard_map/all_to_all | solution.py:239
  104.4 0.7 convert_add_fusion.2
  (40 shorter events, 0.4 us)
Async XLA Ops:
  0.6 3.1 %copy-start.1 = (bf16[256,1536]{1,0:T(8,128)(2,1)S(1)}, bf16[256,1536]{1,0:T(8,128)(2,1)}, u32[]{:S(2)}) copy-start(bf16[256,1536]{1,0:T(8,128)(2,1)} %refs_8_.1) | copy-start | bytes 2359300
  0.6 3.1 %copy-start.7 = (f32[256]{0:T(256)S(1)}, f32[256]{0:T(256)}, u32[]{:S(2)}) copy-start(f32[256]{0:T(256)} %param.14) | copy-start | bytes 3076
  0.7 3.1 %copy-start.8 = (f32[256]{0:T(256)S(1)}, f32[256]{0:T(256)}, u32[]{:S(2)}) copy-start(f32[256]{0:T(256)} %param.13) | copy-start | bytes 3076
  0.7 3.1 %copy-start.9 = (f32[256]{0:T(256)S(1)}, f32[256]{0:T(256)}, u32[]{:S(2)}) copy-start(f32[256]{0:T(256)} %param.12) | copy-start | bytes 3076
  0.7 3.1 %copy-start.2 = (bf16[256,1024]{1,0:T(8,128)(2,1)S(1)}, bf16[256,1024]{1,0:T(8,128)(2,1)}, u32[]{:S(2)}) copy-start(bf16[256,1024]{1,0:T(8,128)(2,1)} %param.11) | copy-start | bytes 1572868
  2.0 7.2 %collective-permute-start = (bf16[4,2,16,576]{3,2,1,0:T(8,128)(2,1)S(1)}, bf16[4,2,16,576]{3,2,1,0:T(8,128)(2,1)S(1)}, u32[]{:S(2)}, u32[]{:S(2)}) collective-permute-start(bf16[4,2,16,576]{3,2,1,0:T(8,128)(2,1)S(1)} %dynamic-slice_bitcast_fusion), channel_id=1, source_target_pairs={{0,64},{16,80},{32,96},{48,112},{64,0},{80,16},{96,32},{112,48},{1... | collective-permute-start | bytes 442376 | tf_op jit(solution)/shard_map/ppermute | solution.py:228
  4.0 5.2 %copy-start = (bf16[256,1024]{1,0:T(8,128)(2,1)}, bf16[256,1024]{1,0:T(8,128)(2,1)S(1)}, u32[]{:S(2)}) copy-start(bf16[256,1024]{1,0:T(8,128)(2,1)S(1)} %multiply_convert_fusion.refs_9_) | copy-start | bytes 1572868
  4.0 22.6 %copy-start.10 = (s32[16]{0:T(128)S(1)}, s32[16]{0:T(128)}, u32[]{:S(2)}) copy-start(s32[16]{0:T(128)} %param.15) | copy-start | bytes 196
  4.1 23.3 %collective-permute-start.8 = (bf16[256,1280]{1,0:T(8,128)(2,1)S(1)}, bf16[256,1280]{1,0:T(8,128)(2,1)S(1)}, u32[]{:S(2)}, u32[]{:S(2)}) collective-permute-start(bf16[256,1280]{1,0:T(8,128)(2,1)S(1)} %pad_maximum_fusion.1), channel_id=1, source_target_pairs={{0,64},{16,80},{32,96},{48,112},{64,0},{80,16},{96,32},{112,48},{1... | collective-permute-start | bytes 1966088 | tf_op jit(solution)/shard_map/ppermute | solution.py:228
  9.3 19.0 %copy-start.4 = (bf16[4,2,2,16,576]{4,3,2,1,0:T(8,128)(2,1)}, bf16[4,2,2,16,576]{4,3,2,1,0:T(8,128)(2,1)S(1)}, u32[]{:S(2)}) copy-start(bf16[4,2,2,16,576]{4,3,2,1,0:T(8,128)(2,1)S(1)} %pad_maximum_fusion.4) | copy-start | bytes 884740
  9.3 10.6 %collective-permute-start.3 = (bf16[4,2,2,16,576]{4,3,2,1,0:T(8,128)(2,1)S(1)}, bf16[4,2,2,16,576]{4,3,2,1,0:T(8,128)(2,1)S(1)}, u32[]{:S(2)}, u32[]{:S(2)}) collective-permute-start(bf16[4,2,2,16,576]{4,3,2,1,0:T(8,128)(2,1)S(1)} %pad_maximum_fusion.4), channel_id=1, source_target_pairs={{0,16},{1,17},{4,20},{5,21},{8,24},{9,25},{12,28},{13,29},{64,80},... | collective-permute-start | bytes 884744 | tf_op jit(solution)/shard_map/ppermute | solution.py:220
  10.9 15.2 %collective-permute-start.2 = (bf16[4,2,2,16,576]{4,3,2,1,0:T(8,128)(2,1)S(1)}, bf16[4,2,2,16,576]{4,3,2,1,0:T(8,128)(2,1)S(1)}, u32[]{:S(2)}, u32[]{:S(2)}) collective-permute-start(bf16[4,2,2,16,576]{4,3,2,1,0:T(8,128)(2,1)S(1)} %pad_maximum_fusion.4), channel_id=1, source_target_pairs={{0,32},{1,33},{4,36},{5,37},{8,40},{9,41},{12,44},{13,45},{64,96},... | collective-permute-start | bytes 884744 | tf_op jit(solution)/shard_map/ppermute | solution.py:220
  13.6 12.4 %collective-permute-start.1 = (bf16[4,2,2,16,576]{4,3,2,1,0:T(8,128)(2,1)S(1)}, bf16[4,2,2,16,576]{4,3,2,1,0:T(8,128)(2,1)S(1)}, u32[]{:S(2)}, u32[]{:S(2)}) collective-permute-start(bf16[4,2,2,16,576]{4,3,2,1,0:T(8,128)(2,1)S(1)} %pad_maximum_fusion.4), channel_id=1, source_target_pairs={{0,48},{1,49},{4,52},{5,53},{8,56},{9,57},{12,60},{13,61},{64,112}... | collective-permute-start | bytes 884744 | tf_op jit(solution)/shard_map/ppermute | solution.py:220
  15.1 12.2 %collective-permute-start.4 = (bf16[4,2,2,16,576]{4,3,2,1,0:T(8,128)(2,1)S(1)}, bf16[4,2,2,16,576]{4,3,2,1,0:T(8,128)(2,1)S(1)}, u32[]{:S(2)}, u32[]{:S(2)}) collective-permute-start(bf16[4,2,2,16,576]{4,3,2,1,0:T(8,128)(2,1)S(1)} %pad_maximum_fusion.4), channel_id=1, source_target_pairs={{0,1},{1,0},{2,3},{3,2},{4,5},{5,4},{6,7},{7,6},{8,9},{9,8},{10,11... | collective-permute-start | bytes 884744 | tf_op jit(solution)/shard_map/ppermute | solution.py:224
  19.9 8.4 %copy-start.12 = (bf16[4,2,2,16,576]{4,3,2,1,0:T(8,128)(2,1)}, bf16[4,2,2,16,576]{4,3,2,1,0:T(8,128)(2,1)S(1)}, u32[]{:S(2)}) copy-start(bf16[4,2,2,16,576]{4,3,2,1,0:T(8,128)(2,1)S(1)} %collective-permute-done.3) | copy-start | bytes 884740
  19.9 7.5 %collective-permute-start.7 = (bf16[4,2,2,16,576]{4,3,2,1,0:T(8,128)(2,1)S(1)}, bf16[4,2,2,16,576]{4,3,2,1,0:T(8,128)(2,1)}, u32[]{:S(2)}, u32[]{:S(2)}) collective-permute-start(bf16[4,2,2,16,576]{4,3,2,1,0:T(8,128)(2,1)S(1)} %collective-permute-done.3), channel_id=1, source_target_pairs={{0,1},{1,0},{2,3},{3,2},{4,5},{5,4},{6,7},{7,6},{8,9},{9,8},{10,11... | collective-permute-start | bytes 884744 | tf_op jit(solution)/shard_map/ppermute | solution.py:224
  26.1 2.2 %copy-start.13 = (bf16[4,2,2,16,576]{4,3,2,1,0:T(8,128)(2,1)}, bf16[4,2,2,16,576]{4,3,2,1,0:T(8,128)(2,1)S(1)}, u32[]{:S(2)}) copy-start(bf16[4,2,2,16,576]{4,3,2,1,0:T(8,128)(2,1)S(1)} %collective-permute-done.2) | copy-start | bytes 884740
  26.1 1.8 %collective-permute-start.6 = (bf16[4,2,2,16,576]{4,3,2,1,0:T(8,128)(2,1)S(1)}, bf16[4,2,2,16,576]{4,3,2,1,0:T(8,128)(2,1)}, u32[]{:S(2)}, u32[]{:S(2)}) collective-permute-start(bf16[4,2,2,16,576]{4,3,2,1,0:T(8,128)(2,1)S(1)} %collective-permute-done.2), channel_id=1, source_target_pairs={{0,1},{1,0},{2,3},{3,2},{4,5},{5,4},{6,7},{7,6},{8,9},{9,8},{10,11... | collective-permute-start | bytes 884744 | tf_op jit(solution)/shard_map/ppermute | solution.py:224
  26.1 2.2 %copy-start.14 = (bf16[4,2,2,16,576]{4,3,2,1,0:T(8,128)(2,1)}, bf16[4,2,2,16,576]{4,3,2,1,0:T(8,128)(2,1)S(1)}, u32[]{:S(2)}) copy-start(bf16[4,2,2,16,576]{4,3,2,1,0:T(8,128)(2,1)S(1)} %collective-permute-done.1) | copy-start | bytes 884740
  26.1 2.2 %collective-permute-start.5 = (bf16[4,2,2,16,576]{4,3,2,1,0:T(8,128)(2,1)S(1)}, bf16[4,2,2,16,576]{4,3,2,1,0:T(8,128)(2,1)}, u32[]{:S(2)}, u32[]{:S(2)}) collective-permute-start(bf16[4,2,2,16,576]{4,3,2,1,0:T(8,128)(2,1)S(1)} %collective-permute-done.1), channel_id=1, source_target_pairs={{0,1},{1,0},{2,3},{3,2},{4,5},{5,4},{6,7},{7,6},{8,9},{9,8},{10,11... | collective-permute-start | bytes 884744 | tf_op jit(solution)/shard_map/ppermute | solution.py:224
  27.4 1.0 copy-start.15
  27.4 1.0 copy-start.11
  58.7 3.3 %collective-permute-start.9 = (bf16[16,64,576]{2,1,0:T(8,128)(2,1)}, bf16[16,64,576]{2,1,0:T(8,128)(2,1)S(1)}, u32[]{:S(2)}, u32[]{:S(2)}) collective-permute-start(bf16[16,64,576]{2,1,0:T(8,128)(2,1)} %get-tuple-element.22), channel_id=1, source_target_pairs={{0,1},{1,0},{2,3},{3,2},{4,5},{5,4},{6,7},{7,6},{8,9},{9,8},{10,11... | collective-permute-start | bytes 3538952 | tf_op jit(solution)/shard_map/ppermute | solution.py:224
  58.9 23.3 %collective-permute-start.13 = (bf16[256,1280]{1,0:T(8,128)(2,1)}, bf16[256,1280]{1,0:T(8,128)(2,1)S(1)}, u32[]{:S(2)}, u32[]{:S(2)}) collective-permute-start(bf16[256,1280]{1,0:T(8,128)(2,1)} %get-tuple-element.23), channel_id=1, source_target_pairs={{0,64},{16,80},{32,96},{48,112},{64,0},{80,16},{96,32},{112,48},{1... | collective-permute-start | bytes 1966088 | tf_op jit(solution)/shard_map/ppermute | solution.py:228
  63.8 4.4 %copy-start.18 = (bf16[128,1024]{1,0:T(8,128)(2,1)S(1)}, bf16[128,1024]{1,0:T(8,128)(2,1)}, u32[]{:S(2)}) copy-start(bf16[128,1024]{1,0:T(8,128)(2,1)} %get-tuple-element.27) | copy-start | bytes 786436
  63.8 8.8 %copy-start.17 = (bf16[128,1024]{1,0:T(8,128)(2,1)S(1)}, bf16[128,1024]{1,0:T(8,128)(2,1)}, u32[]{:S(2)}) copy-start(bf16[128,1024]{1,0:T(8,128)(2,1)} %get-tuple-element.28) | copy-start | bytes 786436
  63.8 13.8 %copy-start.16 = (bf16[128,1024]{1,0:T(8,128)(2,1)S(1)}, bf16[128,1024]{1,0:T(8,128)(2,1)}, u32[]{:S(2)}) copy-start(bf16[128,1024]{1,0:T(8,128)(2,1)} %get-tuple-element.29) | copy-start | bytes 786436
  63.9 8.7 %collective-permute-start.10 = (bf16[4,64,576]{2,1,0:T(8,128)(2,1)S(1)}, bf16[4,64,576]{2,1,0:T(8,128)(2,1)S(1)}, u32[]{:S(2)}, u32[]{:S(2)}) collective-permute-start(bf16[4,64,576]{2,1,0:T(8,128)(2,1)S(1)} %get-tuple-element.38), channel_id=1, source_target_pairs={{0,32},{1,9},{4,36},{5,13},{8,40},{9,1},{12,44},{13,5},{64,96},{65... | collective-permute-start | bytes 884744 | tf_op jit(solution)/shard_map/ppermute | solution.py:220
  66.2 11.4 %collective-permute-start.12 = (bf16[4,64,576]{2,1,0:T(8,128)(2,1)S(1)}, bf16[4,64,576]{2,1,0:T(8,128)(2,1)S(1)}, u32[]{:S(2)}, u32[]{:S(2)}) collective-permute-start(bf16[4,64,576]{2,1,0:T(8,128)(2,1)S(1)} %get-tuple-element.39), channel_id=1, source_target_pairs={{0,48},{1,13},{4,52},{5,1},{8,56},{9,5},{12,60},{13,9},{64,112},{6... | collective-permute-start | bytes 884744 | tf_op jit(solution)/shard_map/ppermute | solution.py:220
  67.4 13.9 %collective-permute-start.11 = (bf16[4,64,576]{2,1,0:T(8,128)(2,1)S(1)}, bf16[4,64,576]{2,1,0:T(8,128)(2,1)S(1)}, u32[]{:S(2)}, u32[]{:S(2)}) collective-permute-start(bf16[4,64,576]{2,1,0:T(8,128)(2,1)S(1)} %get-tuple-element.40), channel_id=1, source_target_pairs={{0,16},{1,5},{4,20},{5,9},{8,24},{9,13},{12,28},{13,1},{64,80},{65... | collective-permute-start | bytes 884744 | tf_op jit(solution)/shard_map/ppermute | solution.py:220
  68.2 16.2 %collective-permute-start.14 = (bf16[128,1024]{1,0:T(8,128)(2,1)S(1)}, bf16[128,1024]{1,0:T(8,128)(2,1)S(1)}, u32[]{:S(2)}, u32[]{:S(2)}) collective-permute-start(bf16[128,1024]{1,0:T(8,128)(2,1)S(1)} %copy-done.18), channel_id=1, source_target_pairs={{0,32},{1,33},{4,36},{5,37},{8,40},{9,41},{12,44},{13,45},{64,96},... | collective-permute-start | bytes 786440 | tf_op jit(solution)/shard_map/ppermute | solution.py:220
  72.6 14.7 %collective-permute-start.15 = (bf16[128,1024]{1,0:T(8,128)(2,1)S(1)}, bf16[128,1024]{1,0:T(8,128)(2,1)S(1)}, u32[]{:S(2)}, u32[]{:S(2)}) collective-permute-start(bf16[128,1024]{1,0:T(8,128)(2,1)S(1)} %copy-done.17), channel_id=1, source_target_pairs={{0,16},{1,17},{4,20},{5,21},{8,24},{9,25},{12,28},{13,29},{64,80},... | collective-permute-start | bytes 786440 | tf_op jit(solution)/shard_map/ppermute | solution.py:220
  77.6 9.7 %collective-permute-start.16 = (bf16[128,1024]{1,0:T(8,128)(2,1)S(1)}, bf16[128,1024]{1,0:T(8,128)(2,1)S(1)}, u32[]{:S(2)}, u32[]{:S(2)}) collective-permute-start(bf16[128,1024]{1,0:T(8,128)(2,1)S(1)} %copy-done.16), channel_id=1, source_target_pairs={{0,48},{1,49},{4,52},{5,53},{8,56},{9,57},{12,60},{13,61},{64,112}... | collective-permute-start | bytes 786440 | tf_op jit(solution)/shard_map/ppermute | solution.py:220
  81.3 14.0 %copy-start.6 = (bf16[128,1024]{1,0:T(8,128)(2,1)S(1)}, bf16[128,1024]{1,0:T(8,128)(2,1)}, u32[]{:S(2)}) copy-start(bf16[128,1024]{1,0:T(8,128)(2,1)} %get-tuple-element.32) | copy-start | bytes 786436
  82.2 15.3 %copy-start.5 = (bf16[256,512]{1,0:T(8,128)(2,1)S(1)}, bf16[256,512]{1,0:T(8,128)(2,1)}, u32[]{:S(2)}) copy-start(bf16[256,512]{1,0:T(8,128)(2,1)} %get-tuple-element.20) | copy-start | bytes 786436
  87.3 17.1 %all-to-all-start = ((bf16[16,16,576]{2,1,0:T(8,128)(2,1)}), bf16[16,16,576]{2,1,0:T(8,128)(2,1)S(1)}, u32[]{:S(2)}, u32[]{:S(2)}) async-start(bf16[16,16,576]{2,1,0:T(8,128)(2,1)} %bitcast.17), calls=%async_computation | async-start | bytes 655360 | tf_op jit(solution)/shard_map/all_to_all | solution.py:239
  95.4 2.2 %copy-start.3 = (bf16[256,768]{1,0:T(8,128)(2,1)S(1)}, bf16[256,768]{1,0:T(8,128)(2,1)}, u32[]{:S(2)}) copy-start(bf16[256,768]{1,0:T(8,128)(2,1)} %get-tuple-element.31) | copy-start | bytes 1179652
  95.6 6.6 %collective-permute-start.17 = (bf16[64,1024]{1,0:T(8,128)(2,1)S(1)}, bf16[64,1024]{1,0:T(8,128)(2,1)S(1)}, u32[]{:S(2)}, u32[]{:S(2)}) collective-permute-start(bf16[64,1024]{1,0:T(8,128)(2,1)S(1)} %slice.173), channel_id=1, source_target_pairs={{0,64},{16,80},{32,96},{48,112},{64,0},{80,16},{96,32},{112,48},{1... | collective-permute-start | bytes 393224 | tf_op jit(solution)/shard_map/ppermute | solution.py:228

commit v5 on v0

v5 whole, which is shorter than its diff:
```python
import math

import jax
import jax.numpy as jnp
from jax import lax
from jax.experimental import pallas as pl
from jax.experimental.pallas import tpu as pltpu
from jax.sharding import PartitionSpec as P

NOPE = 128
VDIM = 128
KV_RANK = 512
QK = 192
LAT = 576
KEYS = 2048
ROWS = 512
CHUNK = 512
BF = jnp.bfloat16
F32 = jnp.float32
SCALE = QK ** -0.5
SCALE_LOG2 = SCALE * math.log2(math.e)
AT_QUERY, AT_WEIGHT, AT_TERM, AT_YLO = 128, 132, 140, 204


def mm(a, b):
    return jnp.dot(a, b, preferred_element_type=F32)


def mm_last(a, b):
    return lax.dot_general(a, b, (((1,), (1,)), ((), ())), preferred_element_type=F32)


def mm_first(a, b):
    return lax.dot_general(a, b, (((0,), (0,)), ((), ())), preferred_element_type=F32)


def prepare(ints, lat, lat_t, bias, keys):
    for hh in range(4):
        keys[hh, :, NOPE:] = lat[:, KV_RANK:]
    for block in range(8):
        start = pl.multiple_of(ints[AT_WEIGHT + block], 64)
        lat_t[pl.ds(start, 64), :] = lat[:, block * 64 : block * 64 + 64].T
    lane = lax.broadcasted_iota(jnp.int32, (16, ROWS), 1)
    query_pos = lane % 128 - lax.broadcasted_iota(jnp.int32, (16, ROWS), 0)
    for group in range(4):
        query_pos = query_pos + jnp.where(lane // 128 == group, ints[AT_QUERY + group], 0)
    for i in range(128):
        bias[i * 16 : i * 16 + 16, :] = jnp.where(ints[i] <= query_pos, 0.0, -jnp.inf)


def body(ints, *refs):
    pieces, (q_hbm, g_hbm, far_hbm, w_hbm) = refs[:8], refs[8:12]
    out_hbm, dq_hbm, far_out_hbm, wg_keep_hbm, wg_send_hbm, keep_hbm, send_hbm = refs[12:19]
    lat, q, g, far, w, lat_t, bias, keys, vals, scores, exps, dscores, dkv, rope = refs[19:33]
    out_b, dq_b, far_out, wg_b, keep, send, sems = refs[33:]
    used = []

    def copy(source, target):
        handle = pltpu.make_async_copy(source, target, sems.at[len(used)])
        used.append(handle)
        handle.start()
        return handle

    y_lo = ints[AT_YLO]
    loads = [copy(w_hbm.at[:, pl.ds(pl.multiple_of(y_lo * 1024, 1024), 1024)], w)]
    loads += [copy(piece, lat.at[pl.ds(i * 256, 256), :]) for i, piece in enumerate(pieces)]
    loads += [
        copy(q_hbm.at[:, pl.ds(pl.multiple_of(y_lo * 768, 256), 768)], q),
        copy(g_hbm.at[:, pl.ds(pl.multiple_of(y_lo * 512, 512), 512)], g),
        copy(far_hbm, far),
    ]
    for load in loads:
        load.wait()
    prepare(ints, lat, lat_t, bias, keys)

    chunks = [pl.ds(c * CHUNK, CHUNK) for c in range(KEYS // CHUNK)]
    q_t = jnp.concatenate([q[...].T, far[:, : 4 * QK].T], axis=1)
    g_t = jnp.concatenate([g[...].T, far[:, 4 * QK :].T], axis=1)
    q_h = [q_t[hh * QK : hh * QK + QK] for hh in range(4)]
    g_h = [g_t[hh * VDIM : hh * VDIM + VDIM] for hh in range(4)]
    top, norm, out, inverse, delta, q_s, g_s, dq = ([None] * 4 for _ in range(8))

    def project(pair, r):
        kv = mm(lat[r, :KV_RANK], w[:, pair * 512 : pair * 512 + 512]).astype(BF)
        for hh in range(2):
            keys[pair * 2 + hh, r, :NOPE] = kv[:, hh * 256 : hh * 256 + NOPE]
            vals[pair * 2 + hh, r, :] = kv[:, hh * 256 + NOPE : hh * 256 + 256]

    def score(hh, r):
        s = mm(keys[hh, r, :], q_h[hh]) + bias[r, :]
        scores[hh % 2, r, :] = s
        high = jnp.max(s.reshape(CHUNK // 8, 8, ROWS), axis=0)
        top[hh] = high if top[hh] is None else jnp.maximum(top[hh], high)

    def close_score(hh):
        top[hh] = jnp.max(top[hh], axis=0, keepdims=True) * SCALE_LOG2

    def weigh(hh, r):
        e = jnp.exp2(scores[hh % 2, r, :] * SCALE_LOG2 - top[hh])
        low = e.astype(BF)
        exps[hh % 2, r, :] = low
        total = jnp.sum(e.reshape(CHUNK // 8, 8, ROWS), axis=0)
        norm[hh] = total if norm[hh] is None else norm[hh] + total
        o_t = mm_first(vals[hh, r, :], low)
        out[hh] = o_t if out[hh] is None else out[hh] + o_t

    def close_weigh(hh):
        inv = 1.0 / jnp.sum(norm[hh], axis=0, keepdims=True)
        out[hh] = out[hh] * inv
        delta[hh] = jnp.sum(out[hh] * g_h[hh].astype(F32), axis=0, keepdims=True)
        inverse[hh] = inv
        q_s[hh] = (q_h[hh].astype(F32) * (inv * SCALE)).astype(BF)
        g_s[hh] = (g_h[hh].astype(F32) * inv).astype(BF)

    def back(hh, r):
        e = exps[hh % 2, r, :]
        dp = mm(vals[hh, r, :], g_h[hh])
        ds = (e.astype(F32) * (dp - delta[hh])).astype(BF)
        dscores[hh % 2, r, :] = ds
        dk = mm_last(ds, q_s[hh])
        dv = mm_last(e, g_s[hh])
        dkv[r, hh * 256 : hh * 256 + NOPE] = dk[:, :NOPE].astype(BF)
        dkv[r, hh * 256 + NOPE : hh * 256 + 256] = dv.astype(BF)
        if hh == 0:
            rope[r, :] = dk[:, NOPE:]
        else:
            rope[r, :] += dk[:, NOPE:]

    def query_grad(hh):
        dq[hh] = mm_first(keys[hh], dscores[hh % 2]) * (inverse[hh] * SCALE)

    def finish(pair):
        columns = slice(pair * 256, pair * 256 + 256)
        value = jnp.concatenate(out[pair * 2 : pair * 2 + 2], axis=0).T.astype(BF)
        out_b[:, columns] = value[:256]
        far_out[:, 768 + pair * 256 : 1024 + pair * 256] = value[256:]
        copy(out_b.at[:, columns], out_hbm.at[:, columns])
        columns = slice(pair * 384, pair * 384 + 384)
        value = jnp.concatenate(dq[pair * 2 : pair * 2 + 2], axis=0).T.astype(BF)
        dq_b[:, columns] = value[:256]
        far_out[:, columns] = value[256:]
        copy(dq_b.at[:, columns], dq_hbm.at[:, columns])
        columns = slice(pair * 512, pair * 512 + 512)
        wg = mm(lat_t[...], dkv[:, columns]).astype(BF)
        for k, target in enumerate((wg_keep_hbm, wg_send_hbm)):
            wg_b[k, :, columns] = wg[k * 256 : k * 256 + 256]
            copy(wg_b.at[k, :, columns], target.at[:, columns])

    def latent_terms(c):
        terms = mm_last(dkv[chunks[c], :], w[...]).astype(BF)
        tail = rope[chunks[c], :].astype(BF)
        for i in range(CHUNK // 32):
            block = c * (CHUNK // 32) + i
            index, target = ints[AT_TERM + block], keep if block < 32 else send
            target[index, :, :KV_RANK] = terms[i * 32 : i * 32 + 32]
            target[index, :, KV_RANK:] = tail[i * 32 : i * 32 + 32]

    for r in chunks:
        project(0, r)
        score(0, r)
    close_score(0)
    for r in chunks:
        score(1, r)
        weigh(0, r)
    close_score(1)
    close_weigh(0)
    for r in chunks:
        back(0, r)
        weigh(1, r)
    close_weigh(1)
    for r in chunks:
        back(1, r)
        project(1, r)
        score(2, r)
    close_score(2)
    query_grad(0)
    for r in chunks:
        score(3, r)
        weigh(2, r)
    close_score(3)
    close_weigh(2)
    query_grad(1)
    finish(0)
    for r in chunks:
        back(2, r)
        weigh(3, r)
    close_weigh(3)
    query_grad(2)
    order = list(range(len(chunks)))
    order = order[len(order) // 2 :] + order[: len(order) // 2]
    for c in order:
        back(3, chunks[c])
        latent_terms(c)
        if c == len(chunks) - 1:
            copy(send, send_hbm)
    copy(keep, keep_hbm)
    query_grad(3)
    finish(1)
    copy(far_out, far_out_hbm)
    for store in used[len(loads) :]:
        store.wait()


def attention(ints, pieces, queries, out_grad, far, up_weight):
    def shape(*dims):
        return jax.ShapeDtypeStruct(dims, BF)

    anywhere = pl.BlockSpec(memory_space=pl.ANY)
    return pl.pallas_call(
        body,
        in_specs=[pl.BlockSpec(memory_space=pltpu.SMEM)] + [anywhere] * 12,
        out_specs=[anywhere] * 7,
        out_shape=[
            shape(256, 4 * VDIM),
            shape(256, 4 * QK),
            shape(256, 4 * (QK + VDIM)),
            shape(256, 1024),
            shape(256, 1024),
            shape(32, 32, LAT),
            shape(32, 32, LAT),
        ],
        scratch_shapes=[
            pltpu.VMEM((KEYS, LAT), BF),
            pltpu.VMEM((256, 4 * QK), BF),
            pltpu.VMEM((256, 4 * VDIM), BF),
            pltpu.VMEM((256, 4 * (QK + VDIM)), BF),
            pltpu.VMEM((KV_RANK, 1024), BF),
            pltpu.VMEM((KV_RANK, KEYS), BF),
            pltpu.VMEM((KEYS, ROWS), F32),
            pltpu.VMEM((4, KEYS, QK), BF),
            pltpu.VMEM((4, KEYS, VDIM), BF),
            pltpu.VMEM((2, KEYS, ROWS), F32),
            pltpu.VMEM((2, KEYS, ROWS), BF),
            pltpu.VMEM((2, KEYS, ROWS), BF),
            pltpu.VMEM((KEYS, 1024), BF),
            pltpu.VMEM((KEYS, QK - NOPE), F32),
            pltpu.VMEM((256, 4 * VDIM), BF),
            pltpu.VMEM((256, 4 * QK), BF),
            pltpu.VMEM((256, 4 * (QK + VDIM)), BF),
            pltpu.VMEM((2, 256, 1024), BF),
            pltpu.VMEM((32, 32, LAT), BF),
            pltpu.VMEM((32, 32, LAT), BF),
            pltpu.SemaphoreType.DMA((32,)),
        ],
        compiler_params=pltpu.CompilerParams(vmem_limit_bytes=53 * 2**20),
        cost_estimate=pl.CostEstimate(
            flops=20 * 10**9, bytes_accessed=16 * 2**20, transcendentals=2**22
        ),
    )(ints, *pieces, queries, out_grad, far, up_weight)


AXES = ("ctx", "head")


def device_index(x, y, z, core):
    return ((y % 2) * 4 + x) * 16 + z * 4 + (y // 2) * 2 + core


def trade(value, first, second):
    pairs = []
    for x in range(4):
        for y in range(4):
            for z in range(4):
                for core, (a, b, c) in enumerate((first, second)):
                    pairs.append((device_index(x, y, z, core), device_index(x ^ a, y ^ b, z ^ c, core)))
    return lax.ppermute(value, AXES, pairs)


def swap_cores(value):
    return lax.ppermute(value, "head", [(i, i ^ 1) for i in range(16)])


def swap_ylo(value):
    return trade(value, (0, 1, 0), (0, 1, 0))


def shift(value, first, second):
    pairs = []
    for x in range(4):
        for y in range(4):
            for z in range(4):
                for core, (a, c) in enumerate((first, second)):
                    target = device_index((x + a) % 4, y, (z + c) % 4, core)
                    pairs.append((device_index(x, y, z, core), target))
    return lax.ppermute(value, AXES, pairs)


def exchange_rest(value):
    groups = [
        [device_index(x, yh * 2 + yl, z, 0) for z in range(4) for yl in range(2) for yh in range(2)]
        for x in range(4)
    ] + [
        [device_index(x, yh * 2 + yl, z, 1) for x in range(4) for yl in range(2) for yh in range(2)]
        for z in range(4)
    ]
    return lax.all_to_all(value, AXES, 0, 0, tiled=True, axis_index_groups=groups)


def gather_latent(latent, core):
    blocks = latent.reshape(4, 2, 2, 16, LAT)
    own = jnp.where(core == 0, blocks[:, :, 0], blocks[:, :, 1])
    pair = jnp.stack([own, swap_ylo(own)], axis=0)
    far = {k: shift(pair, (-k, 0), (-k, 0)) for k in (1, 3, 2)}
    mine = [pair, far[1], far[2], far[3]]
    return [piece.reshape(256, LAT) for piece in mine + [swap_cores(piece) for piece in mine]]


def kernel_ints(x, y_lo, z, core, group_order):
    def key_blocks(rel):
        return (x + rel // 2) % 4, y_lo ^ (rel % 2)

    block = jnp.arange(128, dtype=jnp.int32)
    which = core ^ (block // 64)
    far_x, far_y = key_blocks(block // 8 % 8)
    row = ((far_y * 4 + far_x) * 16 + block // 2 % 4 * 4 + block % 2 * 2 + which) * 16
    query = jnp.arange(4, dtype=jnp.int32)
    query = ((y_lo ^ (query // 2)) * 4 + x) * 2 + query % 2
    groups = jnp.concatenate([row // 128, query])
    onehot = groups[:, None] == jnp.arange(16, dtype=jnp.int32)[None, :]
    starts = jnp.sum(jnp.where(onehot, group_order[None, :], 0), axis=1) * 128
    starts = starts + jnp.concatenate([row % 128, jnp.zeros((4,), jnp.int32)])
    block = jnp.arange(8, dtype=jnp.int32)
    gap = (block % 4) ^ x
    slot = jnp.where(core == 0, (gap ^ gap // 2) % 2 * 2 + gap // 2, gap ^ (gap // 2))
    weight_rows = slot * 128 + ((block // 4) ^ y_lo) * 64
    block = jnp.arange(64, dtype=jnp.int32)
    far_x, far_y = key_blocks(block // 4 % 8)
    far_z = block % 4
    x_first = block // 8 % 4 * 8 + far_z * 2 + far_y
    z_first = (far_z - z + 4) % 4 * 8 + far_x * 2 + far_y
    terms = jnp.where((core ^ (block // 32)) == 0, x_first, z_first)
    return jnp.concatenate([starts, weight_rows, terms, y_lo[None]])


def sum_terms(first, others):
    total = first.astype(F32)
    for other in others:
        total = total + other.astype(F32)
    return total


def halves(y_lo, near, far, axis=1):
    low, high = jnp.where(y_lo == 0, near, far), jnp.where(y_lo == 0, far, near)
    return jnp.concatenate([low, high], axis=axis)


def other_half(y_lo, value):
    width = value.shape[1] // 2
    return jnp.where(y_lo == 0, value[:, width:], value[:, :width])


def reduce_terms(y_lo, out, dq, far_out, wg_keep, wg_send, keep, send):
    swapped = swap_cores(send)
    far_out = swap_ylo(far_out)
    wg_near = trade(wg_send, (1, 0, 0), (3, 0, 0))
    wire = [sum_terms(keep[8 * k : 8 * k + 8], [swapped[8 * k : 8 * k + 8]]) for k in range(4)]
    terms = [shift(wire[k].astype(BF), (k, 0), (0, k)) for k in (2, 1, 3)]
    wg_near = lax.optimization_barrier((wg_near, *wire))[0]
    wg_sum = sum_terms(wg_keep, [wg_near]).reshape(2, 2, 64, 1024)
    wire_wg = wg_sum.astype(BF)
    wg_terms = (
        trade(wire_wg[1, 0], (3, 0, 0), (1, 0, 0)),
        trade(wire_wg[1, 1], (3, 1, 0), (1, 1, 0)),
        swap_ylo(wire_wg[0, 1]),
    )
    part = sum_terms(wire[0], terms).astype(BF)
    far_out, wg_x, wg_xy, wg_y = lax.optimization_barrier((part, far_out, *wg_terms))[1:]
    moved = exchange_rest(part.reshape(16, 16, LAT))
    wg = halves(y_lo, sum_terms(wg_sum[0, 0], [wg_x]), sum_terms(wg_y, [wg_xy]))
    query_grad = halves(y_lo, dq, far_out[:, : 4 * QK])
    attn_output = halves(y_lo, out, far_out[:, 4 * QK :])
    latent_grad = sum_terms(moved[0], [moved[i] for i in range(1, 16)])
    return attn_output, query_grad, latent_grad, wg


def local(
    latent, queries, up_weight, out_grad, logratio, student_logprob, teacher_logprob, group_order
):
    ctx, head = lax.axis_index("ctx"), lax.axis_index("head")
    x, y_lo, z, core = ctx % 4, ctx // 4, head // 4, head % 2
    tok_weight = jnp.clip(jnp.exp(logratio), 0.8, 1.25) * (teacher_logprob - student_logprob)
    dout = (tok_weight[:, None] * out_grad.astype(F32)).astype(BF)
    far = jnp.concatenate([other_half(y_lo, queries), other_half(y_lo, dout)], axis=1)
    far = swap_ylo(far)
    pieces = gather_latent(latent, core)
    ints = kernel_ints(x, y_lo, z, core, group_order)
    results = attention(ints, pieces, queries, dout, far, up_weight)
    return reduce_terms(y_lo, *results)


def solution(mesh):
    placed = (
        P("ctx", None),
        P("ctx", "head"),
        P(None, "head"),
        P("ctx", "head"),
        P("ctx"),
        P("ctx"),
        P("ctx"),
        P(),
    )
    return jax.shard_map(
        local,
        mesh=mesh,
        in_specs=placed,
        out_specs=(P("ctx", "head"), P("ctx", "head"), P(AXES, None), P("ctx", "head")),
        check_vma=False,
    )
```

time: 903 us -> 102 us (0.11)
  waiting for transfers between devices: 740 us -> 35 us
  matrix products: 81.5 us -> 0 us
  local copies, waits for them, and re-layouts: 44.2 us -> 2.03 us
  starting transfers between devices: 0.12 us -> 30 us
  Pallas kernels: 0 us -> 25.6 us
  other arithmetic: 21.2 us -> 7.7 us
  between operations: 13.8 us -> 0.98 us
    reduce_scatter x2 -> x0, waiting for transfers between devices: 694 us -> none  [the longest x1 648 us: local(): lax.psum_scatter(latent_terms, ('ctx', 'head'), scatter_dimension=0, tile...]
    dot_general x72 -> x0, matrix products: 81.5 us -> none  [the longest x24 29.5 us: contract_last(): lax.dot_general(former, latter, (((1,), (1,)), ((), ())), preferred_eleme...]
    all_gather x1 -> x0, waiting for transfers between devices: 45.2 us -> none  [local(): gathered = lax.all_gather(latent, 'ctx', axis=0, tiled=True)]
    ppermute x0 -> x18, waiting for transfers between devices: none -> 29.2 us  [the longest x7 14.9 us: trade(): return lax.ppermute(value, AXES, pairs)]
    pallas_call x0 -> x1, Pallas kernels: none -> 25.6 us  [attention(): pl.pallas_call(body, in_specs=[pl.BlockSpec(memory_space=pltpu.SMEM)] + [...]
    while x49 -> x0, local copies, waits for them, and re-layouts: 23.2 us -> none
    ppermute x0 -> x18, starting transfers between devices: none -> 21.9 us  [the longest x6 11.3 us: shift(): return lax.ppermute(value, AXES, pairs)]
    add x9 -> x5, other arithmetic: 13.6 us -> 0.87 us  [the longest x2 0.83 us: sum_terms(): total = total + other.astype(F32)]
  transfers between devices with their start and end apart: 3 -> 19, of which waited for: 3 -> 11; matrix products, arithmetic and copies ran while one was open for 2% -> 7% of each run, Pallas kernels for 0% -> 0%
where the time goes in v5:
time: 102 us; the launch traced here: 101 us
  waiting for transfers between devices  35 us (34%)
  starting transfers between devices  30 us (29%)
  Pallas kernels  25.6 us (25%)
  other arithmetic  7.7 us (8%)
  local copies, waits for them, and re-layouts  2.03 us (2%)
    pallas_call x1, Pallas kernels, attention(): pl.pallas_call(body, in_specs=[pl.BlockSpec(memory_space=pltpu.SMEM)] + [...  25.6 us
    ppermute x7, waiting for transfers between devices, trade(): return lax.ppermute(value, AXES, pairs)  14.9 us
    ppermute x6, waiting for transfers between devices, shift(): return lax.ppermute(value, AXES, pairs)  12.8 us
    ppermute x6, starting transfers between devices, shift(): return lax.ppermute(value, AXES, pairs)  11.3 us
    ppermute x7, starting transfers between devices, trade(): return lax.ppermute(value, AXES, pairs)  9.83 us
    all_to_all x1, starting transfers between devices, exchange_rest(): lax.all_to_all(value, AXES, 0, 0, tiled=True, axis_index_groups=groups)  8.03 us
    all_to_all x1, waiting for transfers between devices, exchange_rest(): lax.all_to_all(value, AXES, 0, 0, tiled=True, axis_index_groups=groups)  5.85 us
    concatenate x3, other arithmetic, halves(): return jnp.concatenate([low, high], axis=axis)  2.62 us
  transfers between devices with their start and end apart: 19, of which 11 were waited for; matrix products, arithmetic and copies ran while one was open for 7% of the time, Pallas kernels for 0%

profile of v5, /device:TPU:0, one launch (start us, length us, event | category | flops | bytes accessed | tf_op | source)
XLA Modules:
  0.0 101.3 jit_solution(15042871019960815627)
XLA Ops:
  0.6 0.0 copy-start.1
  0.6 0.0 copy-start.5
  0.7 1.3 %copy.15 = bf16[256,576]{1,0:T(8,128)(2,1)S(1)} copy(bf16[256,576]{0,1:T(8,128)(2,1)} %param.8) | data formatting | bytes 589824 | tf_op args[0]
  2.0 1.7 %collective-permute-start = (bf16[4,2,16,576]{3,2,1,0:T(8,128)(2,1)S(1)}, bf16[4,2,16,576]{3,2,1,0:T(8,128)(2,1)S(1)}, u32[]{:S(2)}, u32[]{:S(2)}) collective-permute-start(bf16[4,2,16,576]{3,2,1,0:T(8,128)(2,1)S(1)} %get-tuple-element.41), channel_id=1, source_target_pairs={{0,64},{1,65},{4,68},{5,69},{8,72},{9,73},{12,76},{13,77},{64,0},{... | collective-permute-start | bytes 442376 | tf_op jit(solution)/shard_map/ppermute | solution.py:266
  3.7 0.0 copy-done.1
  3.8 0.0 copy-done.2
  3.8 0.2 multiply_convert_fusion.refs_9_
  4.0 0.0 copy-start
  4.0 0.0 copy-start.8
  4.1 0.4 collective-permute-start.8
  4.6 4.5 %collective-permute-done = bf16[4,2,16,576]{3,2,1,0:T(8,128)(2,1)S(1)} collective-permute-done((bf16[4,2,16,576]{3,2,1,0:T(8,128)(2,1)S(1)}, bf16[4,2,16,576]{3,2,1,0:T(8,128)(2,1)S(1)}, u32[]{:S(2)}, u32[]{:S(2)}) %collective-permute-start) | collective-permute-done | bytes 147488 | tf_op jit(solution)/shard_map/ppermute | solution.py:266
  9.2 0.0 copy-done
  9.2 1.6 %collective-permute-start.3 = (bf16[2,4,2,16,576]{4,3,2,1,0:T(8,128)(2,1)S(1)}, bf16[2,4,2,16,576]{4,3,2,1,0:T(8,128)(2,1)S(1)}, u32[]{:S(2)}, u32[]{:S(2)}) collective-permute-start(bf16[2,4,2,16,576]{4,3,2,1,0:T(8,128)(2,1)S(1)} %pad_maximum_fusion.4), channel_id=1, source_target_pairs={{0,16},{1,17},{4,20},{5,21},{8,24},{9,25},{12,28},{13,29},{64,80},... | collective-permute-start | bytes 884744 | tf_op jit(solution)/shard_map/ppermute | solution.py:285
  10.9 2.7 %collective-permute-start.2 = (bf16[2,4,2,16,576]{4,3,2,1,0:T(8,128)(2,1)S(1)}, bf16[2,4,2,16,576]{4,3,2,1,0:T(8,128)(2,1)S(1)}, u32[]{:S(2)}, u32[]{:S(2)}) collective-permute-start(bf16[2,4,2,16,576]{4,3,2,1,0:T(8,128)(2,1)S(1)} %pad_maximum_fusion.4), channel_id=1, source_target_pairs={{0,32},{1,33},{4,36},{5,37},{8,40},{9,41},{12,44},{13,45},{64,96},... | collective-permute-start | bytes 884744 | tf_op jit(solution)/shard_map/ppermute | solution.py:285
  13.6 1.4 %collective-permute-start.1 = (bf16[2,4,2,16,576]{4,3,2,1,0:T(8,128)(2,1)S(1)}, bf16[2,4,2,16,576]{4,3,2,1,0:T(8,128)(2,1)S(1)}, u32[]{:S(2)}, u32[]{:S(2)}) collective-permute-start(bf16[2,4,2,16,576]{4,3,2,1,0:T(8,128)(2,1)S(1)} %pad_maximum_fusion.4), channel_id=1, source_target_pairs={{0,48},{1,49},{4,52},{5,53},{8,56},{9,57},{12,60},{13,61},{64,112}... | collective-permute-start | bytes 884744 | tf_op jit(solution)/shard_map/ppermute | solution.py:285
  15.1 0.1 select_reduce_fusion
  15.2 0.1 collective-permute-start.4
  15.3 4.6 %collective-permute-done.3 = bf16[2,4,2,16,576]{4,3,2,1,0:T(8,128)(2,1)S(1)} collective-permute-done((bf16[2,4,2,16,576]{4,3,2,1,0:T(8,128)(2,1)S(1)}, bf16[2,4,2,16,576]{4,3,2,1,0:T(8,128)(2,1)S(1)}, u32[]{:S(2)}, u32[]{:S(2)}) %collective-permute-start.3) | collective-permute-done | bytes 294944 | tf_op jit(solution)/shard_map/ppermute | solution.py:285
  19.9 0.0 collective-permute-start.7
  19.9 6.2 %collective-permute-done.2 = bf16[2,4,2,16,576]{4,3,2,1,0:T(8,128)(2,1)S(1)} collective-permute-done((bf16[2,4,2,16,576]{4,3,2,1,0:T(8,128)(2,1)S(1)}, bf16[2,4,2,16,576]{4,3,2,1,0:T(8,128)(2,1)S(1)}, u32[]{:S(2)}, u32[]{:S(2)}) %collective-permute-start.2) | collective-permute-done | bytes 294944 | tf_op jit(solution)/shard_map/ppermute | solution.py:285
  26.0 0.0 collective-permute-start.6
  26.0 0.0 collective-permute-done.1
  26.0 0.5 collective-permute-start.5
  26.5 0.1 pad_add_fusion.1.ints
  26.6 0.0 collective-permute-done.4
  26.6 0.0 collective-permute-done.8.refs_10_
  26.6 0.0 copy-start.9
  26.6 0.0 collective-permute-done.7
  26.7 1.0 collective-permute-done.6
  27.7 0.5 collective-permute-done.5
  28.2 0.2 copy-done.14
  28.4 0.5 copy-done.15
  28.8 25.6 %shard_map.111 = (bf16[256,512]{1,0:T(8,128)(2,1)S(1)}, bf16[256,768]{1,0:T(8,128)(2,1)}, bf16[256,1280]{1,0:T(8,128)(2,1)}, bf16[256,1024]{1,0:T(8,128)(2,1)}, ...) custom-call(s32[205]{0:T(256)S(1)} %pad_add_fusion.1.ints, ...), custom_call_target="tpu_custom_call" | custom-call | flops 20000000000 | bytes 16777216 | tf_op jit(solution)/shard_map/pallas_call | solution.py:209
  54.5 0.2 collective-permute-start.9
  54.7 0.7 collective-permute-start.14
  55.4 1.7 %collective-permute-start.13 = (bf16[256,1280]{1,0:T(8,128)(2,1)}, bf16[256,1280]{1,0:T(8,128)(2,1)S(1)}, u32[]{:S(2)}, u32[]{:S(2)}) collective-permute-start(bf16[256,1280]{1,0:T(8,128)(2,1)} %get-tuple-element.19), channel_id=1, source_target_pairs={{0,64},{1,65},{4,68},{5,69},{8,72},{9,73},{12,76},{13,77},{64,0},{... | collective-permute-start | bytes 1966088 | tf_op jit(solution)/shard_map/ppermute | solution.py:266
  57.1 6.9 %collective-permute-done.14 = bf16[256,1024]{1,0:T(8,128)(2,1)S(1)} collective-permute-done((bf16[256,1024]{1,0:T(8,128)(2,1)}, bf16[256,1024]{1,0:T(8,128)(2,1)S(1)}, u32[]{:S(2)}, u32[]{:S(2)}) %collective-permute-start.14) | collective-permute-done | bytes 524320 | tf_op jit(solution)/shard_map/ppermute | solution.py:266
  64.1 0.0 collective-permute-done.9
  64.1 1.5 %fusion.46 = (bf16[8,32,576]{2,1,0:T(8,128)(2,1)S(1)}, bf16[8,32,576]{2,1,0:T(8,128)(2,1)S(1)}, bf16[8,32,576]{2,1,0:T(8,128)(2,1)S(1)}) fusion(bf16[32,32,576]{2,1,0:T(8,128)(2,1)S(1)} %collective-permute-done.9, bf16[32,32,576]{2,1,0:T(8,128)(2,1)} %get-tuple-element.17), kind=kLoop, calls=%fused_computation.153 | loop fusion | flops 1769472 | bytes 2654208 | tf_op jit(solution)/shard_map/convert_element_type | solution.py:357
  65.6 2.3 %collective-permute-start.10 = (bf16[8,32,576]{2,1,0:T(8,128)(2,1)S(1)}, bf16[8,32,576]{2,1,0:T(8,128)(2,1)S(1)}, u32[]{:S(2)}, u32[]{:S(2)}) collective-permute-start(bf16[8,32,576]{2,1,0:T(8,128)(2,1)S(1)} %get-tuple-element.28), channel_id=1, source_target_pairs={{0,32},{1,9},{4,36},{5,13},{8,40},{9,1},{12,44},{13,5},{64,96},{65... | collective-permute-start | bytes 884744 | tf_op jit(solution)/shard_map/ppermute | solution.py:285
  67.8 0.4 collective-permute-start.11
  68.2 2.9 %collective-permute-start.12 = (bf16[8,32,576]{2,1,0:T(8,128)(2,1)S(1)}, bf16[8,32,576]{2,1,0:T(8,128)(2,1)S(1)}, u32[]{:S(2)}, u32[]{:S(2)}) collective-permute-start(bf16[8,32,576]{2,1,0:T(8,128)(2,1)S(1)} %get-tuple-element.30), channel_id=1, source_target_pairs={{0,48},{1,13},{4,52},{5,1},{8,56},{9,5},{12,60},{13,9},{64,112},{6... | collective-permute-start | bytes 884744 | tf_op jit(solution)/shard_map/ppermute | solution.py:285
  71.1 0.2 convert_add_fusion
  71.2 0.1 convert_element_type.176
  71.4 1.7 %collective-permute-start.17 = (bf16[64,1024]{1,0:T(8,128)(2,1)S(1)}, bf16[64,1024]{1,0:T(8,128)(2,1)S(1)}, u32[]{:S(2)}, u32[]{:S(2)}) collective-permute-start(bf16[64,1024]{1,0:T(8,128)(2,1)S(1)} %get-tuple-element.37), channel_id=1, source_target_pairs={{0,64},{1,65},{4,68},{5,69},{8,72},{9,73},{12,76},{13,77},{64,0},{... | collective-permute-start | bytes 393224 | tf_op jit(solution)/shard_map/ppermute | solution.py:266
  73.0 1.3 %collective-permute-done.10 = bf16[8,32,576]{2,1,0:T(8,128)(2,1)S(1)} collective-permute-done((bf16[8,32,576]{2,1,0:T(8,128)(2,1)S(1)}, bf16[8,32,576]{2,1,0:T(8,128)(2,1)S(1)}, u32[]{:S(2)}, u32[]{:S(2)}) %collective-permute-start.10) | collective-permute-done | bytes 294944 | tf_op jit(solution)/shard_map/ppermute | solution.py:285
  74.3 2.7 %collective-permute-start.16 = (bf16[64,1024]{1,0:T(8,128)(2,1)S(1)}, bf16[64,1024]{1,0:T(8,128)(2,1)S(1)}, u32[]{:S(2)}, u32[]{:S(2)}) collective-permute-start(bf16[64,1024]{1,0:T(8,128)(2,1)S(1)} %get-tuple-element.38), channel_id=1, source_target_pairs={{0,112},{1,81},{4,116},{5,85},{8,120},{9,89},{12,124},{13,93},{64,... | collective-permute-start | bytes 393224 | tf_op jit(solution)/shard_map/ppermute | solution.py:266
  77.0 0.7 collective-permute-done.11
  77.7 0.8 collective-permute-start.15
  78.6 0.0 collective-permute-done.12
  78.6 1.9 %add_convert_fusion = bf16[8,32,576]{2,1,0:T(8,128)(2,1)} fusion(bf16[8,32,576]{2,1,0:T(8,128)(2,1)S(1)} %collective-permute-done.12, bf16[8,32,576]{2,1,0:T(8,128)(2,1)S(1)} %collective-permute-done.11, bf16[8,32,576]{2,1,0:T(8,128)(2,1)S(1)} %collective-permute-done.10, bf16[32,32,576]{2,1,0:T(8,128)(2,1)S(1)} %collective-permute-done.9, ...), kind=kLoop, calls=%fused_computation.4 | loop fusion | flops 1474560 | bytes 1769472 | tf_op jit(solution)/shard_map/convert_element_type | solution.py:366
  80.5 0.0 collective-permute-done.17
  80.5 0.9 collective-permute-done.16
  81.4 2.5 %collective-permute-done.15 = bf16[64,1024]{1,0:T(8,128)(2,1)S(1)} collective-permute-done((bf16[64,1024]{1,0:T(8,128)(2,1)S(1)}, bf16[64,1024]{1,0:T(8,128)(2,1)S(1)}, u32[]{:S(2)}, u32[]{:S(2)}) %collective-permute-start.15) | collective-permute-done | bytes 131104 | tf_op jit(solution)/shard_map/ppermute | solution.py:266
  83.9 0.0 collective-permute-done.13
  83.9 8.0 %all-to-all-start = ((bf16[16,16,576]{2,1,0:T(8,128)(2,1)}), bf16[16,16,576]{2,1,0:T(8,128)(2,1)S(1)}, u32[]{:S(2)}, u32[]{:S(2)}) async-start(bf16[16,16,576]{2,1,0:T(8,128)(2,1)} %bitcast.17), calls=%async_computation | async-start | bytes 655360 | tf_op jit(solution)/shard_map/all_to_all | solution.py:296
  92.0 0.0 copy-done.4
  92.0 0.1 broadcast_select_fusion.1
  92.1 0.1 fusion.2
  92.2 0.8 pad_maximum_fusion.3
  93.0 0.9 pad_maximum_fusion.2
  93.8 0.9 pad_maximum_fusion
  94.8 5.9 %all-to-all-done = bf16[16,16,576]{2,1,0:T(8,128)(2,1)S(1)} async-done(((bf16[16,16,576]{2,1,0:T(8,128)(2,1)}), bf16[16,16,576]{2,1,0:T(8,128)(2,1)S(1)}, u32[]{:S(2)}, u32[]{:S(2)}) %all-to-all-start) | async-done | bytes 294944 | tf_op jit(solution)/shard_map/all_to_all | solution.py:296
  100.6 0.7 convert_add_fusion.6
  (35 shorter events, 0.4 us)
Async XLA Ops:
  0.6 3.1 %copy-start.1 = (bf16[256,1536]{1,0:T(8,128)(2,1)S(1)}, bf16[256,1536]{1,0:T(8,128)(2,1)}, u32[]{:S(2)}) copy-start(bf16[256,1536]{1,0:T(8,128)(2,1)} %refs_8_.1) | copy-start | bytes 2359300
  0.6 3.1 %copy-start.5 = (f32[256]{0:T(256)S(1)}, f32[256]{0:T(256)}, u32[]{:S(2)}) copy-start(f32[256]{0:T(256)} %param.14) | copy-start | bytes 3076
  0.7 3.1 %copy-start.6 = (f32[256]{0:T(256)S(1)}, f32[256]{0:T(256)}, u32[]{:S(2)}) copy-start(f32[256]{0:T(256)} %param.13) | copy-start | bytes 3076
  0.7 3.1 %copy-start.7 = (f32[256]{0:T(256)S(1)}, f32[256]{0:T(256)}, u32[]{:S(2)}) copy-start(f32[256]{0:T(256)} %param.12) | copy-start | bytes 3076
  0.7 3.2 %copy-start.2 = (bf16[256,1024]{1,0:T(8,128)(2,1)S(1)}, bf16[256,1024]{1,0:T(8,128)(2,1)}, u32[]{:S(2)}) copy-start(bf16[256,1024]{1,0:T(8,128)(2,1)} %param.11) | copy-start | bytes 1572868
  2.0 7.2 %collective-permute-start = (bf16[4,2,16,576]{3,2,1,0:T(8,128)(2,1)S(1)}, bf16[4,2,16,576]{3,2,1,0:T(8,128)(2,1)S(1)}, u32[]{:S(2)}, u32[]{:S(2)}) collective-permute-start(bf16[4,2,16,576]{3,2,1,0:T(8,128)(2,1)S(1)} %get-tuple-element.41), channel_id=1, source_target_pairs={{0,64},{1,65},{4,68},{5,69},{8,72},{9,73},{12,76},{13,77},{64,0},{... | collective-permute-start | bytes 442376 | tf_op jit(solution)/shard_map/ppermute | solution.py:266
  4.0 5.2 %copy-start = (bf16[256,1024]{1,0:T(8,128)(2,1)}, bf16[256,1024]{1,0:T(8,128)(2,1)S(1)}, u32[]{:S(2)}) copy-start(bf16[256,1024]{1,0:T(8,128)(2,1)S(1)} %multiply_convert_fusion.refs_9_) | copy-start | bytes 1572868
  4.0 11.1 %copy-start.8 = (s32[16]{0:T(128)S(1)}, s32[16]{0:T(128)}, u32[]{:S(2)}) copy-start(s32[16]{0:T(128)} %param.15) | copy-start | bytes 196
  4.1 22.5 %collective-permute-start.8 = (bf16[256,1280]{1,0:T(8,128)(2,1)S(1)}, bf16[256,1280]{1,0:T(8,128)(2,1)S(1)}, u32[]{:S(2)}, u32[]{:S(2)}) collective-permute-start(bf16[256,1280]{1,0:T(8,128)(2,1)S(1)} %pad_maximum_fusion.1), channel_id=1, source_target_pairs={{0,64},{1,65},{4,68},{5,69},{8,72},{9,73},{12,76},{13,77},{64,0},{... | collective-permute-start | bytes 1966088 | tf_op jit(solution)/shard_map/ppermute | solution.py:266
  9.2 10.6 %collective-permute-start.3 = (bf16[2,4,2,16,576]{4,3,2,1,0:T(8,128)(2,1)S(1)}, bf16[2,4,2,16,576]{4,3,2,1,0:T(8,128)(2,1)S(1)}, u32[]{:S(2)}, u32[]{:S(2)}) collective-permute-start(bf16[2,4,2,16,576]{4,3,2,1,0:T(8,128)(2,1)S(1)} %pad_maximum_fusion.4), channel_id=1, source_target_pairs={{0,16},{1,17},{4,20},{5,21},{8,24},{9,25},{12,28},{13,29},{64,80},... | collective-permute-start | bytes 884744 | tf_op jit(solution)/shard_map/ppermute | solution.py:285
  10.9 15.2 %collective-permute-start.2 = (bf16[2,4,2,16,576]{4,3,2,1,0:T(8,128)(2,1)S(1)}, bf16[2,4,2,16,576]{4,3,2,1,0:T(8,128)(2,1)S(1)}, u32[]{:S(2)}, u32[]{:S(2)}) collective-permute-start(bf16[2,4,2,16,576]{4,3,2,1,0:T(8,128)(2,1)S(1)} %pad_maximum_fusion.4), channel_id=1, source_target_pairs={{0,32},{1,33},{4,36},{5,37},{8,40},{9,41},{12,44},{13,45},{64,96},... | collective-permute-start | bytes 884744 | tf_op jit(solution)/shard_map/ppermute | solution.py:285
  13.6 12.4 %collective-permute-start.1 = (bf16[2,4,2,16,576]{4,3,2,1,0:T(8,128)(2,1)S(1)}, bf16[2,4,2,16,576]{4,3,2,1,0:T(8,128)(2,1)S(1)}, u32[]{:S(2)}, u32[]{:S(2)}) collective-permute-start(bf16[2,4,2,16,576]{4,3,2,1,0:T(8,128)(2,1)S(1)} %pad_maximum_fusion.4), channel_id=1, source_target_pairs={{0,48},{1,49},{4,52},{5,53},{8,56},{9,57},{12,60},{13,61},{64,112}... | collective-permute-start | bytes 884744 | tf_op jit(solution)/shard_map/ppermute | solution.py:285
  15.2 11.5 %collective-permute-start.4 = (bf16[2,4,2,16,576]{4,3,2,1,0:T(8,128)(2,1)S(1)}, bf16[2,4,2,16,576]{4,3,2,1,0:T(8,128)(2,1)S(1)}, u32[]{:S(2)}, u32[]{:S(2)}) collective-permute-start(bf16[2,4,2,16,576]{4,3,2,1,0:T(8,128)(2,1)S(1)} %pad_maximum_fusion.4), channel_id=1, source_target_pairs={{0,1},{1,0},{2,3},{3,2},{4,5},{5,4},{6,7},{7,6},{8,9},{9,8},{10,11... | collective-permute-start | bytes 884744 | tf_op jit(solution)/shard_map/ppermute | solution.py:270
  19.9 8.3 %copy-start.10 = (bf16[2,4,2,16,576]{4,3,2,1,0:T(8,128)(2,1)}, bf16[2,4,2,16,576]{4,3,2,1,0:T(8,128)(2,1)S(1)}, u32[]{:S(2)}) copy-start(bf16[2,4,2,16,576]{4,3,2,1,0:T(8,128)(2,1)S(1)} %collective-permute-done.3) | copy-start | bytes 884740
  19.9 6.8 %collective-permute-start.7 = (bf16[2,4,2,16,576]{4,3,2,1,0:T(8,128)(2,1)S(1)}, bf16[2,4,2,16,576]{4,3,2,1,0:T(8,128)(2,1)S(1)}, u32[]{:S(2)}, u32[]{:S(2)}) collective-permute-start(bf16[2,4,2,16,576]{4,3,2,1,0:T(8,128)(2,1)S(1)} %collective-permute-done.3), channel_id=1, source_target_pairs={{0,1},{1,0},{2,3},{3,2},{4,5},{5,4},{6,7},{7,6},{8,9},{9,8},{10,11... | collective-permute-start | bytes 884744 | tf_op jit(solution)/shard_map/ppermute | solution.py:270
  26.0 2.1 %copy-start.11 = (bf16[2,4,2,16,576]{4,3,2,1,0:T(8,128)(2,1)}, bf16[2,4,2,16,576]{4,3,2,1,0:T(8,128)(2,1)S(1)}, u32[]{:S(2)}) copy-start(bf16[2,4,2,16,576]{4,3,2,1,0:T(8,128)(2,1)S(1)} %collective-permute-done.2) | copy-start | bytes 884740
  26.0 1.6 %collective-permute-start.6 = (bf16[2,4,2,16,576]{4,3,2,1,0:T(8,128)(2,1)S(1)}, bf16[2,4,2,16,576]{4,3,2,1,0:T(8,128)(2,1)S(1)}, u32[]{:S(2)}, u32[]{:S(2)}) collective-permute-start(bf16[2,4,2,16,576]{4,3,2,1,0:T(8,128)(2,1)S(1)} %collective-permute-done.2), channel_id=1, source_target_pairs={{0,1},{1,0},{2,3},{3,2},{4,5},{5,4},{6,7},{7,6},{8,9},{9,8},{10,11... | collective-permute-start | bytes 884744 | tf_op jit(solution)/shard_map/ppermute | solution.py:270
  26.0 2.1 %collective-permute-start.5 = (bf16[2,4,2,16,576]{4,3,2,1,0:T(8,128)(2,1)S(1)}, bf16[2,4,2,16,576]{4,3,2,1,0:T(8,128)(2,1)S(1)}, u32[]{:S(2)}, u32[]{:S(2)}) collective-permute-start(bf16[2,4,2,16,576]{4,3,2,1,0:T(8,128)(2,1)S(1)} %collective-permute-done.1), channel_id=1, source_target_pairs={{0,1},{1,0},{2,3},{3,2},{4,5},{5,4},{6,7},{7,6},{8,9},{9,8},{10,11... | collective-permute-start | bytes 884744 | tf_op jit(solution)/shard_map/ppermute | solution.py:270
  26.6 1.5 %copy-start.12 = (bf16[2,4,2,16,576]{4,3,2,1,0:T(8,128)(2,1)}, bf16[2,4,2,16,576]{4,3,2,1,0:T(8,128)(2,1)S(1)}, u32[]{:S(2)}) copy-start(bf16[2,4,2,16,576]{4,3,2,1,0:T(8,128)(2,1)S(1)} %collective-permute-done.4) | copy-start | bytes 884740
  26.6 1.5 %copy-start.9 = (bf16[256,1280]{1,0:T(8,128)(2,1)}, bf16[256,1280]{1,0:T(8,128)(2,1)S(1)}, u32[]{:S(2)}) copy-start(bf16[256,1280]{1,0:T(8,128)(2,1)S(1)} %collective-permute-done.8.refs_10_) | copy-start | bytes 1966084
  26.7 1.5 %copy-start.13 = (bf16[2,4,2,16,576]{4,3,2,1,0:T(8,128)(2,1)}, bf16[2,4,2,16,576]{4,3,2,1,0:T(8,128)(2,1)S(1)}, u32[]{:S(2)}) copy-start(bf16[2,4,2,16,576]{4,3,2,1,0:T(8,128)(2,1)S(1)} %collective-permute-done.7) | copy-start | bytes 884740
  27.7 0.7 copy-start.14
  28.1 0.7 copy-start.15
  54.5 9.6 %collective-permute-start.9 = (bf16[32,32,576]{2,1,0:T(8,128)(2,1)}, bf16[32,32,576]{2,1,0:T(8,128)(2,1)S(1)}, u32[]{:S(2)}, u32[]{:S(2)}) collective-permute-start(bf16[32,32,576]{2,1,0:T(8,128)(2,1)} %get-tuple-element.18), channel_id=1, source_target_pairs={{0,1},{1,0},{2,3},{3,2},{4,5},{5,4},{6,7},{7,6},{8,9},{9,8},{10,11... | collective-permute-start | bytes 3538952 | tf_op jit(solution)/shard_map/ppermute | solution.py:270
  54.7 9.4 %collective-permute-start.14 = (bf16[256,1024]{1,0:T(8,128)(2,1)}, bf16[256,1024]{1,0:T(8,128)(2,1)S(1)}, u32[]{:S(2)}, u32[]{:S(2)}) collective-permute-start(bf16[256,1024]{1,0:T(8,128)(2,1)} %get-tuple-element.21), channel_id=1, source_target_pairs={{0,16},{1,49},{4,20},{5,53},{8,24},{9,57},{12,28},{13,61},{64,80},... | collective-permute-start | bytes 1572872 | tf_op jit(solution)/shard_map/ppermute | solution.py:266
  55.4 28.5 %collective-permute-start.13 = (bf16[256,1280]{1,0:T(8,128)(2,1)}, bf16[256,1280]{1,0:T(8,128)(2,1)S(1)}, u32[]{:S(2)}, u32[]{:S(2)}) collective-permute-start(bf16[256,1280]{1,0:T(8,128)(2,1)} %get-tuple-element.19), channel_id=1, source_target_pairs={{0,64},{1,65},{4,68},{5,69},{8,72},{9,73},{12,76},{13,77},{64,0},{... | collective-permute-start | bytes 1966088 | tf_op jit(solution)/shard_map/ppermute | solution.py:266
  64.1 7.0 %copy-start.3 = (bf16[256,1024]{1,0:T(8,128)(2,1)S(1)}, bf16[256,1024]{1,0:T(8,128)(2,1)}, u32[]{:S(2)}) copy-start(bf16[256,1024]{1,0:T(8,128)(2,1)} %get-tuple-element.20) | copy-start | bytes 1572868
  65.6 8.8 %collective-permute-start.10 = (bf16[8,32,576]{2,1,0:T(8,128)(2,1)S(1)}, bf16[8,32,576]{2,1,0:T(8,128)(2,1)S(1)}, u32[]{:S(2)}, u32[]{:S(2)}) collective-permute-start(bf16[8,32,576]{2,1,0:T(8,128)(2,1)S(1)} %get-tuple-element.28), channel_id=1, source_target_pairs={{0,32},{1,9},{4,36},{5,13},{8,40},{9,1},{12,44},{13,5},{64,96},{65... | collective-permute-start | bytes 884744 | tf_op jit(solution)/shard_map/ppermute | solution.py:285
  67.8 9.9 %collective-permute-start.11 = (bf16[8,32,576]{2,1,0:T(8,128)(2,1)S(1)}, bf16[8,32,576]{2,1,0:T(8,128)(2,1)S(1)}, u32[]{:S(2)}, u32[]{:S(2)}) collective-permute-start(bf16[8,32,576]{2,1,0:T(8,128)(2,1)S(1)} %get-tuple-element.29), channel_id=1, source_target_pairs={{0,16},{1,5},{4,20},{5,9},{8,24},{9,13},{12,28},{13,1},{64,80},{65... | collective-permute-start | bytes 884744 | tf_op jit(solution)/shard_map/ppermute | solution.py:285
  68.2 10.4 %collective-permute-start.12 = (bf16[8,32,576]{2,1,0:T(8,128)(2,1)S(1)}, bf16[8,32,576]{2,1,0:T(8,128)(2,1)S(1)}, u32[]{:S(2)}, u32[]{:S(2)}) collective-permute-start(bf16[8,32,576]{2,1,0:T(8,128)(2,1)S(1)} %get-tuple-element.30), channel_id=1, source_target_pairs={{0,48},{1,13},{4,52},{5,1},{8,56},{9,5},{12,60},{13,9},{64,112},{6... | collective-permute-start | bytes 884744 | tf_op jit(solution)/shard_map/ppermute | solution.py:285
  71.4 9.1 %collective-permute-start.17 = (bf16[64,1024]{1,0:T(8,128)(2,1)S(1)}, bf16[64,1024]{1,0:T(8,128)(2,1)S(1)}, u32[]{:S(2)}, u32[]{:S(2)}) collective-permute-start(bf16[64,1024]{1,0:T(8,128)(2,1)S(1)} %get-tuple-element.37), channel_id=1, source_target_pairs={{0,64},{1,65},{4,68},{5,69},{8,72},{9,73},{12,76},{13,77},{64,0},{... | collective-permute-start | bytes 393224 | tf_op jit(solution)/shard_map/ppermute | solution.py:266
  74.3 7.1 %collective-permute-start.16 = (bf16[64,1024]{1,0:T(8,128)(2,1)S(1)}, bf16[64,1024]{1,0:T(8,128)(2,1)S(1)}, u32[]{:S(2)}, u32[]{:S(2)}) collective-permute-start(bf16[64,1024]{1,0:T(8,128)(2,1)S(1)} %get-tuple-element.38), channel_id=1, source_target_pairs={{0,112},{1,81},{4,116},{5,85},{8,120},{9,89},{12,124},{13,93},{64,... | collective-permute-start | bytes 393224 | tf_op jit(solution)/shard_map/ppermute | solution.py:266
  77.7 6.2 %collective-permute-start.15 = (bf16[64,1024]{1,0:T(8,128)(2,1)S(1)}, bf16[64,1024]{1,0:T(8,128)(2,1)S(1)}, u32[]{:S(2)}, u32[]{:S(2)}) collective-permute-start(bf16[64,1024]{1,0:T(8,128)(2,1)S(1)} %get-tuple-element.39), channel_id=1, source_target_pairs={{0,48},{1,17},{4,52},{5,21},{8,56},{9,25},{12,60},{13,29},{64,112}... | collective-permute-start | bytes 393224 | tf_op jit(solution)/shard_map/ppermute | solution.py:266
  80.5 11.5 %copy-start.4 = (bf16[256,768]{1,0:T(8,128)(2,1)S(1)}, bf16[256,768]{1,0:T(8,128)(2,1)}, u32[]{:S(2)}) copy-start(bf16[256,768]{1,0:T(8,128)(2,1)} %get-tuple-element.24) | copy-start | bytes 1179652
  83.9 16.7 %all-to-all-start = ((bf16[16,16,576]{2,1,0:T(8,128)(2,1)}), bf16[16,16,576]{2,1,0:T(8,128)(2,1)S(1)}, u32[]{:S(2)}, u32[]{:S(2)}) async-start(bf16[16,16,576]{2,1,0:T(8,128)(2,1)} %bitcast.17), calls=%async_computation | async-start | bytes 655360 | tf_op jit(solution)/shard_map/all_to_all | solution.py:296

commit v6 on v5

--- a/solution.py
+++ b/solution.py
@@ -355,7 +355,7 @@
     wg_near = trade(wg_send, (1, 0, 0), (3, 0, 0))
     wire = [sum_terms(keep[8 * k : 8 * k + 8], [swapped[8 * k : 8 * k + 8]]) for k in range(4)]
     terms = [shift(wire[k].astype(BF), (k, 0), (0, k)) for k in (2, 1, 3)]
-    wg_near = lax.optimization_barrier((wg_near, *wire))[0]
+    wg_near = lax.optimization_barrier((wg_near, terms[0]))[0]
     wg_sum = sum_terms(wg_keep, [wg_near]).reshape(2, 2, 64, 1024)
     wire_wg = wg_sum.astype(BF)
     wg_terms = (

time: 102 us -> 93.6 us (0.918)
  waiting for transfers between devices: 35 us -> 28.5 us
  starting transfers between devices: 30 us -> 28.5 us
    ppermute x7, waiting for transfers between devices: 14.9 us -> 5.03 us  [trade(): return lax.ppermute(value, AXES, pairs)]
    ppermute x5, waiting for transfers between devices: 1.46 us -> 3.81 us  [swap_cores(): return lax.ppermute(value, 'head', [(i, i ^ 1) for i in range(16)])]
    ppermute x6, waiting for transfers between devices: 12.8 us -> 14.3 us  [shift(): return lax.ppermute(value, AXES, pairs)]
    ppermute x6, starting transfers between devices: 11.3 us -> 10.1 us  [shift(): return lax.ppermute(value, AXES, pairs)]
  transfers between devices with their start and end apart: 19 -> 19, of which waited for: 11 -> 9; matrix products, arithmetic and copies ran while one was open for 7% -> 8% of each run, Pallas kernels for 0% -> 0%
where the time goes in v6:
time: 93.6 us; the launch traced here: 93.3 us
  starting transfers between devices  28.5 us (30%)
  waiting for transfers between devices  28.5 us (30%)
  Pallas kernels  25.6 us (27%)
  other arithmetic  7.7 us (8%)
  local copies, waits for them, and re-layouts  2.03 us (2%)
  between operations  0.98 us (1%)
    pallas_call x1, Pallas kernels, attention(): pl.pallas_call(body, in_specs=[pl.BlockSpec(memory_space=pltpu.SMEM)] + [...  25.6 us
    ppermute x6, waiting for transfers between devices, shift(): return lax.ppermute(value, AXES, pairs)  14.3 us
    ppermute x6, starting transfers between devices, shift(): return lax.ppermute(value, AXES, pairs)  10.1 us
    ppermute x7, starting transfers between devices, trade(): return lax.ppermute(value, AXES, pairs)  9.29 us
    all_to_all x1, starting transfers between devices, exchange_rest(): lax.all_to_all(value, AXES, 0, 0, tiled=True, axis_index_groups=groups)  8.27 us
    all_to_all x1, waiting for transfers between devices, exchange_rest(): lax.all_to_all(value, AXES, 0, 0, tiled=True, axis_index_groups=groups)  5.36 us
    ppermute x7, waiting for transfers between devices, trade(): return lax.ppermute(value, AXES, pairs)  5.03 us
    ppermute x5, waiting for transfers between devices, swap_cores(): return lax.ppermute(value, 'head', [(i, i ^ 1) for i in range(16)])  3.81 us
  transfers between devices with their start and end apart: 19, of which 9 were waited for; matrix products, arithmetic and copies ran while one was open for 8% of the time, Pallas kernels for 0%

profile of v6, /device:TPU:0, one launch (start us, length us, event | category | flops | bytes accessed | tf_op | source)
XLA Modules:
  0.0 93.3 jit_solution(3212953534839008178)
XLA Ops:
  0.6 0.0 copy-start.1
  0.7 1.3 %copy.15 = bf16[256,576]{1,0:T(8,128)(2,1)S(1)} copy(bf16[256,576]{0,1:T(8,128)(2,1)} %param.8) | data formatting | bytes 589824 | tf_op args[0]
  2.0 1.7 %collective-permute-start = (bf16[4,2,16,576]{3,2,1,0:T(8,128)(2,1)S(1)}, bf16[4,2,16,576]{3,2,1,0:T(8,128)(2,1)S(1)}, u32[]{:S(2)}, u32[]{:S(2)}) collective-permute-start(bf16[4,2,16,576]{3,2,1,0:T(8,128)(2,1)S(1)} %get-tuple-element.41), channel_id=1, source_target_pairs={{0,64},{1,65},{4,68},{5,69},{8,72},{9,73},{12,76},{13,77},{64,0},{... | collective-permute-start | bytes 442376 | tf_op jit(solution)/shard_map/ppermute | solution.py:266
  3.7 0.0 copy-done.1
  3.8 0.0 copy-done.5
  3.8 0.0 copy-done.6
  3.8 0.0 copy-done.7
  3.8 0.0 copy-done.2
  3.8 0.2 multiply_convert_fusion.refs_9_
  4.0 0.0 copy-start
  4.0 0.0 copy-start.8
  4.1 0.4 collective-permute-start.8
  4.6 4.5 %collective-permute-done = bf16[4,2,16,576]{3,2,1,0:T(8,128)(2,1)S(1)} collective-permute-done((bf16[4,2,16,576]{3,2,1,0:T(8,128)(2,1)S(1)}, bf16[4,2,16,576]{3,2,1,0:T(8,128)(2,1)S(1)}, u32[]{:S(2)}, u32[]{:S(2)}) %collective-permute-start) | collective-permute-done | bytes 147488 | tf_op jit(solution)/shard_map/ppermute | solution.py:266
  9.2 1.6 %collective-permute-start.3 = (bf16[2,4,2,16,576]{4,3,2,1,0:T(8,128)(2,1)S(1)}, bf16[2,4,2,16,576]{4,3,2,1,0:T(8,128)(2,1)S(1)}, u32[]{:S(2)}, u32[]{:S(2)}) collective-permute-start(bf16[2,4,2,16,576]{4,3,2,1,0:T(8,128)(2,1)S(1)} %pad_maximum_fusion.4), channel_id=1, source_target_pairs={{0,16},{1,17},{4,20},{5,21},{8,24},{9,25},{12,28},{13,29},{64,80},... | collective-permute-start | bytes 884744 | tf_op jit(solution)/shard_map/ppermute | solution.py:285
  10.9 2.7 %collective-permute-start.2 = (bf16[2,4,2,16,576]{4,3,2,1,0:T(8,128)(2,1)S(1)}, bf16[2,4,2,16,576]{4,3,2,1,0:T(8,128)(2,1)S(1)}, u32[]{:S(2)}, u32[]{:S(2)}) collective-permute-start(bf16[2,4,2,16,576]{4,3,2,1,0:T(8,128)(2,1)S(1)} %pad_maximum_fusion.4), channel_id=1, source_target_pairs={{0,32},{1,33},{4,36},{5,37},{8,40},{9,41},{12,44},{13,45},{64,96},... | collective-permute-start | bytes 884744 | tf_op jit(solution)/shard_map/ppermute | solution.py:285
  13.6 1.4 %collective-permute-start.1 = (bf16[2,4,2,16,576]{4,3,2,1,0:T(8,128)(2,1)S(1)}, bf16[2,4,2,16,576]{4,3,2,1,0:T(8,128)(2,1)S(1)}, u32[]{:S(2)}, u32[]{:S(2)}) collective-permute-start(bf16[2,4,2,16,576]{4,3,2,1,0:T(8,128)(2,1)S(1)} %pad_maximum_fusion.4), channel_id=1, source_target_pairs={{0,48},{1,49},{4,52},{5,53},{8,56},{9,57},{12,60},{13,61},{64,112}... | collective-permute-start | bytes 884744 | tf_op jit(solution)/shard_map/ppermute | solution.py:285
  15.1 0.1 select_reduce_fusion
  15.2 0.1 collective-permute-start.4
  15.3 4.6 %collective-permute-done.3 = bf16[2,4,2,16,576]{4,3,2,1,0:T(8,128)(2,1)S(1)} collective-permute-done((bf16[2,4,2,16,576]{4,3,2,1,0:T(8,128)(2,1)S(1)}, bf16[2,4,2,16,576]{4,3,2,1,0:T(8,128)(2,1)S(1)}, u32[]{:S(2)}, u32[]{:S(2)}) %collective-permute-start.3) | collective-permute-done | bytes 294944 | tf_op jit(solution)/shard_map/ppermute | solution.py:285
  19.9 0.0 collective-permute-start.7
  19.9 6.2 %collective-permute-done.2 = bf16[2,4,2,16,576]{4,3,2,1,0:T(8,128)(2,1)S(1)} collective-permute-done((bf16[2,4,2,16,576]{4,3,2,1,0:T(8,128)(2,1)S(1)}, bf16[2,4,2,16,576]{4,3,2,1,0:T(8,128)(2,1)S(1)}, u32[]{:S(2)}, u32[]{:S(2)}) %collective-permute-start.2) | collective-permute-done | bytes 294944 | tf_op jit(solution)/shard_map/ppermute | solution.py:285
  26.0 0.0 collective-permute-start.6
  26.0 0.0 collective-permute-done.1
  26.0 0.5 collective-permute-start.5
  26.5 0.1 pad_add_fusion.1.ints
  26.6 0.0 collective-permute-done.4
  26.6 0.0 collective-permute-done.8.refs_10_
  26.6 0.0 copy-start.9
  26.6 0.0 collective-permute-done.7
  26.7 1.0 %collective-permute-done.6 = bf16[2,4,2,16,576]{4,3,2,1,0:T(8,128)(2,1)S(1)} collective-permute-done((bf16[2,4,2,16,576]{4,3,2,1,0:T(8,128)(2,1)S(1)}, bf16[2,4,2,16,576]{4,3,2,1,0:T(8,128)(2,1)S(1)}, u32[]{:S(2)}, u32[]{:S(2)}) %collective-permute-start.6) | collective-permute-done | bytes 294944 | tf_op jit(solution)/shard_map/ppermute | solution.py:270
  27.7 0.5 collective-permute-done.5
  28.2 0.2 copy-done.14
  28.4 0.5 copy-done.15
  28.8 25.6 %shard_map.111 = (bf16[256,512]{1,0:T(8,128)(2,1)S(1)}, bf16[256,768]{1,0:T(8,128)(2,1)}, bf16[256,1280]{1,0:T(8,128)(2,1)}, bf16[256,1024]{1,0:T(8,128)(2,1)}, ...) custom-call(s32[205]{0:T(256)S(1)} %pad_add_fusion.1.ints, ...), custom_call_target="tpu_custom_call" | custom-call | flops 20000000000 | bytes 16777216 | tf_op jit(solution)/shard_map/pallas_call | solution.py:209
  54.5 0.2 collective-permute-start.9
  54.7 0.7 collective-permute-start.14
  55.4 2.3 %collective-permute-done.9 = bf16[32,32,576]{2,1,0:T(8,128)(2,1)S(1)} collective-permute-done((bf16[32,32,576]{2,1,0:T(8,128)(2,1)}, bf16[32,32,576]{2,1,0:T(8,128)(2,1)S(1)}, u32[]{:S(2)}, u32[]{:S(2)}) %collective-permute-start.9) | collective-permute-done | bytes 1179680 | tf_op jit(solution)/shard_map/ppermute | solution.py:270
  57.8 1.5 %add_convert_fusion.3 = (bf16[8,32,576]{2,1,0:T(8,128)(2,1)S(1)}, bf16[8,32,576]{2,1,0:T(8,128)(2,1)S(1)}, bf16[8,32,576]{2,1,0:T(8,128)(2,1)S(1)}) fusion(bf16[32,32,576]{2,1,0:T(8,128)(2,1)S(1)} %collective-permute-done.9, bf16[32,32,576]{2,1,0:T(8,128)(2,1)} %get-tuple-element.17), kind=kLoop, calls=%fused_computation.7 | loop fusion | flops 1769472 | bytes 2654208 | tf_op jit(solution)/shard_map/convert_element_type | solution.py:357
  59.3 2.3 %collective-permute-start.10 = (bf16[8,32,576]{2,1,0:T(8,128)(2,1)S(1)}, bf16[8,32,576]{2,1,0:T(8,128)(2,1)S(1)}, u32[]{:S(2)}, u32[]{:S(2)}) collective-permute-start(bf16[8,32,576]{2,1,0:T(8,128)(2,1)S(1)} %get-tuple-element.28), channel_id=1, source_target_pairs={{0,32},{1,9},{4,36},{5,13},{8,40},{9,1},{12,44},{13,5},{64,96},{65... | collective-permute-start | bytes 884744 | tf_op jit(solution)/shard_map/ppermute | solution.py:285
  61.5 1.6 %collective-permute-start.13 = (bf16[256,1280]{1,0:T(8,128)(2,1)}, bf16[256,1280]{1,0:T(8,128)(2,1)S(1)}, u32[]{:S(2)}, u32[]{:S(2)}) collective-permute-start(bf16[256,1280]{1,0:T(8,128)(2,1)} %get-tuple-element.19), channel_id=1, source_target_pairs={{0,64},{1,65},{4,68},{5,69},{8,72},{9,73},{12,76},{13,77},{64,0},{... | collective-permute-start | bytes 1966088 | tf_op jit(solution)/shard_map/ppermute | solution.py:266
  63.1 1.3 %collective-permute-start.12 = (bf16[8,32,576]{2,1,0:T(8,128)(2,1)S(1)}, bf16[8,32,576]{2,1,0:T(8,128)(2,1)S(1)}, u32[]{:S(2)}, u32[]{:S(2)}) collective-permute-start(bf16[8,32,576]{2,1,0:T(8,128)(2,1)S(1)} %get-tuple-element.29), channel_id=1, source_target_pairs={{0,48},{1,13},{4,52},{5,1},{8,56},{9,5},{12,60},{13,9},{64,112},{6... | collective-permute-start | bytes 884744 | tf_op jit(solution)/shard_map/ppermute | solution.py:285
  64.5 0.7 collective-permute-start.11
  65.2 0.0 collective-permute-done.14
  65.2 3.6 %collective-permute-done.10 = bf16[8,32,576]{2,1,0:T(8,128)(2,1)S(1)} collective-permute-done((bf16[8,32,576]{2,1,0:T(8,128)(2,1)S(1)}, bf16[8,32,576]{2,1,0:T(8,128)(2,1)S(1)}, u32[]{:S(2)}, u32[]{:S(2)}) %collective-permute-start.10) | collective-permute-done | bytes 294944 | tf_op jit(solution)/shard_map/ppermute | solution.py:285
  68.7 0.2 convert_add_fusion
  68.9 0.1 convert_element_type.176
  69.0 1.8 %collective-permute-start.17 = (bf16[64,1024]{1,0:T(8,128)(2,1)S(1)}, bf16[64,1024]{1,0:T(8,128)(2,1)S(1)}, u32[]{:S(2)}, u32[]{:S(2)}) collective-permute-start(bf16[64,1024]{1,0:T(8,128)(2,1)S(1)} %get-tuple-element.37), channel_id=1, source_target_pairs={{0,64},{1,65},{4,68},{5,69},{8,72},{9,73},{12,76},{13,77},{64,0},{... | collective-permute-start | bytes 393224 | tf_op jit(solution)/shard_map/ppermute | solution.py:266
  70.8 1.4 %collective-permute-start.16 = (bf16[64,1024]{1,0:T(8,128)(2,1)S(1)}, bf16[64,1024]{1,0:T(8,128)(2,1)S(1)}, u32[]{:S(2)}, u32[]{:S(2)}) collective-permute-start(bf16[64,1024]{1,0:T(8,128)(2,1)S(1)} %get-tuple-element.38), channel_id=1, source_target_pairs={{0,112},{1,81},{4,116},{5,85},{8,120},{9,89},{12,124},{13,93},{64,... | collective-permute-start | bytes 393224 | tf_op jit(solution)/shard_map/ppermute | solution.py:266
  72.2 0.0 collective-permute-done.12
  72.2 1.6 %collective-permute-start.15 = (bf16[64,1024]{1,0:T(8,128)(2,1)S(1)}, bf16[64,1024]{1,0:T(8,128)(2,1)S(1)}, u32[]{:S(2)}, u32[]{:S(2)}) collective-permute-start(bf16[64,1024]{1,0:T(8,128)(2,1)S(1)} %get-tuple-element.39), channel_id=1, source_target_pairs={{0,48},{1,17},{4,52},{5,21},{8,56},{9,25},{12,60},{13,29},{64,112}... | collective-permute-start | bytes 393224 | tf_op jit(solution)/shard_map/ppermute | solution.py:266
  73.8 0.0 collective-permute-done.11
  73.8 1.9 %add_convert_fusion = bf16[8,32,576]{2,1,0:T(8,128)(2,1)} fusion(bf16[8,32,576]{2,1,0:T(8,128)(2,1)S(1)} %collective-permute-done.12, bf16[8,32,576]{2,1,0:T(8,128)(2,1)S(1)} %collective-permute-done.11, bf16[8,32,576]{2,1,0:T(8,128)(2,1)S(1)} %collective-permute-done.10, bf16[32,32,576]{2,1,0:T(8,128)(2,1)S(1)} %collective-permute-done.9, ...), kind=kLoop, calls=%fused_computation.4 | loop fusion | flops 1474560 | bytes 1769472 | tf_op jit(solution)/shard_map/convert_element_type | solution.py:366
  75.7 8.3 %all-to-all-start = ((bf16[16,16,576]{2,1,0:T(8,128)(2,1)}), bf16[16,16,576]{2,1,0:T(8,128)(2,1)S(1)}, u32[]{:S(2)}, u32[]{:S(2)}) async-start(bf16[16,16,576]{2,1,0:T(8,128)(2,1)} %bitcast.17), calls=%async_computation | async-start | bytes 655360 | tf_op jit(solution)/shard_map/all_to_all | solution.py:296
  84.0 0.0 collective-permute-done.13
  84.0 0.5 collective-permute-done.17
  84.5 0.0 collective-permute-done.16
  84.5 0.0 collective-permute-done.15
  84.5 0.1 broadcast_select_fusion.1
  84.6 0.1 fusion.2
  84.7 0.8 pad_maximum_fusion.3
  85.5 0.9 pad_maximum_fusion.2
  86.4 0.9 pad_maximum_fusion
  87.3 5.4 %all-to-all-done = bf16[16,16,576]{2,1,0:T(8,128)(2,1)S(1)} async-done(((bf16[16,16,576]{2,1,0:T(8,128)(2,1)}), bf16[16,16,576]{2,1,0:T(8,128)(2,1)S(1)}, u32[]{:S(2)}, u32[]{:S(2)}) %all-to-all-start) | async-done | bytes 294944 | tf_op jit(solution)/shard_map/all_to_all | solution.py:296
  92.7 0.7 convert_add_fusion.2
  (35 shorter events, 0.4 us)
Async XLA Ops:
  0.6 3.1 %copy-start.1 = (bf16[256,1536]{1,0:T(8,128)(2,1)S(1)}, bf16[256,1536]{1,0:T(8,128)(2,1)}, u32[]{:S(2)}) copy-start(bf16[256,1536]{1,0:T(8,128)(2,1)} %refs_8_.1) | copy-start | bytes 2359300
  0.6 3.1 %copy-start.5 = (f32[256]{0:T(256)S(1)}, f32[256]{0:T(256)}, u32[]{:S(2)}) copy-start(f32[256]{0:T(256)} %param.14) | copy-start | bytes 3076
  0.7 3.1 %copy-start.6 = (f32[256]{0:T(256)S(1)}, f32[256]{0:T(256)}, u32[]{:S(2)}) copy-start(f32[256]{0:T(256)} %param.13) | copy-start | bytes 3076
  0.7 3.1 %copy-start.7 = (f32[256]{0:T(256)S(1)}, f32[256]{0:T(256)}, u32[]{:S(2)}) copy-start(f32[256]{0:T(256)} %param.12) | copy-start | bytes 3076
  0.7 3.2 %copy-start.2 = (bf16[256,1024]{1,0:T(8,128)(2,1)S(1)}, bf16[256,1024]{1,0:T(8,128)(2,1)}, u32[]{:S(2)}) copy-start(bf16[256,1024]{1,0:T(8,128)(2,1)} %param.11) | copy-start | bytes 1572868
  2.0 7.2 %collective-permute-start = (bf16[4,2,16,576]{3,2,1,0:T(8,128)(2,1)S(1)}, bf16[4,2,16,576]{3,2,1,0:T(8,128)(2,1)S(1)}, u32[]{:S(2)}, u32[]{:S(2)}) collective-permute-start(bf16[4,2,16,576]{3,2,1,0:T(8,128)(2,1)S(1)} %get-tuple-element.41), channel_id=1, source_target_pairs={{0,64},{1,65},{4,68},{5,69},{8,72},{9,73},{12,76},{13,77},{64,0},{... | collective-permute-start | bytes 442376 | tf_op jit(solution)/shard_map/ppermute | solution.py:266
  4.0 5.2 %copy-start = (bf16[256,1024]{1,0:T(8,128)(2,1)}, bf16[256,1024]{1,0:T(8,128)(2,1)S(1)}, u32[]{:S(2)}) copy-start(bf16[256,1024]{1,0:T(8,128)(2,1)S(1)} %multiply_convert_fusion.refs_9_) | copy-start | bytes 1572868
  4.0 11.1 %copy-start.8 = (s32[16]{0:T(128)S(1)}, s32[16]{0:T(128)}, u32[]{:S(2)}) copy-start(s32[16]{0:T(128)} %param.15) | copy-start | bytes 196
  4.1 22.5 %collective-permute-start.8 = (bf16[256,1280]{1,0:T(8,128)(2,1)S(1)}, bf16[256,1280]{1,0:T(8,128)(2,1)S(1)}, u32[]{:S(2)}, u32[]{:S(2)}) collective-permute-start(bf16[256,1280]{1,0:T(8,128)(2,1)S(1)} %pad_maximum_fusion.1), channel_id=1, source_target_pairs={{0,64},{1,65},{4,68},{5,69},{8,72},{9,73},{12,76},{13,77},{64,0},{... | collective-permute-start | bytes 1966088 | tf_op jit(solution)/shard_map/ppermute | solution.py:266
  9.2 10.6 %collective-permute-start.3 = (bf16[2,4,2,16,576]{4,3,2,1,0:T(8,128)(2,1)S(1)}, bf16[2,4,2,16,576]{4,3,2,1,0:T(8,128)(2,1)S(1)}, u32[]{:S(2)}, u32[]{:S(2)}) collective-permute-start(bf16[2,4,2,16,576]{4,3,2,1,0:T(8,128)(2,1)S(1)} %pad_maximum_fusion.4), channel_id=1, source_target_pairs={{0,16},{1,17},{4,20},{5,21},{8,24},{9,25},{12,28},{13,29},{64,80},... | collective-permute-start | bytes 884744 | tf_op jit(solution)/shard_map/ppermute | solution.py:285
  10.9 15.2 %collective-permute-start.2 = (bf16[2,4,2,16,576]{4,3,2,1,0:T(8,128)(2,1)S(1)}, bf16[2,4,2,16,576]{4,3,2,1,0:T(8,128)(2,1)S(1)}, u32[]{:S(2)}, u32[]{:S(2)}) collective-permute-start(bf16[2,4,2,16,576]{4,3,2,1,0:T(8,128)(2,1)S(1)} %pad_maximum_fusion.4), channel_id=1, source_target_pairs={{0,32},{1,33},{4,36},{5,37},{8,40},{9,41},{12,44},{13,45},{64,96},... | collective-permute-start | bytes 884744 | tf_op jit(solution)/shard_map/ppermute | solution.py:285
  13.6 12.4 %collective-permute-start.1 = (bf16[2,4,2,16,576]{4,3,2,1,0:T(8,128)(2,1)S(1)}, bf16[2,4,2,16,576]{4,3,2,1,0:T(8,128)(2,1)S(1)}, u32[]{:S(2)}, u32[]{:S(2)}) collective-permute-start(bf16[2,4,2,16,576]{4,3,2,1,0:T(8,128)(2,1)S(1)} %pad_maximum_fusion.4), channel_id=1, source_target_pairs={{0,48},{1,49},{4,52},{5,53},{8,56},{9,57},{12,60},{13,61},{64,112}... | collective-permute-start | bytes 884744 | tf_op jit(solution)/shard_map/ppermute | solution.py:285
  15.2 11.5 %collective-permute-start.4 = (bf16[2,4,2,16,576]{4,3,2,1,0:T(8,128)(2,1)S(1)}, bf16[2,4,2,16,576]{4,3,2,1,0:T(8,128)(2,1)S(1)}, u32[]{:S(2)}, u32[]{:S(2)}) collective-permute-start(bf16[2,4,2,16,576]{4,3,2,1,0:T(8,128)(2,1)S(1)} %pad_maximum_fusion.4), channel_id=1, source_target_pairs={{0,1},{1,0},{2,3},{3,2},{4,5},{5,4},{6,7},{7,6},{8,9},{9,8},{10,11... | collective-permute-start | bytes 884744 | tf_op jit(solution)/shard_map/ppermute | solution.py:270
  19.9 8.3 %copy-start.10 = (bf16[2,4,2,16,576]{4,3,2,1,0:T(8,128)(2,1)}, bf16[2,4,2,16,576]{4,3,2,1,0:T(8,128)(2,1)S(1)}, u32[]{:S(2)}) copy-start(bf16[2,4,2,16,576]{4,3,2,1,0:T(8,128)(2,1)S(1)} %collective-permute-done.3) | copy-start | bytes 884740
  19.9 6.8 %collective-permute-start.7 = (bf16[2,4,2,16,576]{4,3,2,1,0:T(8,128)(2,1)S(1)}, bf16[2,4,2,16,576]{4,3,2,1,0:T(8,128)(2,1)S(1)}, u32[]{:S(2)}, u32[]{:S(2)}) collective-permute-start(bf16[2,4,2,16,576]{4,3,2,1,0:T(8,128)(2,1)S(1)} %collective-permute-done.3), channel_id=1, source_target_pairs={{0,1},{1,0},{2,3},{3,2},{4,5},{5,4},{6,7},{7,6},{8,9},{9,8},{10,11... | collective-permute-start | bytes 884744 | tf_op jit(solution)/shard_map/ppermute | solution.py:270
  26.0 2.1 %copy-start.11 = (bf16[2,4,2,16,576]{4,3,2,1,0:T(8,128)(2,1)}, bf16[2,4,2,16,576]{4,3,2,1,0:T(8,128)(2,1)S(1)}, u32[]{:S(2)}) copy-start(bf16[2,4,2,16,576]{4,3,2,1,0:T(8,128)(2,1)S(1)} %collective-permute-done.2) | copy-start | bytes 884740
  26.0 1.6 %collective-permute-start.6 = (bf16[2,4,2,16,576]{4,3,2,1,0:T(8,128)(2,1)S(1)}, bf16[2,4,2,16,576]{4,3,2,1,0:T(8,128)(2,1)S(1)}, u32[]{:S(2)}, u32[]{:S(2)}) collective-permute-start(bf16[2,4,2,16,576]{4,3,2,1,0:T(8,128)(2,1)S(1)} %collective-permute-done.2), channel_id=1, source_target_pairs={{0,1},{1,0},{2,3},{3,2},{4,5},{5,4},{6,7},{7,6},{8,9},{9,8},{10,11... | collective-permute-start | bytes 884744 | tf_op jit(solution)/shard_map/ppermute | solution.py:270
  26.0 2.1 %collective-permute-start.5 = (bf16[2,4,2,16,576]{4,3,2,1,0:T(8,128)(2,1)S(1)}, bf16[2,4,2,16,576]{4,3,2,1,0:T(8,128)(2,1)S(1)}, u32[]{:S(2)}, u32[]{:S(2)}) collective-permute-start(bf16[2,4,2,16,576]{4,3,2,1,0:T(8,128)(2,1)S(1)} %collective-permute-done.1), channel_id=1, source_target_pairs={{0,1},{1,0},{2,3},{3,2},{4,5},{5,4},{6,7},{7,6},{8,9},{9,8},{10,11... | collective-permute-start | bytes 884744 | tf_op jit(solution)/shard_map/ppermute | solution.py:270
  26.6 1.5 %copy-start.12 = (bf16[2,4,2,16,576]{4,3,2,1,0:T(8,128)(2,1)}, bf16[2,4,2,16,576]{4,3,2,1,0:T(8,128)(2,1)S(1)}, u32[]{:S(2)}) copy-start(bf16[2,4,2,16,576]{4,3,2,1,0:T(8,128)(2,1)S(1)} %collective-permute-done.4) | copy-start | bytes 884740
  26.6 1.5 %copy-start.9 = (bf16[256,1280]{1,0:T(8,128)(2,1)}, bf16[256,1280]{1,0:T(8,128)(2,1)S(1)}, u32[]{:S(2)}) copy-start(bf16[256,1280]{1,0:T(8,128)(2,1)S(1)} %collective-permute-done.8.refs_10_) | copy-start | bytes 1966084
  26.7 1.5 %copy-start.13 = (bf16[2,4,2,16,576]{4,3,2,1,0:T(8,128)(2,1)}, bf16[2,4,2,16,576]{4,3,2,1,0:T(8,128)(2,1)S(1)}, u32[]{:S(2)}) copy-start(bf16[2,4,2,16,576]{4,3,2,1,0:T(8,128)(2,1)S(1)} %collective-permute-done.7) | copy-start | bytes 884740
  27.7 0.7 copy-start.14
  28.1 0.7 copy-start.15
  54.5 3.3 %collective-permute-start.9 = (bf16[32,32,576]{2,1,0:T(8,128)(2,1)}, bf16[32,32,576]{2,1,0:T(8,128)(2,1)S(1)}, u32[]{:S(2)}, u32[]{:S(2)}) collective-permute-start(bf16[32,32,576]{2,1,0:T(8,128)(2,1)} %get-tuple-element.18), channel_id=1, source_target_pairs={{0,1},{1,0},{2,3},{3,2},{4,5},{5,4},{6,7},{7,6},{8,9},{9,8},{10,11... | collective-permute-start | bytes 3538952 | tf_op jit(solution)/shard_map/ppermute | solution.py:270
  54.7 10.5 %collective-permute-start.14 = (bf16[256,1024]{1,0:T(8,128)(2,1)}, bf16[256,1024]{1,0:T(8,128)(2,1)S(1)}, u32[]{:S(2)}, u32[]{:S(2)}) collective-permute-start(bf16[256,1024]{1,0:T(8,128)(2,1)} %get-tuple-element.21), channel_id=1, source_target_pairs={{0,16},{1,49},{4,20},{5,53},{8,24},{9,57},{12,28},{13,61},{64,80},... | collective-permute-start | bytes 1572872 | tf_op jit(solution)/shard_map/ppermute | solution.py:266
  57.8 10.9 %copy-start.3 = (bf16[256,1024]{1,0:T(8,128)(2,1)S(1)}, bf16[256,1024]{1,0:T(8,128)(2,1)}, u32[]{:S(2)}) copy-start(bf16[256,1024]{1,0:T(8,128)(2,1)} %get-tuple-element.20) | copy-start | bytes 1572868
  59.3 9.4 %collective-permute-start.10 = (bf16[8,32,576]{2,1,0:T(8,128)(2,1)S(1)}, bf16[8,32,576]{2,1,0:T(8,128)(2,1)S(1)}, u32[]{:S(2)}, u32[]{:S(2)}) collective-permute-start(bf16[8,32,576]{2,1,0:T(8,128)(2,1)S(1)} %get-tuple-element.28), channel_id=1, source_target_pairs={{0,32},{1,9},{4,36},{5,13},{8,40},{9,1},{12,44},{13,5},{64,96},{65... | collective-permute-start | bytes 884744 | tf_op jit(solution)/shard_map/ppermute | solution.py:285
  61.5 22.4 %collective-permute-start.13 = (bf16[256,1280]{1,0:T(8,128)(2,1)}, bf16[256,1280]{1,0:T(8,128)(2,1)S(1)}, u32[]{:S(2)}, u32[]{:S(2)}) collective-permute-start(bf16[256,1280]{1,0:T(8,128)(2,1)} %get-tuple-element.19), channel_id=1, source_target_pairs={{0,64},{1,65},{4,68},{5,69},{8,72},{9,73},{12,76},{13,77},{64,0},{... | collective-permute-start | bytes 1966088 | tf_op jit(solution)/shard_map/ppermute | solution.py:266
  63.1 9.1 %collective-permute-start.12 = (bf16[8,32,576]{2,1,0:T(8,128)(2,1)S(1)}, bf16[8,32,576]{2,1,0:T(8,128)(2,1)S(1)}, u32[]{:S(2)}, u32[]{:S(2)}) collective-permute-start(bf16[8,32,576]{2,1,0:T(8,128)(2,1)S(1)} %get-tuple-element.29), channel_id=1, source_target_pairs={{0,48},{1,13},{4,52},{5,1},{8,56},{9,5},{12,60},{13,9},{64,112},{6... | collective-permute-start | bytes 884744 | tf_op jit(solution)/shard_map/ppermute | solution.py:285
  64.5 9.3 %collective-permute-start.11 = (bf16[8,32,576]{2,1,0:T(8,128)(2,1)S(1)}, bf16[8,32,576]{2,1,0:T(8,128)(2,1)S(1)}, u32[]{:S(2)}, u32[]{:S(2)}) collective-permute-start(bf16[8,32,576]{2,1,0:T(8,128)(2,1)S(1)} %get-tuple-element.30), channel_id=1, source_target_pairs={{0,16},{1,5},{4,20},{5,9},{8,24},{9,13},{12,28},{13,1},{64,80},{65... | collective-permute-start | bytes 884744 | tf_op jit(solution)/shard_map/ppermute | solution.py:285
  69.0 15.5 %collective-permute-start.17 = (bf16[64,1024]{1,0:T(8,128)(2,1)S(1)}, bf16[64,1024]{1,0:T(8,128)(2,1)S(1)}, u32[]{:S(2)}, u32[]{:S(2)}) collective-permute-start(bf16[64,1024]{1,0:T(8,128)(2,1)S(1)} %get-tuple-element.37), channel_id=1, source_target_pairs={{0,64},{1,65},{4,68},{5,69},{8,72},{9,73},{12,76},{13,77},{64,0},{... | collective-permute-start | bytes 393224 | tf_op jit(solution)/shard_map/ppermute | solution.py:266
  70.8 13.6 %collective-permute-start.16 = (bf16[64,1024]{1,0:T(8,128)(2,1)S(1)}, bf16[64,1024]{1,0:T(8,128)(2,1)S(1)}, u32[]{:S(2)}, u32[]{:S(2)}) collective-permute-start(bf16[64,1024]{1,0:T(8,128)(2,1)S(1)} %get-tuple-element.38), channel_id=1, source_target_pairs={{0,112},{1,81},{4,116},{5,85},{8,120},{9,89},{12,124},{13,93},{64,... | collective-permute-start | bytes 393224 | tf_op jit(solution)/shard_map/ppermute | solution.py:266
  72.2 12.3 %collective-permute-start.15 = (bf16[64,1024]{1,0:T(8,128)(2,1)S(1)}, bf16[64,1024]{1,0:T(8,128)(2,1)S(1)}, u32[]{:S(2)}, u32[]{:S(2)}) collective-permute-start(bf16[64,1024]{1,0:T(8,128)(2,1)S(1)} %get-tuple-element.39), channel_id=1, source_target_pairs={{0,48},{1,17},{4,52},{5,21},{8,56},{9,25},{12,60},{13,29},{64,112}... | collective-permute-start | bytes 393224 | tf_op jit(solution)/shard_map/ppermute | solution.py:266
  75.7 8.8 %copy-start.4 = (bf16[256,768]{1,0:T(8,128)(2,1)S(1)}, bf16[256,768]{1,0:T(8,128)(2,1)}, u32[]{:S(2)}) copy-start(bf16[256,768]{1,0:T(8,128)(2,1)} %get-tuple-element.24) | copy-start | bytes 1179652
  75.7 17.0 %all-to-all-start = ((bf16[16,16,576]{2,1,0:T(8,128)(2,1)}), bf16[16,16,576]{2,1,0:T(8,128)(2,1)S(1)}, u32[]{:S(2)}, u32[]{:S(2)}) async-start(bf16[16,16,576]{2,1,0:T(8,128)(2,1)} %bitcast.17), calls=%async_computation | async-start | bytes 655360 | tf_op jit(solution)/shard_map/all_to_all | solution.py:296

commit v7 on v6

--- a/solution.py
+++ b/solution.py
@@ -34,12 +34,14 @@
     return lax.dot_general(a, b, (((0,), (0,)), ((), ())), preferred_element_type=F32)
 
 
-def prepare(ints, lat, lat_t, bias, keys):
-    for hh in range(4):
-        keys[hh, :, NOPE:] = lat[:, KV_RANK:]
-    for block in range(8):
-        start = pl.multiple_of(ints[AT_WEIGHT + block], 64)
-        lat_t[pl.ds(start, 64), :] = lat[:, block * 64 : block * 64 + 64].T
+def prepare(ints, pieces, lat_t, bias, keys):
+    for i, piece in enumerate(pieces):
+        rows = slice(i * 256, i * 256 + 256)
+        for hh in range(4):
+            keys[hh, rows, NOPE:] = piece[:, KV_RANK:]
+        for block in range(8):
+            start = pl.multiple_of(ints[AT_WEIGHT + block], 64)
+            lat_t[pl.ds(start, 64), rows] = piece[:, block * 64 : block * 64 + 64].T
     lane = lax.broadcasted_iota(jnp.int32, (16, ROWS), 1)
     query_pos = lane % 128 - lax.broadcasted_iota(jnp.int32, (16, ROWS), 0)
     for group in range(4):
@@ -49,10 +51,9 @@
 
 
 def body(ints, *refs):
-    pieces, (q_hbm, g_hbm, far_hbm, w_hbm) = refs[:8], refs[8:12]
-    out_hbm, dq_hbm, far_out_hbm, wg_keep_hbm, wg_send_hbm, keep_hbm, send_hbm = refs[12:19]
-    lat, q, g, far, w, lat_t, bias, keys, vals, scores, exps, dscores, dkv, rope = refs[19:33]
-    out_b, dq_b, far_out, wg_b, keep, send, sems = refs[33:]
+    pieces, (q_hbm, g_hbm, far, w_hbm) = refs[:8], refs[8:12]
+    out_b, dq_b, far_out, wg_keep, wg_send, keep, send = refs[12:19]
+    q, g, w, lat_t, bias, keys, vals, scores, exps, dscores, dkv, rope, sems = refs[19:]
     used = []
 
     def copy(source, target):
@@ -63,15 +64,13 @@
 
     y_lo = ints[AT_YLO]
     loads = [copy(w_hbm.at[:, pl.ds(pl.multiple_of(y_lo * 1024, 1024), 1024)], w)]
-    loads += [copy(piece, lat.at[pl.ds(i * 256, 256), :]) for i, piece in enumerate(pieces)]
     loads += [
         copy(q_hbm.at[:, pl.ds(pl.multiple_of(y_lo * 768, 256), 768)], q),
         copy(g_hbm.at[:, pl.ds(pl.multiple_of(y_lo * 512, 512), 512)], g),
-        copy(far_hbm, far),
     ]
     for load in loads:
         load.wait()
-    prepare(ints, lat, lat_t, bias, keys)
+    prepare(ints, pieces, lat_t, bias, keys)
 
     chunks = [pl.ds(c * CHUNK, CHUNK) for c in range(KEYS // CHUNK)]
     q_t = jnp.concatenate([q[...].T, far[:, : 4 * QK].T], axis=1)
@@ -81,7 +80,9 @@
     top, norm, out, inverse, delta, q_s, g_s, dq = ([None] * 4 for _ in range(8))
 
     def project(pair, r):
-        kv = mm(lat[r, :KV_RANK], w[:, pair * 512 : pair * 512 + 512]).astype(BF)
+        first = r.start // 256
+        lat = [piece[:, :KV_RANK] for piece in pieces[first : first + CHUNK // 256]]
+        kv = mm(jnp.concatenate(lat, axis=0), w[:, pair * 512 : pair * 512 + 512]).astype(BF)
         for hh in range(2):
             keys[pair * 2 + hh, r, :NOPE] = kv[:, hh * 256 : hh * 256 + NOPE]
             vals[pair * 2 + hh, r, :] = kv[:, hh * 256 + NOPE : hh * 256 + 256]
@@ -134,17 +135,14 @@
         value = jnp.concatenate(out[pair * 2 : pair * 2 + 2], axis=0).T.astype(BF)
         out_b[:, columns] = value[:256]
         far_out[:, 768 + pair * 256 : 1024 + pair * 256] = value[256:]
-        copy(out_b.at[:, columns], out_hbm.at[:, columns])
         columns = slice(pair * 384, pair * 384 + 384)
         value = jnp.concatenate(dq[pair * 2 : pair * 2 + 2], axis=0).T.astype(BF)
         dq_b[:, columns] = value[:256]
         far_out[:, columns] = value[256:]
-        copy(dq_b.at[:, columns], dq_hbm.at[:, columns])
         columns = slice(pair * 512, pair * 512 + 512)
         wg = mm(lat_t[...], dkv[:, columns]).astype(BF)
-        for k, target in enumerate((wg_keep_hbm, wg_send_hbm)):
-            wg_b[k, :, columns] = wg[k * 256 : k * 256 + 256]
-            copy(wg_b.at[k, :, columns], target.at[:, columns])
+        wg_keep[:, columns] = wg[:256]
+        wg_send[:, columns] = wg[256:]
 
     def latent_terms(c):
         terms = mm_last(dkv[chunks[c], :], w[...]).astype(BF)
@@ -191,14 +189,8 @@
     for c in order:
         back(3, chunks[c])
         latent_terms(c)
-        if c == len(chunks) - 1:
-            copy(send, send_hbm)
-    copy(keep, keep_hbm)
     query_grad(3)
     finish(1)
-    copy(far_out, far_out_hbm)
-    for store in used[len(loads) :]:
-        store.wait()
 
 
 def attention(ints, pieces, queries, out_grad, far, up_weight):
@@ -206,10 +198,13 @@
         return jax.ShapeDtypeStruct(dims, BF)
 
     anywhere = pl.BlockSpec(memory_space=pl.ANY)
+    inside = pl.BlockSpec(memory_space=pltpu.VMEM)
     return pl.pallas_call(
         body,
-        in_specs=[pl.BlockSpec(memory_space=pltpu.SMEM)] + [anywhere] * 12,
-        out_specs=[anywhere] * 7,
+        in_specs=[pl.BlockSpec(memory_space=pltpu.SMEM)]
+        + [inside] * 8
+        + [anywhere, anywhere, inside, anywhere],
+        out_specs=[inside] * 7,
         out_shape=[
             shape(256, 4 * VDIM),
             shape(256, 4 * QK),
@@ -220,10 +215,8 @@
             shape(32, 32, LAT),
         ],
         scratch_shapes=[
-            pltpu.VMEM((KEYS, LAT), BF),
             pltpu.VMEM((256, 4 * QK), BF),
             pltpu.VMEM((256, 4 * VDIM), BF),
-            pltpu.VMEM((256, 4 * (QK + VDIM)), BF),
             pltpu.VMEM((KV_RANK, 1024), BF),
             pltpu.VMEM((KV_RANK, KEYS), BF),
             pltpu.VMEM((KEYS, ROWS), F32),
@@ -234,15 +227,9 @@
             pltpu.VMEM((2, KEYS, ROWS), BF),
             pltpu.VMEM((KEYS, 1024), BF),
             pltpu.VMEM((KEYS, QK - NOPE), F32),
-            pltpu.VMEM((256, 4 * VDIM), BF),
-            pltpu.VMEM((256, 4 * QK), BF),
-            pltpu.VMEM((256, 4 * (QK + VDIM)), BF),
-            pltpu.VMEM((2, 256, 1024), BF),
-            pltpu.VMEM((32, 32, LAT), BF),
-            pltpu.VMEM((32, 32, LAT), BF),
-            pltpu.SemaphoreType.DMA((32,)),
+            pltpu.SemaphoreType.DMA((3,)),
         ],
-        compiler_params=pltpu.CompilerParams(vmem_limit_bytes=53 * 2**20),
+        compiler_params=pltpu.CompilerParams(vmem_limit_bytes=46 * 2**20),
         cost_estimate=pl.CostEstimate(
             flops=20 * 10**9, bytes_accessed=16 * 2**20, transcendentals=2**22
         ),

time: 93.6 us -> 90.8 us (0.970)
    select_n x3, other arithmetic: 0.17 us -> 2.12 us  [halves(): jnp.where(y_lo == 0, near, far)]
    all_to_all x1, waiting for transfers between devices: 5.36 us -> 3.45 us  [exchange_rest(): lax.all_to_all(value, AXES, 0, 0, tiled=True, axis_index_groups=groups)]
    convert_element_type x1, other arithmetic: 1.48 us -> 0.26 us  [reduce_terms(): terms = [shift(wire[k].astype(BF), (k, 0), (0, k)) for k in (2, 1, 3)]]
    ppermute x6, waiting for transfers between devices: 14.3 us -> 15.4 us  [shift(): return lax.ppermute(value, AXES, pairs)]
    convert_element_type x1, other arithmetic: 1.9 us -> 0.95 us  [reduce_terms(): part = sum_terms(wire[0], terms).astype(BF)]
    unnamed x33 -> x13, local copies, waits for them, and re-layouts: 2.01 us -> 1.28 us
where the time goes in v7:
time: 90.8 us; the launch traced here: 90.5 us
  starting transfers between devices  28.4 us (31%)
  waiting for transfers between devices  27.7 us (31%)
  Pallas kernels  24.7 us (27%)
  other arithmetic  7.47 us (8%)
  local copies, waits for them, and re-layouts  1.31 us (1%)
  between operations  0.91 us (1%)
    pallas_call x1, Pallas kernels, attention(): pl.pallas_call(body, in_specs=[pl.BlockSpec(memory_space=pltpu.SMEM)] + [...  24.7 us
    ppermute x6, waiting for transfers between devices, shift(): return lax.ppermute(value, AXES, pairs)  15.4 us
    ppermute x6, starting transfers between devices, shift(): return lax.ppermute(value, AXES, pairs)  10.1 us
    ppermute x7, starting transfers between devices, trade(): return lax.ppermute(value, AXES, pairs)  9.31 us
    all_to_all x1, starting transfers between devices, exchange_rest(): lax.all_to_all(value, AXES, 0, 0, tiled=True, axis_index_groups=groups)  8.21 us
    ppermute x7, waiting for transfers between devices, trade(): return lax.ppermute(value, AXES, pairs)  5.01 us
    ppermute x5, waiting for transfers between devices, swap_cores(): return lax.ppermute(value, 'head', [(i, i ^ 1) for i in range(16)])  3.82 us
    all_to_all x1, waiting for transfers between devices, exchange_rest(): lax.all_to_all(value, AXES, 0, 0, tiled=True, axis_index_groups=groups)  3.45 us
  transfers between devices with their start and end apart: 19, of which 9 were waited for; matrix products, arithmetic and copies ran while one was open for 8% of the time, Pallas kernels for 0%

profile of v7, /device:TPU:0, one launch (start us, length us, event | category | flops | bytes accessed | tf_op | source)
XLA Modules:
  0.0 90.5 jit_solution(7955584045021123698)
XLA Ops:
  0.6 0.0 copy-start
  0.6 0.0 copy-start.2
  0.7 0.0 copy-start.3
  0.7 0.0 copy-start.4
  0.7 0.0 copy-start.1
  0.7 1.3 %copy.15 = bf16[256,576]{1,0:T(8,128)(2,1)S(1)} copy(bf16[256,576]{0,1:T(8,128)(2,1)} %param.8) | data formatting | bytes 589824 | tf_op args[0]
  2.0 1.7 %collective-permute-start = (bf16[4,2,16,576]{3,2,1,0:T(8,128)(2,1)S(1)}, bf16[4,2,16,576]{3,2,1,0:T(8,128)(2,1)S(1)}, u32[]{:S(2)}, u32[]{:S(2)}) collective-permute-start(bf16[4,2,16,576]{3,2,1,0:T(8,128)(2,1)S(1)} %get-tuple-element.41), channel_id=1, source_target_pairs={{0,64},{1,65},{4,68},{5,69},{8,72},{9,73},{12,76},{13,77},{64,0},{... | collective-permute-start | bytes 442376 | tf_op jit(solution)/shard_map/ppermute | solution.py:253
  3.8 0.0 copy-done.2
  3.8 0.0 copy-done.3
  3.8 0.0 copy-done.4
  3.8 0.2 multiply_convert_fusion.refs_9_
  4.0 0.0 copy-start.5
  4.1 0.4 collective-permute-start.8
  4.6 4.5 %collective-permute-done = bf16[4,2,16,576]{3,2,1,0:T(8,128)(2,1)S(1)} collective-permute-done((bf16[4,2,16,576]{3,2,1,0:T(8,128)(2,1)S(1)}, bf16[4,2,16,576]{3,2,1,0:T(8,128)(2,1)S(1)}, u32[]{:S(2)}, u32[]{:S(2)}) %collective-permute-start) | collective-permute-done | bytes 147488 | tf_op jit(solution)/shard_map/ppermute | solution.py:253
  9.2 1.6 %collective-permute-start.3 = (bf16[2,4,2,16,576]{4,3,2,1,0:T(8,128)(2,1)S(1)}, bf16[2,4,2,16,576]{4,3,2,1,0:T(8,128)(2,1)S(1)}, u32[]{:S(2)}, u32[]{:S(2)}) collective-permute-start(bf16[2,4,2,16,576]{4,3,2,1,0:T(8,128)(2,1)S(1)} %pad_maximum_fusion.4), channel_id=1, source_target_pairs={{0,16},{1,17},{4,20},{5,21},{8,24},{9,25},{12,28},{13,29},{64,80},... | collective-permute-start | bytes 884744 | tf_op jit(solution)/shard_map/ppermute | solution.py:272
  10.9 2.7 %collective-permute-start.2 = (bf16[2,4,2,16,576]{4,3,2,1,0:T(8,128)(2,1)S(1)}, bf16[2,4,2,16,576]{4,3,2,1,0:T(8,128)(2,1)S(1)}, u32[]{:S(2)}, u32[]{:S(2)}) collective-permute-start(bf16[2,4,2,16,576]{4,3,2,1,0:T(8,128)(2,1)S(1)} %pad_maximum_fusion.4), channel_id=1, source_target_pairs={{0,32},{1,33},{4,36},{5,37},{8,40},{9,41},{12,44},{13,45},{64,96},... | collective-permute-start | bytes 884744 | tf_op jit(solution)/shard_map/ppermute | solution.py:272
  13.6 1.4 %collective-permute-start.1 = (bf16[2,4,2,16,576]{4,3,2,1,0:T(8,128)(2,1)S(1)}, bf16[2,4,2,16,576]{4,3,2,1,0:T(8,128)(2,1)S(1)}, u32[]{:S(2)}, u32[]{:S(2)}) collective-permute-start(bf16[2,4,2,16,576]{4,3,2,1,0:T(8,128)(2,1)S(1)} %pad_maximum_fusion.4), channel_id=1, source_target_pairs={{0,48},{1,49},{4,52},{5,53},{8,56},{9,57},{12,60},{13,61},{64,112}... | collective-permute-start | bytes 884744 | tf_op jit(solution)/shard_map/ppermute | solution.py:272
  15.1 0.0 copy-done.5
  15.1 0.1 select_reduce_fusion
  15.2 0.1 collective-permute-start.4
  15.2 4.6 %collective-permute-done.3 = bf16[2,4,2,16,576]{4,3,2,1,0:T(8,128)(2,1)S(1)} collective-permute-done((bf16[2,4,2,16,576]{4,3,2,1,0:T(8,128)(2,1)S(1)}, bf16[2,4,2,16,576]{4,3,2,1,0:T(8,128)(2,1)S(1)}, u32[]{:S(2)}, u32[]{:S(2)}) %collective-permute-start.3) | collective-permute-done | bytes 294944 | tf_op jit(solution)/shard_map/ppermute | solution.py:272
  19.8 0.0 collective-permute-start.7
  19.9 6.2 %collective-permute-done.2 = bf16[2,4,2,16,576]{4,3,2,1,0:T(8,128)(2,1)S(1)} collective-permute-done((bf16[2,4,2,16,576]{4,3,2,1,0:T(8,128)(2,1)S(1)}, bf16[2,4,2,16,576]{4,3,2,1,0:T(8,128)(2,1)S(1)}, u32[]{:S(2)}, u32[]{:S(2)}) %collective-permute-start.2) | collective-permute-done | bytes 294944 | tf_op jit(solution)/shard_map/ppermute | solution.py:272
  26.0 0.0 collective-permute-start.6
  26.0 0.0 collective-permute-done.1
  26.0 0.5 collective-permute-start.5
  26.5 0.1 pad_add_fusion.1.ints
  26.6 0.0 collective-permute-done.4
  26.6 0.0 collective-permute-done.8.refs_10_
  26.6 0.0 collective-permute-done.7
  26.6 1.0 %collective-permute-done.6 = bf16[2,4,2,16,576]{4,3,2,1,0:T(8,128)(2,1)S(1)} collective-permute-done((bf16[2,4,2,16,576]{4,3,2,1,0:T(8,128)(2,1)S(1)}, bf16[2,4,2,16,576]{4,3,2,1,0:T(8,128)(2,1)S(1)}, u32[]{:S(2)}, u32[]{:S(2)}) %collective-permute-start.6) | collective-permute-done | bytes 294944 | tf_op jit(solution)/shard_map/ppermute | solution.py:257
  27.6 0.5 collective-permute-done.5
  28.1 24.7 %shard_map.111 = (bf16[256,512]{1,0:T(8,128)(2,1)S(1)}, bf16[256,768]{1,0:T(8,128)(2,1)S(1)}, bf16[256,1280]{1,0:T(8,128)(2,1)S(1)}, bf16[256,1024]{1,0:T(8,128)...) custom-call(s32[205]{0:T(256)S(1)} %pad_add_fusion.1.ints, ...), custom_call_target="tpu_custom_call" | custom-call | flops 20000000000 | bytes 16777216 | tf_op jit(solution)/shard_map/pallas_call | solution.py:202
  52.8 0.2 collective-permute-start.9
  53.1 0.8 collective-permute-start.14
  53.8 2.3 %collective-permute-done.9 = bf16[32,32,576]{2,1,0:T(8,128)(2,1)S(1)} collective-permute-done((bf16[32,32,576]{2,1,0:T(8,128)(2,1)}, bf16[32,32,576]{2,1,0:T(8,128)(2,1)S(1)}, u32[]{:S(2)}, u32[]{:S(2)}) %collective-permute-start.9) | collective-permute-done | bytes 1179680 | tf_op jit(solution)/shard_map/ppermute | solution.py:257
  56.2 0.3 add_convert_fusion.3
  56.4 2.3 %collective-permute-start.10 = (bf16[8,32,576]{2,1,0:T(8,128)(2,1)S(1)}, bf16[8,32,576]{2,1,0:T(8,128)(2,1)S(1)}, u32[]{:S(2)}, u32[]{:S(2)}) collective-permute-start(bf16[8,32,576]{2,1,0:T(8,128)(2,1)S(1)} %get-tuple-element.28), channel_id=1, source_target_pairs={{0,32},{1,9},{4,36},{5,13},{8,40},{9,1},{12,44},{13,5},{64,96},{65... | collective-permute-start | bytes 884744 | tf_op jit(solution)/shard_map/ppermute | solution.py:272
  58.7 1.6 %collective-permute-start.13 = (bf16[256,1280]{1,0:T(8,128)(2,1)S(1)}, bf16[256,1280]{1,0:T(8,128)(2,1)}, u32[]{:S(2)}, u32[]{:S(2)}) collective-permute-start(bf16[256,1280]{1,0:T(8,128)(2,1)S(1)} %get-tuple-element.19), channel_id=1, source_target_pairs={{0,64},{1,65},{4,68},{5,69},{8,72},{9,73},{12,76},{13,77},{64,0},{... | collective-permute-start | bytes 1966088 | tf_op jit(solution)/shard_map/ppermute | solution.py:253
  60.3 1.3 %collective-permute-start.12 = (bf16[8,32,576]{2,1,0:T(8,128)(2,1)S(1)}, bf16[8,32,576]{2,1,0:T(8,128)(2,1)S(1)}, u32[]{:S(2)}, u32[]{:S(2)}) collective-permute-start(bf16[8,32,576]{2,1,0:T(8,128)(2,1)S(1)} %get-tuple-element.29), channel_id=1, source_target_pairs={{0,48},{1,13},{4,52},{5,1},{8,56},{9,5},{12,60},{13,9},{64,112},{6... | collective-permute-start | bytes 884744 | tf_op jit(solution)/shard_map/ppermute | solution.py:272
  61.6 0.7 collective-permute-start.11
  62.3 0.0 collective-permute-done.14
  62.3 4.6 %collective-permute-done.10 = bf16[8,32,576]{2,1,0:T(8,128)(2,1)S(1)} collective-permute-done((bf16[8,32,576]{2,1,0:T(8,128)(2,1)S(1)}, bf16[8,32,576]{2,1,0:T(8,128)(2,1)S(1)}, u32[]{:S(2)}, u32[]{:S(2)}) %collective-permute-start.10) | collective-permute-done | bytes 294944 | tf_op jit(solution)/shard_map/ppermute | solution.py:272
  66.9 0.2 convert_add_fusion
  67.1 0.1 convert_element_type.176
  67.2 1.8 %collective-permute-start.17 = (bf16[64,1024]{1,0:T(8,128)(2,1)S(1)}, bf16[64,1024]{1,0:T(8,128)(2,1)S(1)}, u32[]{:S(2)}, u32[]{:S(2)}) collective-permute-start(bf16[64,1024]{1,0:T(8,128)(2,1)S(1)} %get-tuple-element.37), channel_id=1, source_target_pairs={{0,64},{1,65},{4,68},{5,69},{8,72},{9,73},{12,76},{13,77},{64,0},{... | collective-permute-start | bytes 393224 | tf_op jit(solution)/shard_map/ppermute | solution.py:253
  69.0 1.3 %collective-permute-start.16 = (bf16[64,1024]{1,0:T(8,128)(2,1)S(1)}, bf16[64,1024]{1,0:T(8,128)(2,1)S(1)}, u32[]{:S(2)}, u32[]{:S(2)}) collective-permute-start(bf16[64,1024]{1,0:T(8,128)(2,1)S(1)} %get-tuple-element.38), channel_id=1, source_target_pairs={{0,112},{1,81},{4,116},{5,85},{8,120},{9,89},{12,124},{13,93},{64,... | collective-permute-start | bytes 393224 | tf_op jit(solution)/shard_map/ppermute | solution.py:253
  70.4 0.0 collective-permute-done.12
  70.4 1.6 %collective-permute-start.15 = (bf16[64,1024]{1,0:T(8,128)(2,1)S(1)}, bf16[64,1024]{1,0:T(8,128)(2,1)S(1)}, u32[]{:S(2)}, u32[]{:S(2)}) collective-permute-start(bf16[64,1024]{1,0:T(8,128)(2,1)S(1)} %get-tuple-element.39), channel_id=1, source_target_pairs={{0,48},{1,17},{4,52},{5,21},{8,56},{9,25},{12,60},{13,29},{64,112}... | collective-permute-start | bytes 393224 | tf_op jit(solution)/shard_map/ppermute | solution.py:253
  72.0 0.0 collective-permute-done.11
  72.0 0.9 %add_convert_fusion = bf16[8,32,576]{2,1,0:T(8,128)(2,1)} fusion(bf16[8,32,576]{2,1,0:T(8,128)(2,1)S(1)} %collective-permute-done.12, bf16[8,32,576]{2,1,0:T(8,128)(2,1)S(1)} %collective-permute-done.11, bf16[8,32,576]{2,1,0:T(8,128)(2,1)S(1)} %collective-permute-done.10, bf16[32,32,576]{2,1,0:T(8,128)(2,1)S(1)} %collective-permute-done.9, ...), kind=kLoop, calls=%fused_computation.4 | loop fusion | flops 1474560 | bytes 1769472 | tf_op jit(solution)/shard_map/convert_element_type | solution.py:353
  73.0 8.2 %all-to-all-start = ((bf16[16,16,576]{2,1,0:T(8,128)(2,1)}), bf16[16,16,576]{2,1,0:T(8,128)(2,1)S(1)}, u32[]{:S(2)}, u32[]{:S(2)}) async-start(bf16[16,16,576]{2,1,0:T(8,128)(2,1)} %bitcast.17), calls=%async_computation | async-start | bytes 655360 | tf_op jit(solution)/shard_map/all_to_all | solution.py:283
  81.2 0.0 collective-permute-done.13
  81.2 0.5 collective-permute-done.17
  81.6 0.0 collective-permute-done.16
  81.6 0.0 collective-permute-done.15
  81.6 1.0 %broadcast_select_fusion.3 = (bf16[256,512]{1,0:T(8,128)(2,1)S(1)}, bf16[256,512]{1,0:T(8,128)(2,1)S(1)}) fusion(bf16[256,512]{1,0:T(8,128)(2,1)S(1)} %get-tuple-element.16, pred[]{:T(512)S(6)} %eq.53, bf16[256,1280]{1,0:T(8,128)(2,1)} %collective-permute-done.13), kind=kLoop, calls=%fused_computation.19 | loop fusion | flops 262144 | bytes 1048577 | tf_op jit(solution)/shard_map/jit(_where)/select_n | solution.py:330
  82.6 1.1 %broadcast_select_fusion.1 = (bf16[256,768]{1,0:T(8,128)(2,1)S(1)}, bf16[256,768]{1,0:T(8,128)(2,1)S(1)}) fusion(bf16[256,768]{1,0:T(8,128)(2,1)S(1)} %get-tuple-element.24, pred[]{:T(512)S(6)} %eq.53, bf16[256,1280]{1,0:T(8,128)(2,1)} %collective-permute-done.13), kind=kLoop, calls=%fused_computation.12 | loop fusion | flops 393216 | bytes 1572865 | tf_op jit(solution)/shard_map/jit(_where)/select_n | solution.py:330
  83.7 0.1 fusion.2
  83.8 0.8 pad_maximum_fusion.3
  84.6 0.9 pad_maximum_fusion.2
  85.5 0.9 %pad_maximum_fusion = bf16[256,1536]{1,0:T(8,128)(2,1)} fusion(bf16[256,768]{1,0:T(8,128)(2,1)S(1)} %get-tuple-element.34, bf16[256,768]{1,0:T(8,128)(2,1)S(1)} %get-tuple-element.33), kind=kLoop, calls=%fused_computation.2 | loop fusion | flops 1572864 | bytes 1572864 | tf_op jit(solution)/shard_map/concatenate | solution.py:331
  86.4 3.5 %all-to-all-done = bf16[16,16,576]{2,1,0:T(8,128)(2,1)S(1)} async-done(((bf16[16,16,576]{2,1,0:T(8,128)(2,1)}), bf16[16,16,576]{2,1,0:T(8,128)(2,1)S(1)}, u32[]{:S(2)}, u32[]{:S(2)}) %all-to-all-start) | async-done | bytes 294944 | tf_op jit(solution)/shard_map/all_to_all | solution.py:283
  89.8 0.7 convert_add_fusion.2
  (15 shorter events, 0.3 us)
Async XLA Ops:
  0.6 3.1 %copy-start = (bf16[256,1536]{1,0:T(8,128)(2,1)S(1)}, bf16[256,1536]{1,0:T(8,128)(2,1)}, u32[]{:S(2)}) copy-start(bf16[256,1536]{1,0:T(8,128)(2,1)} %refs_8_.1) | copy-start | bytes 2359300
  0.6 3.1 %copy-start.2 = (f32[256]{0:T(256)S(1)}, f32[256]{0:T(256)}, u32[]{:S(2)}) copy-start(f32[256]{0:T(256)} %param.14) | copy-start | bytes 3076
  0.7 3.1 %copy-start.3 = (f32[256]{0:T(256)S(1)}, f32[256]{0:T(256)}, u32[]{:S(2)}) copy-start(f32[256]{0:T(256)} %param.13) | copy-start | bytes 3076
  0.7 3.1 %copy-start.4 = (f32[256]{0:T(256)S(1)}, f32[256]{0:T(256)}, u32[]{:S(2)}) copy-start(f32[256]{0:T(256)} %param.12) | copy-start | bytes 3076
  0.7 3.2 %copy-start.1 = (bf16[256,1024]{1,0:T(8,128)(2,1)S(1)}, bf16[256,1024]{1,0:T(8,128)(2,1)}, u32[]{:S(2)}) copy-start(bf16[256,1024]{1,0:T(8,128)(2,1)} %param.11) | copy-start | bytes 1572868
  2.0 7.2 %collective-permute-start = (bf16[4,2,16,576]{3,2,1,0:T(8,128)(2,1)S(1)}, bf16[4,2,16,576]{3,2,1,0:T(8,128)(2,1)S(1)}, u32[]{:S(2)}, u32[]{:S(2)}) collective-permute-start(bf16[4,2,16,576]{3,2,1,0:T(8,128)(2,1)S(1)} %get-tuple-element.41), channel_id=1, source_target_pairs={{0,64},{1,65},{4,68},{5,69},{8,72},{9,73},{12,76},{13,77},{64,0},{... | collective-permute-start | bytes 442376 | tf_op jit(solution)/shard_map/ppermute | solution.py:253
  4.0 11.1 %copy-start.5 = (s32[16]{0:T(128)S(1)}, s32[16]{0:T(128)}, u32[]{:S(2)}) copy-start(s32[16]{0:T(128)} %param.15) | copy-start | bytes 196
  4.1 22.5 %collective-permute-start.8 = (bf16[256,1280]{1,0:T(8,128)(2,1)S(1)}, bf16[256,1280]{1,0:T(8,128)(2,1)S(1)}, u32[]{:S(2)}, u32[]{:S(2)}) collective-permute-start(bf16[256,1280]{1,0:T(8,128)(2,1)S(1)} %pad_maximum_fusion.1), channel_id=1, source_target_pairs={{0,64},{1,65},{4,68},{5,69},{8,72},{9,73},{12,76},{13,77},{64,0},{... | collective-permute-start | bytes 1966088 | tf_op jit(solution)/shard_map/ppermute | solution.py:253
  9.2 10.6 %collective-permute-start.3 = (bf16[2,4,2,16,576]{4,3,2,1,0:T(8,128)(2,1)S(1)}, bf16[2,4,2,16,576]{4,3,2,1,0:T(8,128)(2,1)S(1)}, u32[]{:S(2)}, u32[]{:S(2)}) collective-permute-start(bf16[2,4,2,16,576]{4,3,2,1,0:T(8,128)(2,1)S(1)} %pad_maximum_fusion.4), channel_id=1, source_target_pairs={{0,16},{1,17},{4,20},{5,21},{8,24},{9,25},{12,28},{13,29},{64,80},... | collective-permute-start | bytes 884744 | tf_op jit(solution)/shard_map/ppermute | solution.py:272
  10.9 15.2 %collective-permute-start.2 = (bf16[2,4,2,16,576]{4,3,2,1,0:T(8,128)(2,1)S(1)}, bf16[2,4,2,16,576]{4,3,2,1,0:T(8,128)(2,1)S(1)}, u32[]{:S(2)}, u32[]{:S(2)}) collective-permute-start(bf16[2,4,2,16,576]{4,3,2,1,0:T(8,128)(2,1)S(1)} %pad_maximum_fusion.4), channel_id=1, source_target_pairs={{0,32},{1,33},{4,36},{5,37},{8,40},{9,41},{12,44},{13,45},{64,96},... | collective-permute-start | bytes 884744 | tf_op jit(solution)/shard_map/ppermute | solution.py:272
  13.6 12.4 %collective-permute-start.1 = (bf16[2,4,2,16,576]{4,3,2,1,0:T(8,128)(2,1)S(1)}, bf16[2,4,2,16,576]{4,3,2,1,0:T(8,128)(2,1)S(1)}, u32[]{:S(2)}, u32[]{:S(2)}) collective-permute-start(bf16[2,4,2,16,576]{4,3,2,1,0:T(8,128)(2,1)S(1)} %pad_maximum_fusion.4), channel_id=1, source_target_pairs={{0,48},{1,49},{4,52},{5,53},{8,56},{9,57},{12,60},{13,61},{64,112}... | collective-permute-start | bytes 884744 | tf_op jit(solution)/shard_map/ppermute | solution.py:272
  15.2 11.5 %collective-permute-start.4 = (bf16[2,4,2,16,576]{4,3,2,1,0:T(8,128)(2,1)S(1)}, bf16[2,4,2,16,576]{4,3,2,1,0:T(8,128)(2,1)S(1)}, u32[]{:S(2)}, u32[]{:S(2)}) collective-permute-start(bf16[2,4,2,16,576]{4,3,2,1,0:T(8,128)(2,1)S(1)} %pad_maximum_fusion.4), channel_id=1, source_target_pairs={{0,1},{1,0},{2,3},{3,2},{4,5},{5,4},{6,7},{7,6},{8,9},{9,8},{10,11... | collective-permute-start | bytes 884744 | tf_op jit(solution)/shard_map/ppermute | solution.py:257
  19.8 6.8 %collective-permute-start.7 = (bf16[2,4,2,16,576]{4,3,2,1,0:T(8,128)(2,1)S(1)}, bf16[2,4,2,16,576]{4,3,2,1,0:T(8,128)(2,1)S(1)}, u32[]{:S(2)}, u32[]{:S(2)}) collective-permute-start(bf16[2,4,2,16,576]{4,3,2,1,0:T(8,128)(2,1)S(1)} %collective-permute-done.3), channel_id=1, source_target_pairs={{0,1},{1,0},{2,3},{3,2},{4,5},{5,4},{6,7},{7,6},{8,9},{9,8},{10,11... | collective-permute-start | bytes 884744 | tf_op jit(solution)/shard_map/ppermute | solution.py:257
  26.0 1.6 %collective-permute-start.6 = (bf16[2,4,2,16,576]{4,3,2,1,0:T(8,128)(2,1)S(1)}, bf16[2,4,2,16,576]{4,3,2,1,0:T(8,128)(2,1)S(1)}, u32[]{:S(2)}, u32[]{:S(2)}) collective-permute-start(bf16[2,4,2,16,576]{4,3,2,1,0:T(8,128)(2,1)S(1)} %collective-permute-done.2), channel_id=1, source_target_pairs={{0,1},{1,0},{2,3},{3,2},{4,5},{5,4},{6,7},{7,6},{8,9},{9,8},{10,11... | collective-permute-start | bytes 884744 | tf_op jit(solution)/shard_map/ppermute | solution.py:257
  26.0 2.1 %collective-permute-start.5 = (bf16[2,4,2,16,576]{4,3,2,1,0:T(8,128)(2,1)S(1)}, bf16[2,4,2,16,576]{4,3,2,1,0:T(8,128)(2,1)S(1)}, u32[]{:S(2)}, u32[]{:S(2)}) collective-permute-start(bf16[2,4,2,16,576]{4,3,2,1,0:T(8,128)(2,1)S(1)} %collective-permute-done.1), channel_id=1, source_target_pairs={{0,1},{1,0},{2,3},{3,2},{4,5},{5,4},{6,7},{7,6},{8,9},{9,8},{10,11... | collective-permute-start | bytes 884744 | tf_op jit(solution)/shard_map/ppermute | solution.py:257
  52.8 3.3 %collective-permute-start.9 = (bf16[32,32,576]{2,1,0:T(8,128)(2,1)}, bf16[32,32,576]{2,1,0:T(8,128)(2,1)S(1)}, u32[]{:S(2)}, u32[]{:S(2)}) collective-permute-start(bf16[32,32,576]{2,1,0:T(8,128)(2,1)} %get-tuple-element.18), channel_id=1, source_target_pairs={{0,1},{1,0},{2,3},{3,2},{4,5},{5,4},{6,7},{7,6},{8,9},{9,8},{10,11... | collective-permute-start | bytes 3538952 | tf_op jit(solution)/shard_map/ppermute | solution.py:257
  53.1 9.2 %collective-permute-start.14 = (bf16[256,1024]{1,0:T(8,128)(2,1)S(1)}, bf16[256,1024]{1,0:T(8,128)(2,1)S(1)}, u32[]{:S(2)}, u32[]{:S(2)}) collective-permute-start(bf16[256,1024]{1,0:T(8,128)(2,1)S(1)} %get-tuple-element.21), channel_id=1, source_target_pairs={{0,16},{1,49},{4,20},{5,53},{8,24},{9,57},{12,28},{13,61},{64,80},... | collective-permute-start | bytes 1572872 | tf_op jit(solution)/shard_map/ppermute | solution.py:253
  56.4 10.5 %collective-permute-start.10 = (bf16[8,32,576]{2,1,0:T(8,128)(2,1)S(1)}, bf16[8,32,576]{2,1,0:T(8,128)(2,1)S(1)}, u32[]{:S(2)}, u32[]{:S(2)}) collective-permute-start(bf16[8,32,576]{2,1,0:T(8,128)(2,1)S(1)} %get-tuple-element.28), channel_id=1, source_target_pairs={{0,32},{1,9},{4,36},{5,13},{8,40},{9,1},{12,44},{13,5},{64,96},{65... | collective-permute-start | bytes 884744 | tf_op jit(solution)/shard_map/ppermute | solution.py:272
  58.7 22.5 %collective-permute-start.13 = (bf16[256,1280]{1,0:T(8,128)(2,1)S(1)}, bf16[256,1280]{1,0:T(8,128)(2,1)}, u32[]{:S(2)}, u32[]{:S(2)}) collective-permute-start(bf16[256,1280]{1,0:T(8,128)(2,1)S(1)} %get-tuple-element.19), channel_id=1, source_target_pairs={{0,64},{1,65},{4,68},{5,69},{8,72},{9,73},{12,76},{13,77},{64,0},{... | collective-permute-start | bytes 1966088 | tf_op jit(solution)/shard_map/ppermute | solution.py:253
  60.3 10.1 %collective-permute-start.12 = (bf16[8,32,576]{2,1,0:T(8,128)(2,1)S(1)}, bf16[8,32,576]{2,1,0:T(8,128)(2,1)S(1)}, u32[]{:S(2)}, u32[]{:S(2)}) collective-permute-start(bf16[8,32,576]{2,1,0:T(8,128)(2,1)S(1)} %get-tuple-element.29), channel_id=1, source_target_pairs={{0,48},{1,13},{4,52},{5,1},{8,56},{9,5},{12,60},{13,9},{64,112},{6... | collective-permute-start | bytes 884744 | tf_op jit(solution)/shard_map/ppermute | solution.py:272
  61.6 10.4 %collective-permute-start.11 = (bf16[8,32,576]{2,1,0:T(8,128)(2,1)S(1)}, bf16[8,32,576]{2,1,0:T(8,128)(2,1)S(1)}, u32[]{:S(2)}, u32[]{:S(2)}) collective-permute-start(bf16[8,32,576]{2,1,0:T(8,128)(2,1)S(1)} %get-tuple-element.30), channel_id=1, source_target_pairs={{0,16},{1,5},{4,20},{5,9},{8,24},{9,13},{12,28},{13,1},{64,80},{65... | collective-permute-start | bytes 884744 | tf_op jit(solution)/shard_map/ppermute | solution.py:272
  67.2 14.4 %collective-permute-start.17 = (bf16[64,1024]{1,0:T(8,128)(2,1)S(1)}, bf16[64,1024]{1,0:T(8,128)(2,1)S(1)}, u32[]{:S(2)}, u32[]{:S(2)}) collective-permute-start(bf16[64,1024]{1,0:T(8,128)(2,1)S(1)} %get-tuple-element.37), channel_id=1, source_target_pairs={{0,64},{1,65},{4,68},{5,69},{8,72},{9,73},{12,76},{13,77},{64,0},{... | collective-permute-start | bytes 393224 | tf_op jit(solution)/shard_map/ppermute | solution.py:253
  69.0 12.6 %collective-permute-start.16 = (bf16[64,1024]{1,0:T(8,128)(2,1)S(1)}, bf16[64,1024]{1,0:T(8,128)(2,1)S(1)}, u32[]{:S(2)}, u32[]{:S(2)}) collective-permute-start(bf16[64,1024]{1,0:T(8,128)(2,1)S(1)} %get-tuple-element.38), channel_id=1, source_target_pairs={{0,112},{1,81},{4,116},{5,85},{8,120},{9,89},{12,124},{13,93},{64,... | collective-permute-start | bytes 393224 | tf_op jit(solution)/shard_map/ppermute | solution.py:253
  70.4 11.3 %collective-permute-start.15 = (bf16[64,1024]{1,0:T(8,128)(2,1)S(1)}, bf16[64,1024]{1,0:T(8,128)(2,1)S(1)}, u32[]{:S(2)}, u32[]{:S(2)}) collective-permute-start(bf16[64,1024]{1,0:T(8,128)(2,1)S(1)} %get-tuple-element.39), channel_id=1, source_target_pairs={{0,48},{1,17},{4,52},{5,21},{8,56},{9,25},{12,60},{13,29},{64,112}... | collective-permute-start | bytes 393224 | tf_op jit(solution)/shard_map/ppermute | solution.py:253
  73.0 16.9 %all-to-all-start = ((bf16[16,16,576]{2,1,0:T(8,128)(2,1)}), bf16[16,16,576]{2,1,0:T(8,128)(2,1)S(1)}, u32[]{:S(2)}, u32[]{:S(2)}) async-start(bf16[16,16,576]{2,1,0:T(8,128)(2,1)} %bitcast.17), calls=%async_computation | async-start | bytes 655360 | tf_op jit(solution)/shard_map/all_to_all | solution.py:283

commit v8 on v7

--- a/solution.py
+++ b/solution.py
@@ -19,7 +19,7 @@
 F32 = jnp.float32
 SCALE = QK ** -0.5
 SCALE_LOG2 = SCALE * math.log2(math.e)
-AT_QUERY, AT_WEIGHT, AT_TERM, AT_YLO = 128, 132, 140, 204
+AT_QUERY, AT_WEIGHT, AT_TERM = 128, 132, 140
 
 
 def mm(a, b):
@@ -51,25 +51,9 @@
 
 
 def body(ints, *refs):
-    pieces, (q_hbm, g_hbm, far, w_hbm) = refs[:8], refs[8:12]
+    pieces, (q, g, far, w) = refs[:8], refs[8:12]
     out_b, dq_b, far_out, wg_keep, wg_send, keep, send = refs[12:19]
-    q, g, w, lat_t, bias, keys, vals, scores, exps, dscores, dkv, rope, sems = refs[19:]
-    used = []
-
-    def copy(source, target):
-        handle = pltpu.make_async_copy(source, target, sems.at[len(used)])
-        used.append(handle)
-        handle.start()
-        return handle
-
-    y_lo = ints[AT_YLO]
-    loads = [copy(w_hbm.at[:, pl.ds(pl.multiple_of(y_lo * 1024, 1024), 1024)], w)]
-    loads += [
-        copy(q_hbm.at[:, pl.ds(pl.multiple_of(y_lo * 768, 256), 768)], q),
-        copy(g_hbm.at[:, pl.ds(pl.multiple_of(y_lo * 512, 512), 512)], g),
-    ]
-    for load in loads:
-        load.wait()
+    lat_t, bias, keys, vals, scores, exps, dscores, dkv, rope = refs[19:]
     prepare(ints, pieces, lat_t, bias, keys)
 
     chunks = [pl.ds(c * CHUNK, CHUNK) for c in range(KEYS // CHUNK)]
@@ -197,13 +181,11 @@
     def shape(*dims):
         return jax.ShapeDtypeStruct(dims, BF)
 
-    anywhere = pl.BlockSpec(memory_space=pl.ANY)
     inside = pl.BlockSpec(memory_space=pltpu.VMEM)
     return pl.pallas_call(
         body,
         in_specs=[pl.BlockSpec(memory_space=pltpu.SMEM)]
-        + [inside] * 8
-        + [anywhere, anywhere, inside, anywhere],
+        + [inside] * 12,
         out_specs=[inside] * 7,
         out_shape=[
             shape(256, 4 * VDIM),
@@ -215,9 +197,6 @@
             shape(32, 32, LAT),
         ],
         scratch_shapes=[
-            pltpu.VMEM((256, 4 * QK), BF),
-            pltpu.VMEM((256, 4 * VDIM), BF),
-            pltpu.VMEM((KV_RANK, 1024), BF),
             pltpu.VMEM((KV_RANK, KEYS), BF),
             pltpu.VMEM((KEYS, ROWS), F32),
             pltpu.VMEM((4, KEYS, QK), BF),
@@ -227,9 +206,8 @@
             pltpu.VMEM((2, KEYS, ROWS), BF),
             pltpu.VMEM((KEYS, 1024), BF),
             pltpu.VMEM((KEYS, QK - NOPE), F32),
-            pltpu.SemaphoreType.DMA((3,)),
         ],
-        compiler_params=pltpu.CompilerParams(vmem_limit_bytes=46 * 2**20),
+        compiler_params=pltpu.CompilerParams(vmem_limit_bytes=41 * 2**20),
         cost_estimate=pl.CostEstimate(
             flops=20 * 10**9, bytes_accessed=16 * 2**20, transcendentals=2**22
         ),
@@ -289,7 +267,8 @@
     pair = jnp.stack([own, swap_ylo(own)], axis=0)
     far = {k: shift(pair, (-k, 0), (-k, 0)) for k in (1, 3, 2)}
     mine = [pair, far[1], far[2], far[3]]
-    return [piece.reshape(256, LAT) for piece in mine + [swap_cores(piece) for piece in mine]]
+    pieces = mine + [swap_cores(piece) for piece in mine]
+    return pair, [piece.reshape(256, LAT) for piece in pieces]
 
 
 def kernel_ints(x, y_lo, z, core, group_order):
@@ -316,7 +295,7 @@
     x_first = block // 8 % 4 * 8 + far_z * 2 + far_y
     z_first = (far_z - z + 4) % 4 * 8 + far_x * 2 + far_y
     terms = jnp.where((core ^ (block // 32)) == 0, x_first, z_first)
-    return jnp.concatenate([starts, weight_rows, terms, y_lo[None]])
+    return jnp.concatenate([starts, weight_rows, terms])
 
 
 def sum_terms(first, others):
@@ -331,9 +310,13 @@
     return jnp.concatenate([low, high], axis=axis)
 
 
+def own_half(y_lo, value):
+    width = value.shape[1] // 2
+    return jnp.where(y_lo == 0, value[:, :width], value[:, width:])
+
+
 def other_half(y_lo, value):
-    width = value.shape[1] // 2
-    return jnp.where(y_lo == 0, value[:, width:], value[:, :width])
+    return own_half(1 - y_lo, value)
 
 
 def reduce_terms(y_lo, out, dq, far_out, wg_keep, wg_send, keep, send):
@@ -369,9 +352,11 @@
     dout = (tok_weight[:, None] * out_grad.astype(F32)).astype(BF)
     far = jnp.concatenate([other_half(y_lo, queries), other_half(y_lo, dout)], axis=1)
     far = swap_ylo(far)
-    pieces = gather_latent(latent, core)
+    pair, pieces = gather_latent(latent, core)
     ints = kernel_ints(x, y_lo, z, core, group_order)
-    results = attention(ints, pieces, queries, dout, far, up_weight)
+    own = lax.optimization_barrier((queries, dout, up_weight, pair))[:3]
+    own = [own_half(y_lo, value) for value in own]
+    results = attention(ints, pieces, own[0], own[1], far, own[2])
     return reduce_terms(y_lo, *results)
 
 

time: 90.8 us -> 89 us (0.980)
  waiting for transfers between devices: 27.7 us -> 25.1 us
  other arithmetic: 7.47 us -> 10 us
  Pallas kernels: 24.7 us -> 22.4 us
    pallas_call x1, Pallas kernels: 24.7 us -> 22.4 us  [attention(): pl.pallas_call(body, in_specs=[pl.BlockSpec(memory_space=pltpu.SMEM)] + [...]
    ppermute x5, waiting for transfers between devices: 3.82 us -> 1.81 us  [swap_cores(): return lax.ppermute(value, 'head', [(i, i ^ 1) for i in range(16)])]
    ppermute x7, waiting for transfers between devices: 5.01 us -> 3.13 us  [trade(): return lax.ppermute(value, AXES, pairs)]
    select_n x2 -> x5, other arithmetic: 0.07 us -> 1.79 us  [own_half(): return jnp.where(y_lo == 0, value[:, :width], value[:, width:])]
    ppermute x6, waiting for transfers between devices: 15.4 us -> 16.4 us  [shift(): return lax.ppermute(value, AXES, pairs)]
  transfers between devices with their start and end apart: 19 -> 19, of which waited for: 9 -> 7; matrix products, arithmetic and copies ran while one was open for 8% -> 11% of each run, Pallas kernels for 0% -> 0%
where the time goes in v8:
time: 89 us; the launch traced here: 88.7 us
  starting transfers between devices  28.9 us (32%)
  waiting for transfers between devices  25.1 us (28%)
  Pallas kernels  22.4 us (25%)
  other arithmetic  10 us (11%)
  local copies, waits for them, and re-layouts  1.31 us (1%)
  between operations  0.95 us (1%)
    pallas_call x1, Pallas kernels, attention(): pl.pallas_call(body, in_specs=[pl.BlockSpec(memory_space=pltpu.SMEM)] + [...  22.4 us
    ppermute x6, waiting for transfers between devices, shift(): return lax.ppermute(value, AXES, pairs)  16.4 us
    ppermute x6, starting transfers between devices, shift(): return lax.ppermute(value, AXES, pairs)  10.5 us
    ppermute x7, starting transfers between devices, trade(): return lax.ppermute(value, AXES, pairs)  9.68 us
    all_to_all x1, starting transfers between devices, exchange_rest(): lax.all_to_all(value, AXES, 0, 0, tiled=True, axis_index_groups=groups)  8.16 us
    all_to_all x1, waiting for transfers between devices, exchange_rest(): lax.all_to_all(value, AXES, 0, 0, tiled=True, axis_index_groups=groups)  3.8 us
    ppermute x7, waiting for transfers between devices, trade(): return lax.ppermute(value, AXES, pairs)  3.13 us
    concatenate x3, other arithmetic, halves(): return jnp.concatenate([low, high], axis=axis)  2.62 us
  transfers between devices with their start and end apart: 19, of which 7 were waited for; matrix products, arithmetic and copies ran while one was open for 11% of the time, Pallas kernels for 0%

profile of v8, /device:TPU:0, one launch (start us, length us, event | category | flops | bytes accessed | tf_op | source)
XLA Modules:
  0.0 88.7 jit_solution(2316768279555984309)
XLA Ops:
  0.6 0.0 copy-start
  0.6 0.0 copy-start.2
  0.7 0.0 copy-start.3
  0.7 0.0 copy-start.4
  0.7 1.3 %copy.15 = bf16[256,576]{1,0:T(8,128)(2,1)S(1)} copy(bf16[256,576]{0,1:T(8,128)(2,1)} %param.8) | data formatting | bytes 589824 | tf_op args[0]
  2.0 1.7 %collective-permute-start = (bf16[4,2,16,576]{3,2,1,0:T(8,128)(2,1)S(1)}, bf16[4,2,16,576]{3,2,1,0:T(8,128)(2,1)S(1)}, u32[]{:S(2)}, u32[]{:S(2)}) collective-permute-start(bf16[4,2,16,576]{3,2,1,0:T(8,128)(2,1)S(1)} %get-tuple-element.47), channel_id=1, source_target_pairs={{0,64},{1,65},{4,68},{5,69},{8,72},{9,73},{12,76},{13,77},{64,0},{... | collective-permute-start | bytes 442376 | tf_op jit(solution)/shard_map/ppermute | solution.py:231
  3.7 0.0 copy-done
  3.8 0.0 copy-done.1
  3.8 0.2 multiply_convert_fusion
  4.0 0.0 copy-start.5
  4.0 0.9 pad_maximum_fusion.1
  4.9 0.4 collective-permute-start.8
  5.3 0.0 copy-done.5
  5.4 0.1 select_reduce_fusion
  5.5 3.0 %collective-permute-done = bf16[4,2,16,576]{3,2,1,0:T(8,128)(2,1)S(1)} collective-permute-done((bf16[4,2,16,576]{3,2,1,0:T(8,128)(2,1)S(1)}, bf16[4,2,16,576]{3,2,1,0:T(8,128)(2,1)S(1)}, u32[]{:S(2)}, u32[]{:S(2)}) %collective-permute-start) | collective-permute-done | bytes 147488 | tf_op jit(solution)/shard_map/ppermute | solution.py:231
  8.6 1.9 %collective-permute-start.3 = (bf16[2,4,2,16,576]{4,3,2,1,0:T(8,128)(2,1)S(1)}, bf16[2,4,2,16,576]{4,3,2,1,0:T(8,128)(2,1)S(1)}, u32[]{:S(2)}, u32[]{:S(2)}) collective-permute-start(bf16[2,4,2,16,576]{4,3,2,1,0:T(8,128)(2,1)S(1)} %pad_maximum_fusion.4), channel_id=1, source_target_pairs={{0,16},{1,17},{4,20},{5,21},{8,24},{9,25},{12,28},{13,29},{64,80},... | collective-permute-start | bytes 884744 | tf_op jit(solution)/shard_map/ppermute | solution.py:250
  10.5 2.7 %collective-permute-start.2 = (bf16[2,4,2,16,576]{4,3,2,1,0:T(8,128)(2,1)S(1)}, bf16[2,4,2,16,576]{4,3,2,1,0:T(8,128)(2,1)S(1)}, u32[]{:S(2)}, u32[]{:S(2)}) collective-permute-start(bf16[2,4,2,16,576]{4,3,2,1,0:T(8,128)(2,1)S(1)} %pad_maximum_fusion.4), channel_id=1, source_target_pairs={{0,32},{1,33},{4,36},{5,37},{8,40},{9,41},{12,44},{13,45},{64,96},... | collective-permute-start | bytes 884744 | tf_op jit(solution)/shard_map/ppermute | solution.py:250
  13.2 1.4 %collective-permute-start.1 = (bf16[2,4,2,16,576]{4,3,2,1,0:T(8,128)(2,1)S(1)}, bf16[2,4,2,16,576]{4,3,2,1,0:T(8,128)(2,1)S(1)}, u32[]{:S(2)}, u32[]{:S(2)}) collective-permute-start(bf16[2,4,2,16,576]{4,3,2,1,0:T(8,128)(2,1)S(1)} %pad_maximum_fusion.4), channel_id=1, source_target_pairs={{0,48},{1,49},{4,52},{5,53},{8,56},{9,57},{12,60},{13,61},{64,112}... | collective-permute-start | bytes 884744 | tf_op jit(solution)/shard_map/ppermute | solution.py:250
  14.6 0.1 pad_add_fusion.1.ints
  14.7 0.0 collective-permute-start.4
  14.8 4.7 %collective-permute-done.3 = bf16[2,4,2,16,576]{4,3,2,1,0:T(8,128)(2,1)S(1)} collective-permute-done((bf16[2,4,2,16,576]{4,3,2,1,0:T(8,128)(2,1)S(1)}, bf16[2,4,2,16,576]{4,3,2,1,0:T(8,128)(2,1)S(1)}, u32[]{:S(2)}, u32[]{:S(2)}) %collective-permute-start.3) | collective-permute-done | bytes 294944 | tf_op jit(solution)/shard_map/ppermute | solution.py:250
  19.4 0.0 collective-permute-start.7
  19.5 6.6 %collective-permute-done.2 = bf16[2,4,2,16,576]{4,3,2,1,0:T(8,128)(2,1)S(1)} collective-permute-done((bf16[2,4,2,16,576]{4,3,2,1,0:T(8,128)(2,1)S(1)}, bf16[2,4,2,16,576]{4,3,2,1,0:T(8,128)(2,1)S(1)}, u32[]{:S(2)}, u32[]{:S(2)}) %collective-permute-start.2) | collective-permute-done | bytes 294944 | tf_op jit(solution)/shard_map/ppermute | solution.py:250
  26.0 0.0 collective-permute-start.6
  26.0 0.0 collective-permute-done.1
  26.0 0.5 collective-permute-start.5
  26.6 1.7 %slice_select_fusion.refs_11_ = bf16[512,1024]{1,0:T(8,128)(2,1)S(1)} fusion(bf16[512,2048]{1,0:T(8,128)(2,1)} %param.10, pred[]{:T(512)S(6)} %eq.58), kind=kLoop, calls=%fused_computation.1 | loop fusion | flops 524288 | bytes 3145729 | tf_op jit(solution)/shard_map/jit(_where)/select_n | solution.py:315
  28.2 0.0 collective-permute-done.4
  28.2 0.0 collective-permute-done.8.refs_10_
  28.2 0.0 collective-permute-done.7
  28.2 0.0 collective-permute-done.6
  28.3 0.0 collective-permute-done.5
  28.3 22.4 %shard_map.111 = (bf16[256,512]{1,0:T(8,128)(2,1)S(1)}, bf16[256,768]{1,0:T(8,128)(2,1)S(1)}, bf16[256,1280]{1,0:T(8,128)(2,1)S(1)}, bf16[256,1024]{1,0:T(8,128)...) custom-call(s32[204]{0:T(256)S(1)} %pad_add_fusion.1.ints, ...), custom_call_target="tpu_custom_call" | custom-call | flops 20000000000 | bytes 16777216 | tf_op jit(solution)/shard_map/pallas_call | solution.py:185
  50.7 0.1 collective-permute-start.9
  50.8 1.2 %collective-permute-start.14 = (bf16[256,1024]{1,0:T(8,128)(2,1)S(1)}, bf16[256,1024]{1,0:T(8,128)(2,1)S(1)}, u32[]{:S(2)}, u32[]{:S(2)}) collective-permute-start(bf16[256,1024]{1,0:T(8,128)(2,1)S(1)} %get-tuple-element.27), channel_id=1, source_target_pairs={{0,16},{1,49},{4,20},{5,53},{8,24},{9,57},{12,28},{13,61},{64,80},... | collective-permute-start | bytes 1572872 | tf_op jit(solution)/shard_map/ppermute | solution.py:231
  52.0 1.8 %collective-permute-done.9 = bf16[32,32,576]{2,1,0:T(8,128)(2,1)S(1)} collective-permute-done((bf16[32,32,576]{2,1,0:T(8,128)(2,1)S(1)}, bf16[32,32,576]{2,1,0:T(8,128)(2,1)S(1)}, u32[]{:S(2)}, u32[]{:S(2)}) %collective-permute-start.9) | collective-permute-done | bytes 1179680 | tf_op jit(solution)/shard_map/ppermute | solution.py:235
  53.8 0.2 add_convert_fusion.3
  54.1 2.4 %collective-permute-start.10 = (bf16[8,32,576]{2,1,0:T(8,128)(2,1)S(1)}, bf16[8,32,576]{2,1,0:T(8,128)(2,1)S(1)}, u32[]{:S(2)}, u32[]{:S(2)}) collective-permute-start(bf16[8,32,576]{2,1,0:T(8,128)(2,1)S(1)} %get-tuple-element.34), channel_id=1, source_target_pairs={{0,32},{1,9},{4,36},{5,13},{8,40},{9,1},{12,44},{13,5},{64,96},{65... | collective-permute-start | bytes 884744 | tf_op jit(solution)/shard_map/ppermute | solution.py:250
  56.4 1.6 %collective-permute-start.13 = (bf16[256,1280]{1,0:T(8,128)(2,1)S(1)}, bf16[256,1280]{1,0:T(8,128)(2,1)}, u32[]{:S(2)}, u32[]{:S(2)}) collective-permute-start(bf16[256,1280]{1,0:T(8,128)(2,1)S(1)} %get-tuple-element.25), channel_id=1, source_target_pairs={{0,64},{1,65},{4,68},{5,69},{8,72},{9,73},{12,76},{13,77},{64,0},{... | collective-permute-start | bytes 1966088 | tf_op jit(solution)/shard_map/ppermute | solution.py:231
  58.0 1.3 %collective-permute-start.12 = (bf16[8,32,576]{2,1,0:T(8,128)(2,1)S(1)}, bf16[8,32,576]{2,1,0:T(8,128)(2,1)S(1)}, u32[]{:S(2)}, u32[]{:S(2)}) collective-permute-start(bf16[8,32,576]{2,1,0:T(8,128)(2,1)S(1)} %get-tuple-element.35), channel_id=1, source_target_pairs={{0,48},{1,13},{4,52},{5,1},{8,56},{9,5},{12,60},{13,9},{64,112},{6... | collective-permute-start | bytes 884744 | tf_op jit(solution)/shard_map/ppermute | solution.py:250
  59.3 0.7 collective-permute-start.11
  60.0 0.0 collective-permute-done.14
  60.0 5.1 %collective-permute-done.10 = bf16[8,32,576]{2,1,0:T(8,128)(2,1)S(1)} collective-permute-done((bf16[8,32,576]{2,1,0:T(8,128)(2,1)S(1)}, bf16[8,32,576]{2,1,0:T(8,128)(2,1)S(1)}, u32[]{:S(2)}, u32[]{:S(2)}) %collective-permute-start.10) | collective-permute-done | bytes 294944 | tf_op jit(solution)/shard_map/ppermute | solution.py:250
  65.2 0.2 convert_add_fusion
  65.3 0.1 convert_element_type.176
  65.5 1.8 %collective-permute-start.17 = (bf16[64,1024]{1,0:T(8,128)(2,1)S(1)}, bf16[64,1024]{1,0:T(8,128)(2,1)S(1)}, u32[]{:S(2)}, u32[]{:S(2)}) collective-permute-start(bf16[64,1024]{1,0:T(8,128)(2,1)S(1)} %get-tuple-element.43), channel_id=1, source_target_pairs={{0,64},{1,65},{4,68},{5,69},{8,72},{9,73},{12,76},{13,77},{64,0},{... | collective-permute-start | bytes 393224 | tf_op jit(solution)/shard_map/ppermute | solution.py:231
  67.2 0.9 %collective-permute-start.16 = (bf16[64,1024]{1,0:T(8,128)(2,1)S(1)}, bf16[64,1024]{1,0:T(8,128)(2,1)S(1)}, u32[]{:S(2)}, u32[]{:S(2)}) collective-permute-start(bf16[64,1024]{1,0:T(8,128)(2,1)S(1)} %get-tuple-element.44), channel_id=1, source_target_pairs={{0,112},{1,81},{4,116},{5,85},{8,120},{9,89},{12,124},{13,93},{64,... | collective-permute-start | bytes 393224 | tf_op jit(solution)/shard_map/ppermute | solution.py:231
  68.2 0.0 collective-permute-done.12
  68.2 2.1 %collective-permute-start.15 = (bf16[64,1024]{1,0:T(8,128)(2,1)S(1)}, bf16[64,1024]{1,0:T(8,128)(2,1)S(1)}, u32[]{:S(2)}, u32[]{:S(2)}) collective-permute-start(bf16[64,1024]{1,0:T(8,128)(2,1)S(1)} %get-tuple-element.45), channel_id=1, source_target_pairs={{0,48},{1,17},{4,52},{5,21},{8,56},{9,25},{12,60},{13,29},{64,112}... | collective-permute-start | bytes 393224 | tf_op jit(solution)/shard_map/ppermute | solution.py:231
  70.2 0.0 collective-permute-done.11
  70.2 0.9 %add_convert_fusion = bf16[8,32,576]{2,1,0:T(8,128)(2,1)} fusion(bf16[8,32,576]{2,1,0:T(8,128)(2,1)S(1)} %collective-permute-done.12, bf16[8,32,576]{2,1,0:T(8,128)(2,1)S(1)} %collective-permute-done.11, bf16[8,32,576]{2,1,0:T(8,128)(2,1)S(1)} %collective-permute-done.10, bf16[32,32,576]{2,1,0:T(8,128)(2,1)S(1)} %collective-permute-done.9, ...), kind=kLoop, calls=%fused_computation.5 | loop fusion | flops 1474560 | bytes 1769472 | tf_op jit(solution)/shard_map/convert_element_type | solution.py:336
  71.2 8.2 %all-to-all-start = ((bf16[16,16,576]{2,1,0:T(8,128)(2,1)}), bf16[16,16,576]{2,1,0:T(8,128)(2,1)S(1)}, u32[]{:S(2)}, u32[]{:S(2)}) async-start(bf16[16,16,576]{2,1,0:T(8,128)(2,1)} %bitcast.16), calls=%async_computation | async-start | bytes 655360 | tf_op jit(solution)/shard_map/all_to_all | solution.py:261
  79.4 0.0 collective-permute-done.13
  79.4 0.1 collective-permute-done.17
  79.5 0.0 collective-permute-done.16
  79.5 0.0 collective-permute-done.15
  79.5 1.0 %broadcast_select_fusion.3 = (bf16[256,512]{1,0:T(8,128)(2,1)S(1)}, bf16[256,512]{1,0:T(8,128)(2,1)S(1)}) fusion(bf16[256,512]{1,0:T(8,128)(2,1)S(1)} %get-tuple-element.22, pred[]{:T(512)S(6)} %eq.58, bf16[256,1280]{1,0:T(8,128)(2,1)} %collective-permute-done.13), kind=kLoop, calls=%fused_computation.22 | loop fusion | flops 262144 | bytes 1048577 | tf_op jit(solution)/shard_map/jit(_where)/select_n | solution.py:309
  80.5 1.1 %broadcast_select_fusion.1 = (bf16[256,768]{1,0:T(8,128)(2,1)S(1)}, bf16[256,768]{1,0:T(8,128)(2,1)S(1)}) fusion(bf16[256,768]{1,0:T(8,128)(2,1)S(1)} %get-tuple-element.30, pred[]{:T(512)S(6)} %eq.58, bf16[256,1280]{1,0:T(8,128)(2,1)} %collective-permute-done.13), kind=kLoop, calls=%fused_computation.14 | loop fusion | flops 393216 | bytes 1572865 | tf_op jit(solution)/shard_map/jit(_where)/select_n | solution.py:309
  81.5 0.1 fusion.2
  81.6 0.8 pad_maximum_fusion.3
  82.4 0.9 pad_maximum_fusion.2
  83.3 0.9 %pad_maximum_fusion = bf16[256,1536]{1,0:T(8,128)(2,1)} fusion(bf16[256,768]{1,0:T(8,128)(2,1)S(1)} %get-tuple-element.40, bf16[256,768]{1,0:T(8,128)(2,1)S(1)} %get-tuple-element.39), kind=kLoop, calls=%fused_computation.3 | loop fusion | flops 1572864 | bytes 1572864 | tf_op jit(solution)/shard_map/concatenate | solution.py:310
  84.2 3.8 %all-to-all-done = bf16[16,16,576]{2,1,0:T(8,128)(2,1)S(1)} async-done(((bf16[16,16,576]{2,1,0:T(8,128)(2,1)}), bf16[16,16,576]{2,1,0:T(8,128)(2,1)S(1)}, u32[]{:S(2)}, u32[]{:S(2)}) %all-to-all-start) | async-done | bytes 294944 | tf_op jit(solution)/shard_map/all_to_all | solution.py:261
  88.0 0.7 convert_add_fusion.2
  (18 shorter events, 0.4 us)
Async XLA Ops:
  0.6 3.1 %copy-start = (bf16[256,1536]{1,0:T(8,128)(2,1)S(1)}, bf16[256,1536]{1,0:T(8,128)(2,1)}, u32[]{:S(2)}) copy-start(bf16[256,1536]{1,0:T(8,128)(2,1)} %param.9) | copy-start | bytes 2359300
  0.6 3.1 %copy-start.2 = (f32[256]{0:T(256)S(1)}, f32[256]{0:T(256)}, u32[]{:S(2)}) copy-start(f32[256]{0:T(256)} %param.14) | copy-start | bytes 3076
  0.7 3.1 %copy-start.3 = (f32[256]{0:T(256)S(1)}, f32[256]{0:T(256)}, u32[]{:S(2)}) copy-start(f32[256]{0:T(256)} %param.13) | copy-start | bytes 3076
  0.7 3.1 %copy-start.4 = (f32[256]{0:T(256)S(1)}, f32[256]{0:T(256)}, u32[]{:S(2)}) copy-start(f32[256]{0:T(256)} %param.12) | copy-start | bytes 3076
  0.7 3.2 %copy-start.1 = (bf16[256,1024]{1,0:T(8,128)(2,1)S(1)}, bf16[256,1024]{1,0:T(8,128)(2,1)}, u32[]{:S(2)}) copy-start(bf16[256,1024]{1,0:T(8,128)(2,1)} %param.11) | copy-start | bytes 1572868
  2.0 6.5 %collective-permute-start = (bf16[4,2,16,576]{3,2,1,0:T(8,128)(2,1)S(1)}, bf16[4,2,16,576]{3,2,1,0:T(8,128)(2,1)S(1)}, u32[]{:S(2)}, u32[]{:S(2)}) collective-permute-start(bf16[4,2,16,576]{3,2,1,0:T(8,128)(2,1)S(1)} %get-tuple-element.47), channel_id=1, source_target_pairs={{0,64},{1,65},{4,68},{5,69},{8,72},{9,73},{12,76},{13,77},{64,0},{... | collective-permute-start | bytes 442376 | tf_op jit(solution)/shard_map/ppermute | solution.py:231
  4.0 1.4 %copy-start.5 = (s32[16]{0:T(128)S(1)}, s32[16]{0:T(128)}, u32[]{:S(2)}) copy-start(s32[16]{0:T(128)} %param.15) | copy-start | bytes 196
  4.9 23.3 %collective-permute-start.8 = (bf16[256,1280]{1,0:T(8,128)(2,1)}, bf16[256,1280]{1,0:T(8,128)(2,1)S(1)}, u32[]{:S(2)}, u32[]{:S(2)}) collective-permute-start(bf16[256,1280]{1,0:T(8,128)(2,1)} %pad_maximum_fusion.1), channel_id=1, source_target_pairs={{0,64},{1,65},{4,68},{5,69},{8,72},{9,73},{12,76},{13,77},{64,0},{... | collective-permute-start | bytes 1966088 | tf_op jit(solution)/shard_map/ppermute | solution.py:231
  8.6 10.9 %collective-permute-start.3 = (bf16[2,4,2,16,576]{4,3,2,1,0:T(8,128)(2,1)S(1)}, bf16[2,4,2,16,576]{4,3,2,1,0:T(8,128)(2,1)S(1)}, u32[]{:S(2)}, u32[]{:S(2)}) collective-permute-start(bf16[2,4,2,16,576]{4,3,2,1,0:T(8,128)(2,1)S(1)} %pad_maximum_fusion.4), channel_id=1, source_target_pairs={{0,16},{1,17},{4,20},{5,21},{8,24},{9,25},{12,28},{13,29},{64,80},... | collective-permute-start | bytes 884744 | tf_op jit(solution)/shard_map/ppermute | solution.py:250
  10.5 15.6 %collective-permute-start.2 = (bf16[2,4,2,16,576]{4,3,2,1,0:T(8,128)(2,1)S(1)}, bf16[2,4,2,16,576]{4,3,2,1,0:T(8,128)(2,1)S(1)}, u32[]{:S(2)}, u32[]{:S(2)}) collective-permute-start(bf16[2,4,2,16,576]{4,3,2,1,0:T(8,128)(2,1)S(1)} %pad_maximum_fusion.4), channel_id=1, source_target_pairs={{0,32},{1,33},{4,36},{5,37},{8,40},{9,41},{12,44},{13,45},{64,96},... | collective-permute-start | bytes 884744 | tf_op jit(solution)/shard_map/ppermute | solution.py:250
  13.2 12.8 %collective-permute-start.1 = (bf16[2,4,2,16,576]{4,3,2,1,0:T(8,128)(2,1)S(1)}, bf16[2,4,2,16,576]{4,3,2,1,0:T(8,128)(2,1)S(1)}, u32[]{:S(2)}, u32[]{:S(2)}) collective-permute-start(bf16[2,4,2,16,576]{4,3,2,1,0:T(8,128)(2,1)S(1)} %pad_maximum_fusion.4), channel_id=1, source_target_pairs={{0,48},{1,49},{4,52},{5,53},{8,56},{9,57},{12,60},{13,61},{64,112}... | collective-permute-start | bytes 884744 | tf_op jit(solution)/shard_map/ppermute | solution.py:250
  14.7 13.5 %collective-permute-start.4 = (bf16[2,4,2,16,576]{4,3,2,1,0:T(8,128)(2,1)S(1)}, bf16[2,4,2,16,576]{4,3,2,1,0:T(8,128)(2,1)S(1)}, u32[]{:S(2)}, u32[]{:S(2)}) collective-permute-start(bf16[2,4,2,16,576]{4,3,2,1,0:T(8,128)(2,1)S(1)} %pad_maximum_fusion.4), channel_id=1, source_target_pairs={{0,1},{1,0},{2,3},{3,2},{4,5},{5,4},{6,7},{7,6},{8,9},{9,8},{10,11... | collective-permute-start | bytes 884744 | tf_op jit(solution)/shard_map/ppermute | solution.py:235
  19.4 8.8 %collective-permute-start.7 = (bf16[2,4,2,16,576]{4,3,2,1,0:T(8,128)(2,1)S(1)}, bf16[2,4,2,16,576]{4,3,2,1,0:T(8,128)(2,1)S(1)}, u32[]{:S(2)}, u32[]{:S(2)}) collective-permute-start(bf16[2,4,2,16,576]{4,3,2,1,0:T(8,128)(2,1)S(1)} %collective-permute-done.3), channel_id=1, source_target_pairs={{0,1},{1,0},{2,3},{3,2},{4,5},{5,4},{6,7},{7,6},{8,9},{9,8},{10,11... | collective-permute-start | bytes 884744 | tf_op jit(solution)/shard_map/ppermute | solution.py:235
  26.0 2.2 %collective-permute-start.6 = (bf16[2,4,2,16,576]{4,3,2,1,0:T(8,128)(2,1)S(1)}, bf16[2,4,2,16,576]{4,3,2,1,0:T(8,128)(2,1)S(1)}, u32[]{:S(2)}, u32[]{:S(2)}) collective-permute-start(bf16[2,4,2,16,576]{4,3,2,1,0:T(8,128)(2,1)S(1)} %collective-permute-done.2), channel_id=1, source_target_pairs={{0,1},{1,0},{2,3},{3,2},{4,5},{5,4},{6,7},{7,6},{8,9},{9,8},{10,11... | collective-permute-start | bytes 884744 | tf_op jit(solution)/shard_map/ppermute | solution.py:235
  26.0 2.2 %collective-permute-start.5 = (bf16[2,4,2,16,576]{4,3,2,1,0:T(8,128)(2,1)S(1)}, bf16[2,4,2,16,576]{4,3,2,1,0:T(8,128)(2,1)S(1)}, u32[]{:S(2)}, u32[]{:S(2)}) collective-permute-start(bf16[2,4,2,16,576]{4,3,2,1,0:T(8,128)(2,1)S(1)} %collective-permute-done.1), channel_id=1, source_target_pairs={{0,1},{1,0},{2,3},{3,2},{4,5},{5,4},{6,7},{7,6},{8,9},{9,8},{10,11... | collective-permute-start | bytes 884744 | tf_op jit(solution)/shard_map/ppermute | solution.py:235
  50.7 3.1 %collective-permute-start.9 = (bf16[32,32,576]{2,1,0:T(8,128)(2,1)S(1)}, bf16[32,32,576]{2,1,0:T(8,128)(2,1)S(1)}, u32[]{:S(2)}, u32[]{:S(2)}) collective-permute-start(bf16[32,32,576]{2,1,0:T(8,128)(2,1)S(1)} %get-tuple-element.24), channel_id=1, source_target_pairs={{0,1},{1,0},{2,3},{3,2},{4,5},{5,4},{6,7},{7,6},{8,9},{9,8},{10,11... | collective-permute-start | bytes 3538952 | tf_op jit(solution)/shard_map/ppermute | solution.py:235
  50.8 9.3 %collective-permute-start.14 = (bf16[256,1024]{1,0:T(8,128)(2,1)S(1)}, bf16[256,1024]{1,0:T(8,128)(2,1)S(1)}, u32[]{:S(2)}, u32[]{:S(2)}) collective-permute-start(bf16[256,1024]{1,0:T(8,128)(2,1)S(1)} %get-tuple-element.27), channel_id=1, source_target_pairs={{0,16},{1,49},{4,20},{5,53},{8,24},{9,57},{12,28},{13,61},{64,80},... | collective-permute-start | bytes 1572872 | tf_op jit(solution)/shard_map/ppermute | solution.py:231
  54.1 11.1 %collective-permute-start.10 = (bf16[8,32,576]{2,1,0:T(8,128)(2,1)S(1)}, bf16[8,32,576]{2,1,0:T(8,128)(2,1)S(1)}, u32[]{:S(2)}, u32[]{:S(2)}) collective-permute-start(bf16[8,32,576]{2,1,0:T(8,128)(2,1)S(1)} %get-tuple-element.34), channel_id=1, source_target_pairs={{0,32},{1,9},{4,36},{5,13},{8,40},{9,1},{12,44},{13,5},{64,96},{65... | collective-permute-start | bytes 884744 | tf_op jit(solution)/shard_map/ppermute | solution.py:250
  56.4 22.9 %collective-permute-start.13 = (bf16[256,1280]{1,0:T(8,128)(2,1)S(1)}, bf16[256,1280]{1,0:T(8,128)(2,1)}, u32[]{:S(2)}, u32[]{:S(2)}) collective-permute-start(bf16[256,1280]{1,0:T(8,128)(2,1)S(1)} %get-tuple-element.25), channel_id=1, source_target_pairs={{0,64},{1,65},{4,68},{5,69},{8,72},{9,73},{12,76},{13,77},{64,0},{... | collective-permute-start | bytes 1966088 | tf_op jit(solution)/shard_map/ppermute | solution.py:231
  58.0 10.2 %collective-permute-start.12 = (bf16[8,32,576]{2,1,0:T(8,128)(2,1)S(1)}, bf16[8,32,576]{2,1,0:T(8,128)(2,1)S(1)}, u32[]{:S(2)}, u32[]{:S(2)}) collective-permute-start(bf16[8,32,576]{2,1,0:T(8,128)(2,1)S(1)} %get-tuple-element.35), channel_id=1, source_target_pairs={{0,48},{1,13},{4,52},{5,1},{8,56},{9,5},{12,60},{13,9},{64,112},{6... | collective-permute-start | bytes 884744 | tf_op jit(solution)/shard_map/ppermute | solution.py:250
  59.3 10.9 %collective-permute-start.11 = (bf16[8,32,576]{2,1,0:T(8,128)(2,1)S(1)}, bf16[8,32,576]{2,1,0:T(8,128)(2,1)S(1)}, u32[]{:S(2)}, u32[]{:S(2)}) collective-permute-start(bf16[8,32,576]{2,1,0:T(8,128)(2,1)S(1)} %get-tuple-element.36), channel_id=1, source_target_pairs={{0,16},{1,5},{4,20},{5,9},{8,24},{9,13},{12,28},{13,1},{64,80},{65... | collective-permute-start | bytes 884744 | tf_op jit(solution)/shard_map/ppermute | solution.py:250
  65.5 14.0 %collective-permute-start.17 = (bf16[64,1024]{1,0:T(8,128)(2,1)S(1)}, bf16[64,1024]{1,0:T(8,128)(2,1)S(1)}, u32[]{:S(2)}, u32[]{:S(2)}) collective-permute-start(bf16[64,1024]{1,0:T(8,128)(2,1)S(1)} %get-tuple-element.43), channel_id=1, source_target_pairs={{0,64},{1,65},{4,68},{5,69},{8,72},{9,73},{12,76},{13,77},{64,0},{... | collective-permute-start | bytes 393224 | tf_op jit(solution)/shard_map/ppermute | solution.py:231
  67.2 12.3 %collective-permute-start.16 = (bf16[64,1024]{1,0:T(8,128)(2,1)S(1)}, bf16[64,1024]{1,0:T(8,128)(2,1)S(1)}, u32[]{:S(2)}, u32[]{:S(2)}) collective-permute-start(bf16[64,1024]{1,0:T(8,128)(2,1)S(1)} %get-tuple-element.44), channel_id=1, source_target_pairs={{0,112},{1,81},{4,116},{5,85},{8,120},{9,89},{12,124},{13,93},{64,... | collective-permute-start | bytes 393224 | tf_op jit(solution)/shard_map/ppermute | solution.py:231
  68.2 11.3 %collective-permute-start.15 = (bf16[64,1024]{1,0:T(8,128)(2,1)S(1)}, bf16[64,1024]{1,0:T(8,128)(2,1)S(1)}, u32[]{:S(2)}, u32[]{:S(2)}) collective-permute-start(bf16[64,1024]{1,0:T(8,128)(2,1)S(1)} %get-tuple-element.45), channel_id=1, source_target_pairs={{0,48},{1,17},{4,52},{5,21},{8,56},{9,25},{12,60},{13,29},{64,112}... | collective-permute-start | bytes 393224 | tf_op jit(solution)/shard_map/ppermute | solution.py:231
  71.2 16.8 %all-to-all-start = ((bf16[16,16,576]{2,1,0:T(8,128)(2,1)}), bf16[16,16,576]{2,1,0:T(8,128)(2,1)S(1)}, u32[]{:S(2)}, u32[]{:S(2)}) async-start(bf16[16,16,576]{2,1,0:T(8,128)(2,1)} %bitcast.16), calls=%async_computation | async-start | bytes 655360 | tf_op jit(solution)/shard_map/all_to_all | solution.py:261
